TPU v7x, 32 devices: a whole 2x2x4 slice. The times are simulated.
32 devices in a mesh: seq: 8 (over z, x), row: 4 (over y, core).
Axes of the slice: x: 2, y: 2, z: 4, core: 2. Of those that a mesh axis runs over, the one named last changes fastest.
Arguments:
- tokens: bfloat16 [4, 1024, 1536], P('row', 'seq'), may hold values from -6 to 6
- segments: int32 [4, 1024], P('row', 'seq'), may hold values from 0 to 3, as said below
- joint_matrix: bfloat16 [1536, 2048], P(('seq', 'row')), may hold values from -0.21875 to 0.21875
- joint_bias: bfloat16 [2048], P(('seq', 'row')), may hold values from -3 to 3
- merge_matrix: bfloat16 [1536, 1536], P(None, ('seq', 'row')), may hold values from -0.625 to 0.625
- norm_first: bfloat16 [1536], P(('seq', 'row')), may hold values from 0.5 to 1.5
- norm_second: bfloat16 [1536], P(('seq', 'row')), may hold values from 0.5 to 1.5
- gate_matrix: bfloat16 [1536, 8960], P(('seq', 'row')), may hold values from -0.15625 to 0.15625
- up_matrix: bfloat16 [1536, 8960], P(('seq', 'row')), may hold values from -0.15625 to 0.15625
- down_matrix: bfloat16 [8960, 1536], P(None, ('seq', 'row')), may hold values from -0.25 to 0.25
- cotangent: bfloat16 [4, 1024, 1536], P('row', 'seq'), may hold values from -8 to 8
Outputs:
- output: bfloat16 [4, 1024, 1536], P('row', 'seq')
- tokens_grad: float32 [4, 1024, 1536], P('row', 'seq')
- joint_grad: float32 [1536, 2048], P(('seq', 'row'))
- bias_grad: float32 [2048], P(('seq', 'row'))
- merge_grad: float32 [1536, 1536], P(None, ('seq', 'row'))
- first_grad: float32 [1536], P(('seq', 'row'))
- second_grad: float32 [1536], P(('seq', 'row'))
- gate_grad: float32 [1536, 8960], P(('seq', 'row'))
- up_grad: float32 [1536, 8960], P(('seq', 'row'))
- down_grad: float32 [8960, 1536], P(None, ('seq', 'row'))
Inputs may be any that keep to these rules, and one draw needn't show every extreme that they name: `segments`: in each row the document numbers never fall and every number from 0 to 3 occurs; document 2 begins within the first 128 tokens of the row and ends within its last 128.
All inputs are finite; a program needn't handle non-finite values.
Results may differ from a plain program's by a relative error of at most 0.02.
Values may be sent and summed in bfloat16 or wider, within the bound.
A program may use at most 448 MiB of HBM per device.

v0:
```python
import math

import jax
import jax.numpy as jnp
from jax import lax
from jax.sharding import PartitionSpec as P

HEADS = 12
KV_HEADS = 2
HEAD_DIM = 128


eps = 1e-06
theta = 1000000.0
neg = -1e30
last_pair = (((1,), (1,)), ((), ()))
first_pair = (((0,), (0,)), ((), ()))


def normed(values, gain):
    return values * lax.rsqrt(jnp.mean(values * values, axis=-1, keepdims=True) + eps) * gain


def swiglu(gate, upper):
    return jax.nn.silu(gate) * upper


def turn_half(values):
    middle = values.shape[-1] // 2
    return jnp.concatenate([-values[..., middle:], values[..., :middle]], axis=-1)


def unturn_half(values):
    middle = values.shape[-1] // 2
    return jnp.concatenate([values[..., middle:], -values[..., :middle]], axis=-1)


def row_positions(labels):
    length = labels.shape[0]
    places = jnp.arange(length, dtype=jnp.int32)
    change = jnp.concatenate([jnp.ones((1,), dtype=jnp.bool_), labels[1:] != labels[:-1]])
    starts = lax.cummax(jnp.where(change, places, 0), axis=0)
    return places - starts


def rotary(positions, width):
    inverse = jnp.power(
        jnp.float32(theta), -(jnp.arange(width // 2, dtype=jnp.float32) * (2.0 / width))
    )
    angle = positions.astype(jnp.float32)[:, None] * inverse[None, :]
    angle = jnp.concatenate([angle, angle], axis=1)[:, None, :]
    return (jnp.cos(angle), jnp.sin(angle))


def to_groups(values, shared):
    length, heads, width = values.shape
    group = heads // shared
    return (
        values.reshape(length, shared, group, width)
        .transpose(1, 2, 0, 3)
        .reshape(shared, group * length, width)
    )


def from_groups(values, length):
    shared, rows, width = values.shape
    group = rows // length
    return (
        values.reshape(shared, group, length, width)
        .transpose(2, 0, 1, 3)
        .reshape(length, shared * group * width)
    )


def body(
    tokens,
    segments,
    joint_matrix,
    joint_bias,
    merge_matrix,
    norm_first,
    norm_second,
    gate_matrix,
    up_matrix,
    down_matrix,
    cotangent,
):
    floats = jnp.float32
    halves = jnp.bfloat16
    residual = tokens[0].astype(floats)
    length = residual.shape[0]
    own_labels = segments[0]
    labels = lax.all_gather(own_labels, "seq", axis=0, tiled=True)
    row_total = labels.shape[0]
    offset = lax.axis_index("seq") * length
    places = offset + jnp.arange(length, dtype=jnp.int32)
    positions = lax.dynamic_slice_in_dim(row_positions(labels), offset, length, 0)
    cosine, sine = rotary(positions, HEAD_DIM)
    joint_all, merge_all, bias_all, gain_first, gain_second = (
        lax.all_gather(joint_matrix, ("seq", "row"), axis=0, tiled=True),
        lax.all_gather(merge_matrix, ("seq", "row"), axis=1, tiled=True),
        lax.all_gather(joint_bias, ("seq", "row"), axis=0, tiled=True),
        lax.all_gather(norm_first, ("seq", "row"), axis=0, tiled=True),
        lax.all_gather(norm_second, ("seq", "row"), axis=0, tiled=True),
    )
    gain_first = gain_first.astype(floats)
    gain_second = gain_second.astype(floats)
    query_width = HEADS * HEAD_DIM
    key_width = KV_HEADS * HEAD_DIM
    group = HEADS // KV_HEADS
    scale = 1.0 / math.sqrt(HEAD_DIM)
    normal_first, first_back = jax.vjp(normed, residual, gain_first)
    normal_first = normal_first.astype(halves)
    joint = jnp.dot(normal_first, joint_all, preferred_element_type=floats) + bias_all.astype(
        floats
    )
    query = joint[:, :query_width].reshape(length, HEADS, HEAD_DIM)
    keys = joint[:, query_width : query_width + key_width].reshape(length, KV_HEADS, HEAD_DIM)
    values = joint[:, query_width + key_width :].reshape(length, KV_HEADS, HEAD_DIM).astype(halves)
    query = (query * cosine + turn_half(query) * sine).astype(halves)
    keys = (keys * cosine + turn_half(keys) * sine).astype(halves)
    query_group = to_groups(query, KV_HEADS)
    rows = query_group.shape[1]

    def piece_mask(count):
        key_places = jnp.arange(count, dtype=jnp.int32)
        allowed = (places[:, None] >= key_places[None, :]) & (
            own_labels[:, None] == labels[None, :]
        )
        return jnp.tile(allowed, (group, 1))[None]

    start_state = (
        jnp.full((KV_HEADS, rows), neg, floats),
        jnp.zeros((KV_HEADS, rows), floats),
        jnp.zeros((KV_HEADS, rows, HEAD_DIM), floats),
    )
    key_piece = lax.all_gather(keys, "seq", axis=0, tiled=True)
    value_piece = lax.all_gather(values, "seq", axis=0, tiled=True)
    count = key_piece.shape[0]

    def compute(state):
        top, total, summed = state
        scores = (
            jnp.einsum("krd,nkd->krn", query_group, key_piece, preferred_element_type=floats)
            * scale
        )
        allowed = piece_mask(count)
        scores = jnp.where(allowed, scores, neg)
        new_top = jnp.maximum(top, jnp.max(scores, axis=-1))
        weights = jnp.where(allowed, jnp.exp(scores - new_top[..., None]), 0.0)
        total = jnp.sum(weights, axis=-1)
        summed = jnp.einsum(
            "krn,nkd->krd", weights.astype(halves), value_piece, preferred_element_type=floats
        )
        return (new_top, total, summed)

    top, total, summed = compute(start_state)
    attended = summed / total[..., None]
    log_sums = top + jnp.log(total)
    attended_half = from_groups(attended, length).astype(halves)
    mixed = residual + jnp.dot(attended_half, merge_all, preferred_element_type=floats)
    normal_second, second_back = jax.vjp(normed, mixed, gain_second)
    normal_half = normal_second.astype(halves)
    gate_all, upper_all = (
        lax.all_gather(gate_matrix, ("seq", "row"), axis=0, tiled=True),
        lax.all_gather(up_matrix, ("seq", "row"), axis=0, tiled=True),
    )
    gate = jnp.dot(normal_half, gate_all, preferred_element_type=floats)
    upper = jnp.dot(normal_half, upper_all, preferred_element_type=floats)
    hidden, swiglu_back = jax.vjp(swiglu, gate, upper)
    hidden_half = hidden.astype(halves)
    branch = jnp.dot(
        hidden_half,
        lax.all_gather(down_matrix, ("seq", "row"), axis=1, tiled=True),
        preferred_element_type=floats,
    )
    output = (mixed + branch).astype(halves)[None]
    outer_grad = cotangent[0]
    outer_float = outer_grad.astype(floats)
    down_all = lax.all_gather(down_matrix, ("seq", "row"), axis=1, tiled=True)
    hidden_grad = lax.dot_general(outer_grad, down_all, last_pair, preferred_element_type=floats)
    gate_float, upper_float = swiglu_back(hidden_grad)
    gate_half = gate_float.astype(halves)
    upper_half = upper_float.astype(halves)
    gate_back_all, upper_back_all = (
        lax.all_gather(gate_matrix, ("seq", "row"), axis=0, tiled=True),
        lax.all_gather(up_matrix, ("seq", "row"), axis=0, tiled=True),
    )
    normal_grad = lax.dot_general(
        gate_half, gate_back_all, last_pair, preferred_element_type=floats
    ) + lax.dot_general(upper_half, upper_back_all, last_pair, preferred_element_type=floats)
    row_normal, row_outer = (
        lax.all_gather(normal_half, "seq", axis=0, tiled=True),
        lax.all_gather(outer_grad, "seq", axis=0, tiled=True),
    )
    hidden_cols, gate_cols, upper_cols = (
        lax.all_to_all(hidden_half, "seq", split_axis=1, concat_axis=0, tiled=True),
        lax.all_to_all(gate_half, "seq", split_axis=1, concat_axis=0, tiled=True),
        lax.all_to_all(upper_half, "seq", split_axis=1, concat_axis=0, tiled=True),
    )
    down_part = lax.dot_general(row_outer, hidden_cols, first_pair, preferred_element_type=floats)
    gate_part = lax.dot_general(row_normal, gate_cols, first_pair, preferred_element_type=floats)
    upper_part = lax.dot_general(row_normal, upper_cols, first_pair, preferred_element_type=floats)
    down_moved, gate_moved, upper_moved = (
        lax.all_to_all(
            down_part.astype(jnp.bfloat16), "seq", split_axis=0, concat_axis=1, tiled=True
        ).astype(down_part.dtype),
        lax.all_to_all(
            gate_part.astype(jnp.bfloat16), "seq", split_axis=0, concat_axis=1, tiled=True
        ).astype(gate_part.dtype),
        lax.all_to_all(
            upper_part.astype(jnp.bfloat16), "seq", split_axis=0, concat_axis=1, tiled=True
        ).astype(upper_part.dtype),
    )
    down_total, gate_grad, up_grad = (
        lax.psum_scatter(
            down_moved.astype(jnp.bfloat16), "row", scatter_dimension=0, tiled=True
        ).astype(jnp.float32),
        lax.psum_scatter(
            gate_moved.astype(jnp.bfloat16), "row", scatter_dimension=0, tiled=True
        ).astype(jnp.float32),
        lax.psum_scatter(
            upper_moved.astype(jnp.bfloat16), "row", scatter_dimension=0, tiled=True
        ).astype(jnp.float32),
    )
    down_grad = down_total.T
    mixed_part, second_local = second_back(normal_grad)
    mixed_grad = outer_float + mixed_part
    mixed_half = mixed_grad.astype(halves)
    merge_local = lax.dot_general(
        attended_half, mixed_half, first_pair, preferred_element_type=floats
    )
    attended_grad = lax.dot_general(
        mixed_half, merge_all, last_pair, preferred_element_type=floats
    ).astype(halves)
    grad_group = to_groups(attended_grad.reshape(length, HEADS, HEAD_DIM), KV_HEADS)
    row_dots = jnp.sum(grad_group.astype(floats) * attended, axis=-1)
    back_state = (
        jnp.zeros((KV_HEADS, rows, HEAD_DIM), floats),
        jnp.zeros((row_total, 2 * key_width), floats),
    )
    backward_key_piece = lax.all_gather(keys, "seq", axis=0, tiled=True)
    backward_value_piece = lax.all_gather(values, "seq", axis=0, tiled=True)
    backward_count = backward_key_piece.shape[0]

    def compute(state):
        scores = (
            jnp.einsum(
                "krd,nkd->krn", query_group, backward_key_piece, preferred_element_type=floats
            )
            * scale
        )
        allowed = piece_mask(backward_count)
        shares = jnp.where(allowed, jnp.exp(scores - log_sums[..., None]), 0.0)
        shares_half = shares.astype(halves)
        mass_grad = jnp.einsum(
            "krd,nkd->krn", grad_group, backward_value_piece, preferred_element_type=floats
        )
        score_half = (shares * (mass_grad - row_dots[..., None])).astype(halves)
        query_sum = (
            jnp.einsum(
                "krn,nkd->krd", score_half, backward_key_piece, preferred_element_type=floats
            )
            * scale
        )
        key_grad = (
            jnp.einsum("krn,krd->nkd", score_half, query_group, preferred_element_type=floats)
            * scale
        )
        value_grad = jnp.einsum(
            "krn,krd->nkd", shares_half, grad_group, preferred_element_type=floats
        )
        block = jnp.concatenate(
            [
                key_grad.reshape(backward_count, key_width),
                value_grad.reshape(backward_count, key_width),
            ],
            axis=1,
        )
        return (query_sum, block)

    query_sum, pair_sums = compute(back_state)
    pair_mine = lax.psum_scatter(
        pair_sums.astype(jnp.bfloat16), "seq", scatter_dimension=0, tiled=True
    ).astype(jnp.float32)
    key_back = pair_mine[:, :key_width].reshape(length, KV_HEADS, HEAD_DIM)
    value_back = pair_mine[:, key_width:]
    query_back = from_groups(query_sum, length).reshape(length, HEADS, HEAD_DIM)
    query_back = query_back * cosine + unturn_half(query_back * sine)
    key_back = key_back * cosine + unturn_half(key_back * sine)
    joint_back = jnp.concatenate(
        [query_back.reshape(length, query_width), key_back.reshape(length, key_width), value_back],
        axis=1,
    ).astype(halves)
    joint_local = lax.dot_general(
        normal_first, joint_back, first_pair, preferred_element_type=floats
    )
    bias_local = jnp.sum(joint_back.astype(floats), axis=0)
    normal_back = lax.dot_general(joint_back, joint_all, last_pair, preferred_element_type=floats)
    residual_part, first_local = first_back(normal_back)
    tokens_grad = (mixed_grad + residual_part)[None]
    joint_grad, merge_grad, bias_grad, first_grad, second_grad = (
        lax.psum_scatter(joint_local, ("seq", "row"), scatter_dimension=0, tiled=True),
        lax.psum_scatter(merge_local, ("seq", "row"), scatter_dimension=1, tiled=True),
        lax.psum_scatter(bias_local, ("seq", "row"), scatter_dimension=0, tiled=True),
        lax.psum_scatter(first_local, ("seq", "row"), scatter_dimension=0, tiled=True),
        lax.psum_scatter(second_local, ("seq", "row"), scatter_dimension=0, tiled=True),
    )
    return (
        output,
        tokens_grad,
        joint_grad,
        bias_grad,
        merge_grad,
        first_grad,
        second_grad,
        gate_grad,
        up_grad,
        down_grad,
    )


def solution(mesh):
    placed = (
        P("row", "seq", None),
        P("row", "seq"),
        P(("seq", "row"), None),
        P(("seq", "row")),
        P(None, ("seq", "row")),
        P(("seq", "row")),
        P(("seq", "row")),
        P(("seq", "row"), None),
        P(("seq", "row"), None),
        P(None, ("seq", "row")),
        P("row", "seq", None),
    )
    return jax.shard_map(
        body,
        mesh=mesh,
        in_specs=placed,
        out_specs=(
            P("row", "seq", None),
            P("row", "seq", None),
            P(("seq", "row"), None),
            P(("seq", "row")),
            P(None, ("seq", "row")),
            P(("seq", "row")),
            P(("seq", "row")),
            P(("seq", "row"), None),
            P(("seq", "row"), None),
            P(None, ("seq", "row")),
        ),
        check_vma=False,
    )
```

profile of v0, /device:TPU:0, one launch (start us, length us, event | category | flops | bytes accessed | tf_op | source)
XLA Modules:
  0.0 1549.8 jit_solution(15905616791213835330)
XLA Ops:
  13.1 42.3 %all-reduce.7 = (bf16[2048]{0:T(1024)(128)(2,1)S(1)}, bf16[1536]{0:T(1024)(128)(2,1)S(1)}, bf16[1536]{0:T(1024)(128)(2,1)S(1)}) all-reduce(bf16[2048]{0:T(1024)(128)(2,1)S(1)} %dynamic-update-slice.1, bf16[1536]{0:T(1024)(128)(2,1)S(1)} %dynamic-update-slice, ...), channel_id=1, replica_groups=mesh['seq'=8,'row'=4] {'seq','row'}, use_global_device_ids=true, to_apply=%add.1 | all-reduce | flops 5120 | bytes 20480
  55.4 20.5 %all-gather = s32[1,1024]{1,0:T(1,128)S(1)} all-gather(s32[1,128]{1,0:T(1,128)} %param.12), channel_id=2, replica_groups=mesh['seq'=8,'row'=4] {'seq'}, dimensions={1}, use_global_device_ids=true | all-gather | bytes 4608 | tf_op jit(solution)/shard_map/all_gather | solution.py:93
  88.4 32.0 %all_gather.48 = bf16[1024,2,128]{2,0,1:T(8,128)(2,1)S(1)} all-gather(bf16[128,2,128]{2,0,1:T(8,128)(2,1)S(1)} %fusion.45), channel_id=1, replica_groups=mesh['seq'=8,'row'=4] {'seq'}, dimensions={0}, use_global_device_ids=true | all-gather | bytes 589824 | tf_op jit(solution)/shard_map/all_gather | solution.py:137
  122.3 32.3 %all_gather.49 = bf16[1024,2,128]{2,0,1:T(8,128)(2,1)S(1)} all-gather(bf16[128,2,128]{2,0,1:T(8,128)(2,1)S(1)} %copy_bitcast_fusion.1), channel_id=1, replica_groups=mesh['seq'=8,'row'=4] {'seq'}, dimensions={0}, use_global_device_ids=true | all-gather | bytes 589824 | tf_op jit(solution)/shard_map/all_gather | solution.py:138
  164.2 157.6 %all-gather.14.cloned.1.call-done = bf16[1536,8960]{1,0:T(8,128)(2,1)} async-done(((bf16[48,8960]{1,0:T(8,128)(2,1)}), bf16[1536,8960]{1,0:T(8,128)(2,1)}) %all-gather.14.cloned.1.call-update) | async-done | bytes 27525136 | tf_op jit(solution)/shard_map/all_gather | solution.py:165
  321.8 14.7 fusion.65
  336.5 152.2 %all-gather.16.cloned.1.call-done = bf16[1536,8960]{1,0:T(8,128)(2,1)} async-done(((bf16[48,8960]{1,0:T(8,128)(2,1)}), bf16[1536,8960]{1,0:T(8,128)(2,1)}) %all-gather.16.cloned.1.call-update) | async-done | bytes 27525136 | tf_op jit(solution)/shard_map/all_gather | solution.py:166
  488.7 14.9 fusion.66
  503.6 152.1 %all-gather.18.cloned.1.call-done = bf16[8960,1536]{0,1:T(8,128)(2,1)} async-done(((bf16[8960,48]{0,1:T(8,128)(2,1)}), bf16[8960,1536]{0,1:T(8,128)(2,1)}) %all-gather.18.cloned.1.call-update) | async-done | bytes 27525136 | tf_op jit(solution)/shard_map/all_gather | solution.py:174
  655.7 17.1 %multiply_convert_fusion.1 = (bf16[128,8960]{1,0:T(8,128)(2,1)}, bf16[128,8960]{1,0:T(8,128)(2,1)S(1)}, bf16[128,8960]{1,0:T(8,128)(2,1)}) fusion(f32[128,8960]{1,0:T(8,128)} %fusion.65, f32[128,8960]{1,0:T(8,128)} %fusion.66, bf16[8960,1536]{0,1:T(8,128)(2,1)} %all-gather.18.cloned.1.call-done, bf16[1,128,1536]{2,1,0:T(8,128)(2,1)} %param.21), kind=kOutput, calls=%fused_computation.13 | convolution fusion | flops 3541565440 | bytes 43974656 | tf_op jit(solution)/shard_map/dot_general | solution.py:181
  684.4 74.4 %all-to-all-done = bf16[128,8,1120]{0,2,1:T(8,128)(2,1)} async-done(((bf16[128,8,1120]{0,2,1:T(8,128)(2,1)}), bf16[128,8,1120]{0,2,1:T(8,128)(2,1)}, u32[]{:S(2)}, u32[]{:S(2)}) %all-to-all-start) | async-done | bytes 2293792 | tf_op jit(solution)/shard_map/all_to_all | solution.py:198
  773.8 8.1 convolution_convert_fusion.2
  787.6 45.1 %all-to-all-done.2 = bf16[128,8,1120]{0,2,1:T(8,128)(2,1)} async-done(((bf16[128,8,1120]{0,2,1:T(8,128)(2,1)}), bf16[128,8,1120]{0,2,1:T(8,128)(2,1)}, u32[]{:S(2)}, u32[]{:S(2)}) %all-to-all-start.2) | async-done | bytes 2293792 | tf_op jit(solution)/shard_map/all_to_all | solution.py:199
  837.3 14.8 fusion.67
  852.1 15.0 multiply_reduce_fusion
  883.2 8.3 convolution_convert_fusion.1
  897.2 38.2 %all-to-all-done.1 = bf16[8,192,1120]{2,1,0:T(8,128)(2,1)} async-done(((bf16[8,192,1120]{2,1,0:T(8,128)(2,1)}), bf16[8,192,1120]{2,1,0:T(8,128)(2,1)}, u32[]{:S(2)}, u32[]{:S(2)}) %all-to-all-start.1) | async-done | bytes 3440672 | tf_op jit(solution)/shard_map/all_to_all | solution.py:208
  948.9 5.8 copy.118
  954.6 6.8 all_to_all.91
  964.0 63.8 %all-to-all-done.3 = bf16[8,192,1120]{2,1,0:T(8,128)(2,1)} async-done(((bf16[8,192,1120]{2,1,0:T(8,128)(2,1)}), bf16[8,192,1120]{2,1,0:T(8,128)(2,1)}, u32[]{:S(2)}, u32[]{:S(2)}) %all-to-all-start.3) | async-done | bytes 3440672 | tf_op jit(solution)/shard_map/all_to_all | solution.py:211
  1032.2 5.8 copy.122
  1038.0 6.6 all_to_all.99
  1045.1 43.2 %all-to-all-done.4 = bf16[128,8,1120]{0,2,1:T(8,128)(2,1)} async-done(((bf16[128,8,1120]{0,2,1:T(8,128)(2,1)}), bf16[128,8,1120]{0,2,1:T(8,128)(2,1)}, u32[]{:S(2)}, u32[]{:S(2)}) %all-to-all-start.4) | async-done | bytes 2293792 | tf_op jit(solution)/shard_map/all_to_all | solution.py:197
  1092.6 8.2 fusion
  1106.5 83.4 %all_to_all.114 = bf16[8,192,1120]{2,1,0:T(8,128)(2,1)S(1)} all-to-all(bf16[8,192,1120]{2,1,0:T(8,128)(2,1)} %bitcast.148), channel_id=1, replica_groups=mesh['seq'=8,'row'=4] {'seq'}, dimensions={0} | all-to-all | bytes 6881280 | tf_op jit(solution)/shard_map/all_to_all | solution.py:205
  1193.7 6.7 all_to_all.107
  1200.5 7.1 fusion.41
  1227.8 7.4 fusion.47
  1235.3 14.9 fusion.16
  1257.3 38.6 %all-reduce.6 = (f32[2048]{0:T(1024)S(1)}, f32[1536]{0:T(1024)S(1)}, f32[1536]{0:T(1024)S(1)}) all-reduce(f32[2048]{0:T(1024)S(1)} %convert_reduce_fusion, f32[1536]{0:T(1024)S(1)} %get-tuple-element.12, f32[1536]{0:T(1024)S(1)} %get-tuple-element.10), channel_id=6, replica_groups=mesh['seq'=8,'row'=4] {'seq','row'}, use_global_device_ids=true, to_apply=%region_12.13.clone | all-reduce | flops 5120 | bytes 40960
  1306.1 74.9 %reduce-scatter.11.cloned.1.call-done = f32[1536,48]{0,1:T(8,128)} async-done(((f32[1536,1536]{0,1:T(8,128)}), f32[1536,48]{0,1:T(8,128)}) %reduce-scatter.11.cloned.1.call-update) | async-done | bytes 294928 | tf_op jit(solution)/shard_map/reduce_scatter | solution.py:304
  1381.1 162.0 %reduce-scatter.9.cloned.1.call-done = f32[48,2048]{1,0:T(8,128)} async-done(((f32[1536,2048]{1,0:T(8,128)}), f32[48,2048]{1,0:T(8,128)}) %reduce-scatter.9.cloned.1.call-update) | async-done | bytes 393232 | tf_op jit(solution)/shard_map/reduce_scatter | solution.py:303
  (183 shorter events, 160.3 us)
Async XLA Ops:
  7.2 76.2 %all-gather.10.cloned.1.call-start = ((), (), s32[]{:S(2)}) async-start(), calls=%async_computation.12 | async-start | bytes 6488064 | tf_op jit(solution)/shard_map/all_gather | solution.py:100
  7.9 151.9 %all-gather.12.cloned.1.call-start = ((), (), s32[]{:S(2)}) async-start(), calls=%async_computation.13 | async-start | bytes 4866048 | tf_op jit(solution)/shard_map/all_gather | solution.py:101
  8.7 313.2 %all-gather.14.cloned.1.call-start = ((), (), s32[]{:S(2)}) async-start(), calls=%async_computation.14 | async-start | bytes 28385280 | tf_op jit(solution)/shard_map/all_gather | solution.py:165
  9.4 479.4 %all-gather.16.cloned.1.call-start = ((), (), s32[]{:S(2)}) async-start(), calls=%async_computation.15 | async-start | bytes 28385280 | tf_op jit(solution)/shard_map/all_gather | solution.py:166
  10.0 645.7 %all-gather.18.cloned.1.call-start = ((), (), s32[]{:S(2)}) async-start(), calls=%async_computation.16 | async-start | bytes 28385280 | tf_op jit(solution)/shard_map/all_gather | solution.py:174
  55.4 31.9 %copy-start.20 = (f32[1536]{0:T(1024)}, f32[1536]{0:T(1024)S(1)}, u32[]{:S(2)}) copy-start(f32[1536]{0:T(1024)S(1)} %convert_element_type.113) | copy-start | bytes 18436
  77.2 11.1 copy-start.15
  77.3 10.5 copy-start.18
  88.1 34.1 %copy-start.12 = (bf16[2,6,128,128]{3,2,1,0:T(8,128)(2,1)}, bf16[2,6,128,128]{3,2,1,0:T(8,128)(2,1)S(1)}, u32[]{:S(2)}) copy-start(bf16[2,6,128,128]{3,2,1,0:T(8,128)(2,1)S(1)} %copy.99) | copy-start | bytes 1179652
  120.4 34.2 %copy-start.10 = (bf16[1024,2,128]{2,0,1:T(8,128)(2,1)}, bf16[1024,2,128]{2,0,1:T(8,128)(2,1)S(1)}, u32[]{:S(2)}) copy-start(bf16[1024,2,128]{2,0,1:T(8,128)(2,1)S(1)} %all_gather.48) | copy-start | bytes 1572868
  120.7 36.3 %copy-start.8 = (pred[6,128,1024]{2,1,0:T(8,128)(4,1)}, pred[6,128,1024]{2,1,0:T(8,128)(4,1)S(1)}, u32[]{:S(2)}) copy-start(pred[6,128,1024]{2,1,0:T(8,128)(4,1)S(1)} %tile.4) | copy-start | bytes 2359300
  122.2 37.3 %copy-start.6 = (f32[2,768,1024]{2,1,0:T(8,128)}, f32[2,768,1024]{2,1,0:T(8,128)S(1)}, u32[]{:S(2)}) copy-start(f32[2,768,1024]{2,1,0:T(8,128)S(1)} %get-tuple-element.36) | copy-start | bytes 18874372
  164.2 324.6 %copy-start.5 = (bf16[128,1536]{1,0:T(8,128)(2,1)}, bf16[128,1536]{1,0:T(8,128)(2,1)S(1)}, u32[]{:S(2)}) copy-start(bf16[128,1536]{1,0:T(8,128)(2,1)S(1)} %multiply_convert_fusion.3) | copy-start | bytes 1179652
  675.3 83.6 %all-to-all-start = ((bf16[128,8,1120]{0,2,1:T(8,128)(2,1)}), bf16[128,8,1120]{0,2,1:T(8,128)(2,1)}, u32[]{:S(2)}, u32[]{:S(2)}) async-start(bf16[128,8,1120]{0,2,1:T(8,128)(2,1)} %bitcast.151), calls=%async_computation.2 | async-start | bytes 4587520 | tf_op jit(solution)/shard_map/all_to_all | solution.py:198
  679.6 94.2 %all-gather.20.cloned.1.call-start = ((), (), s32[]{:S(2)}) async-start(), calls=%async_computation.19 | async-start | bytes 3538944 | tf_op jit(solution)/shard_map/all_gather | solution.py:193
  758.8 73.9 %all-to-all-start.2 = ((bf16[128,8,1120]{0,2,1:T(8,128)(2,1)}), bf16[128,8,1120]{0,2,1:T(8,128)(2,1)}, u32[]{:S(2)}, u32[]{:S(2)}) async-start(bf16[128,8,1120]{0,2,1:T(8,128)(2,1)} %bitcast.149), calls=%async_computation.5 | async-start | bytes 4587520 | tf_op jit(solution)/shard_map/all_to_all | solution.py:199
  763.2 329.4 %all-gather.22.cloned.1.call-start = ((), (), s32[]{:S(2)}) async-start(), calls=%async_computation.23 | async-start | bytes 3538944 | tf_op jit(solution)/shard_map/all_gather | solution.py:194
  832.7 102.7 %all-to-all-start.1 = ((bf16[8,192,1120]{2,1,0:T(8,128)(2,1)}), bf16[8,192,1120]{2,1,0:T(8,128)(2,1)}, u32[]{:S(2)}, u32[]{:S(2)}) async-start(bf16[8,192,1120]{2,1,0:T(8,128)(2,1)} %bitcast.147), calls=%async_computation.3 | async-start | bytes 7077888 | tf_op jit(solution)/shard_map/all_to_all | solution.py:208
  852.1 15.0 copy-start.11
  935.4 92.4 %all-to-all-start.3 = ((bf16[8,192,1120]{2,1,0:T(8,128)(2,1)}), bf16[8,192,1120]{2,1,0:T(8,128)(2,1)}, u32[]{:S(2)}, u32[]{:S(2)}) async-start(bf16[8,192,1120]{2,1,0:T(8,128)(2,1)} %bitcast.146), calls=%async_computation.6 | async-start | bytes 7077888 | tf_op jit(solution)/shard_map/all_to_all | solution.py:211
  939.8 276.7 %reduce-scatter.19.cloned.1.call-start = ((), (), s32[]{:S(2)}) async-start(), calls=%async_computation.24 | async-start | bytes 1179648
  948.8 349.9 %reduce-scatter.13.cloned.1.call-start = ((), (), s32[]{:S(2)}) async-start(), calls=%async_computation.20 | async-start | bytes 4300800 | tf_op jit(solution)/shard_map/reduce_scatter | solution.py:219
  1027.8 60.6 %all-to-all-start.4 = ((bf16[128,8,1120]{0,2,1:T(8,128)(2,1)}), bf16[128,8,1120]{0,2,1:T(8,128)(2,1)}, u32[]{:S(2)}, u32[]{:S(2)}) async-start(bf16[128,8,1120]{0,2,1:T(8,128)(2,1)} %bitcast.150), calls=%async_computation.8 | async-start | bytes 4587520 | tf_op jit(solution)/shard_map/all_to_all | solution.py:197
  1032.2 269.0 %reduce-scatter.15.cloned.1.call-start = ((), (), s32[]{:S(2)}) async-start(), calls=%async_computation.21 | async-start | bytes 4300800 | tf_op jit(solution)/shard_map/reduce_scatter | solution.py:222
  1044.6 259.0 %reduce-scatter.17.cloned.1.call-start = ((), (), s32[]{:S(2)}) async-start(), calls=%async_computation.22 | async-start | bytes 4300800 | tf_op jit(solution)/shard_map/reduce_scatter | solution.py:216
  1200.5 180.6 %reduce-scatter.11.cloned.1.call-start = ((), (), s32[]{:S(2)}) async-start(), calls=%async_computation.18 | async-start | bytes 9732096 | tf_op jit(solution)/shard_map/reduce_scatter | solution.py:304
  1207.7 335.4 %reduce-scatter.9.cloned.1.call-start = ((), (), s32[]{:S(2)}) async-start(), calls=%async_computation.17 | async-start | bytes 12976128 | tf_op jit(solution)/shard_map/reduce_scatter | solution.py:303
  1214.2 13.6 copy-start.21
  1235.3 15.0 copy-start.17
  1250.3 47.3 %copy-start.25 = (f32[128]{0:T(128)S(1)}, f32[128]{0:T(128)}, u32[]{:S(2)}) copy-start(f32[128]{0:T(128)} %copy-done.24) | copy-start | bytes 1540
  1250.3 47.3 %copy-start.2 = (f32[128,1536]{1,0:T(8,128)S(1)}, f32[128,1536]{1,0:T(8,128)}, u32[]{:S(2)}) copy-start(f32[128,1536]{1,0:T(8,128)} %copy-done.1) | copy-start | bytes 2359300
  1250.3 47.4 %copy-start.23 = (f32[128]{0:T(128)S(1)}, f32[128]{0:T(128)}, u32[]{:S(2)}) copy-start(f32[128]{0:T(128)} %copy-done.22) | copy-start | bytes 1540
  (12 other events, 54.6 us)
Sparse Core Ops, SparseCore 0:
  10.9 72.3 all-gather.9
  86.2 67.2 all-gather.11
  156.4 165.3 all-gather.13
  324.6 164.1 all-gather.15
  491.5 164.1 all-gather.17
  682.9 90.8 all-gather.19
  776.0 112.8 all-gather.21
  948.9 104.7 reduce-scatter.18
  1056.5 51.6 reduce-scatter.12
  1110.5 39.8 reduce-scatter.14
  1200.6 38.4 reduce-scatter.16
  1245.4 135.5 reduce-scatter.10
  1388.7 154.3 reduce-scatter.8
where the time goes:
time: 1560 us; the launch traced here: 1550 us
  waiting for transfers between devices  977 us (63%)
  blocking collectives  249 us (16%)
  matrix products  168 us (11%)
  local copies, waits for them, and re-layouts  94.6 us (6%)
  starting transfers between devices  23.6 us (2%)
  other arithmetic  22.5 us (1%)
    reduce_scatter x1, waiting for transfers between devices, body(): lax.psum_scatter(joint_local, ('seq', 'row'), scatter_dimension=0, tiled=...  162 us
    all_gather x1, waiting for transfers between devices, body(): lax.all_gather(gate_matrix, ('seq', 'row'), axis=0, tiled=True)  158 us
    all_gather x1, waiting for transfers between devices, body(): lax.all_gather(up_matrix, ('seq', 'row'), axis=0, tiled=True)  152 us
    all_gather x1, waiting for transfers between devices, body(): lax.all_gather(down_matrix, ('seq', 'row'), axis=1, tiled=True)  152 us
    all_to_all x1, blocking collectives, body(): lax.all_to_all(down_part.astype(jnp.bfloat16), 'seq', split_axis=0, conca...  83.4 us
    unnamed x2, blocking collectives  80.9 us
    reduce_scatter x1, waiting for transfers between devices, body(): lax.psum_scatter(merge_local, ('seq', 'row'), scatter_dimension=1, tiled=...  74.9 us
    all_to_all x1, waiting for transfers between devices, body(): lax.all_to_all(gate_half, 'seq', split_axis=1, concat_axis=0, tiled=True)  74.4 us
  transfers between devices with their start and end apart: 18, of which 12 were waited for; matrix products, arithmetic and copies ran while one was open for 16% of the time, Pallas kernels for 0%

commit v1 on v0

v1 whole, which is shorter than its diff:
```python
import math

import jax
import jax.numpy as jnp
from jax import lax
from jax.sharding import Mesh, PartitionSpec as P

HEADS = 12
KV_HEADS = 2
HEAD_DIM = 128
GROUP = HEADS // KV_HEADS
QUERY_WIDTH = HEADS * HEAD_DIM
KEY_WIDTH = KV_HEADS * HEAD_DIM
SCALE = 1.0 / math.sqrt(HEAD_DIM)

eps = 1e-06
theta = 1000000.0
neg = -1e30
last_pair = (((1,), (1,)), ((), ()))
first_pair = (((0,), (0,)), ((), ()))
floats = jnp.float32
halves = jnp.bfloat16

AXES = ("z", "x", "y", "c")
SEQ = ("z", "x")
ROW = ("y", "c")
TEAM = ("z", "y")


def turn_half(values):
    middle = values.shape[-1] // 2
    return jnp.concatenate([-values[..., middle:], values[..., :middle]], axis=-1)


def unturn_half(values):
    middle = values.shape[-1] // 2
    return jnp.concatenate([values[..., middle:], -values[..., :middle]], axis=-1)


def row_positions(labels):
    length = labels.shape[0]
    places = jnp.arange(length, dtype=jnp.int32)
    change = jnp.concatenate([jnp.ones((1,), dtype=jnp.bool_), labels[1:] != labels[:-1]])
    starts = lax.cummax(jnp.where(change, places, 0), axis=0)
    return places - starts


def rotary(positions, width):
    inverse = jnp.power(
        jnp.float32(theta), -(jnp.arange(width // 2, dtype=jnp.float32) * (2.0 / width))
    )
    angle = positions.astype(jnp.float32)[:, None] * inverse[None, :]
    angle = jnp.concatenate([angle, angle], axis=1)[:, None, :]
    return (jnp.cos(angle), jnp.sin(angle))


def to_groups(values):
    length = values.shape[0]
    return (
        values.reshape(length, KV_HEADS, GROUP, HEAD_DIM)
        .transpose(1, 2, 0, 3)
        .reshape(KV_HEADS, GROUP * length, HEAD_DIM)
    )


def from_groups(values, length):
    return (
        values.reshape(KV_HEADS, GROUP, length, HEAD_DIM)
        .transpose(2, 0, 1, 3)
        .reshape(length, QUERY_WIDTH)
    )


def norm_parts(values):
    return lax.rsqrt(jnp.mean(values * values, axis=-1, keepdims=True) + eps)


def norm_back(upstream, values, scale, gain):
    scaled = upstream * gain
    inner = jnp.mean(scaled * values, axis=-1, keepdims=True)
    part = scale * scaled - values * (scale * scale * scale) * inner
    gain_grad = jnp.sum(upstream * values * scale, axis=0)
    return part, gain_grad


def body(
    tokens,
    segments,
    joint_matrix,
    joint_bias,
    merge_matrix,
    norm_first,
    norm_second,
    gate_matrix,
    up_matrix,
    down_matrix,
    cotangent,
):
    residual = tokens[0].astype(floats)
    length, model = residual.shape
    depth = joint_matrix.shape[0]
    joint_width = joint_matrix.shape[1]
    hidden_width = gate_matrix.shape[1]
    z_count = lax.axis_size("z")
    team = lax.axis_size(TEAM)
    share = hidden_width // team
    own_labels = segments[0]
    labels = lax.all_gather(own_labels, SEQ, axis=0, tiled=True)
    offset = lax.axis_index(SEQ) * length
    places = offset + jnp.arange(length, dtype=jnp.int32)
    positions = lax.dynamic_slice_in_dim(row_positions(labels), offset, length, 0)
    cosine, sine = rotary(positions, HEAD_DIM)

    small = jnp.concatenate([joint_bias, norm_first, norm_second])
    small = jnp.pad(small, (0, -small.shape[0] % depth)).reshape(depth, -1)
    small_width = small.shape[1]
    packed = jnp.concatenate([joint_matrix, merge_matrix.T, small], axis=1)
    packed = lax.all_gather(packed, AXES, axis=0, tiled=True)
    joint_all = packed[:, :joint_width]
    merge_turned = packed[:, joint_width : joint_width + model]
    small = packed[:, joint_width + model :].reshape(-1, depth * small_width).astype(floats)
    bias_depth = joint_bias.shape[0]
    bias_all = small[:, :bias_depth].reshape(-1)
    gain_first = small[:, bias_depth : bias_depth + depth].reshape(-1)
    gain_second = small[:, bias_depth + depth : bias_depth + 2 * depth].reshape(-1)

    stacked = jnp.stack([gate_matrix, up_matrix, down_matrix.T], axis=1)
    stacked = stacked.reshape(depth, 3, team, share).transpose(2, 0, 1, 3)
    stacked = stacked.reshape(team, depth, 3 * share)
    stacked = lax.all_to_all(stacked, TEAM, split_axis=0, concat_axis=0, tiled=True)
    stacked = stacked.reshape(z_count, 1, team // z_count, 1, depth, 3 * share)
    stacked = lax.all_gather(stacked, "x", axis=1, tiled=True)
    stacked = lax.all_gather(stacked, "c", axis=3, tiled=True)
    stacked = stacked.reshape(model, 3 * share)
    both_all, down_turned = stacked[:, : 2 * share], stacked[:, 2 * share :]
    outer_grad = cotangent[0]
    team_outer = lax.all_gather(outer_grad, TEAM, axis=0, tiled=True)

    scale_first = norm_parts(residual)
    normal_first = (residual * scale_first * gain_first).astype(halves)
    joint = jnp.dot(normal_first, joint_all, preferred_element_type=floats) + bias_all
    query = joint[:, :QUERY_WIDTH].reshape(length, HEADS, HEAD_DIM)
    keys = joint[:, QUERY_WIDTH : QUERY_WIDTH + KEY_WIDTH].reshape(length, KV_HEADS, HEAD_DIM)
    values = joint[:, QUERY_WIDTH + KEY_WIDTH :].astype(halves)
    query = (query * cosine + turn_half(query) * sine).astype(halves)
    keys = (keys * cosine + turn_half(keys) * sine).astype(halves).reshape(length, KEY_WIDTH)
    query_group = to_groups(query)
    pair = lax.all_gather(jnp.concatenate([keys, values], axis=1), SEQ, axis=0, tiled=True)
    count = pair.shape[0]
    key_all = pair[:, :KEY_WIDTH].reshape(count, KV_HEADS, HEAD_DIM)
    value_all = pair[:, KEY_WIDTH:].reshape(count, KV_HEADS, HEAD_DIM)
    allowed = (places[:, None] >= jnp.arange(count, dtype=jnp.int32)[None, :]) & (
        own_labels[:, None] == labels[None, :]
    )
    allowed = jnp.tile(allowed, (GROUP, 1))[None]
    scores = jnp.einsum("krd,nkd->krn", query_group, key_all, preferred_element_type=floats)
    scores = jnp.where(allowed, scores * SCALE, neg)
    top = jnp.max(scores, axis=-1, keepdims=True)
    weights = jnp.where(allowed, jnp.exp(scores - top), 0.0)
    total = jnp.sum(weights, axis=-1, keepdims=True)
    shares = weights / total
    shares_half = shares.astype(halves)
    attended = jnp.einsum("krn,nkd->krd", shares_half, value_all, preferred_element_type=floats)
    attended_half = from_groups(attended, length).astype(halves)
    mixed = residual + lax.dot_general(
        attended_half, merge_turned, last_pair, preferred_element_type=floats
    )
    scale_second = norm_parts(mixed)
    normal_half = (mixed * scale_second * gain_second).astype(halves)

    team_normal = lax.all_gather(normal_half, TEAM, axis=0, tiled=True)
    both = jnp.dot(team_normal, both_all, preferred_element_type=floats)
    gate, upper = both[:, :share], both[:, share:]
    sig = jax.nn.sigmoid(gate)
    silu = gate * sig
    hidden_half = (silu * upper).astype(halves)
    branch = lax.dot_general(hidden_half, down_turned, last_pair, preferred_element_type=floats)
    hidden_grad = jnp.dot(team_outer, down_turned, preferred_element_type=floats)
    gate_half = (hidden_grad * upper * sig * (1.0 + gate * (1.0 - sig))).astype(halves)
    upper_half = (hidden_grad * silu).astype(halves)
    both_half = jnp.concatenate([gate_half, upper_half], axis=1)
    normal_grad = lax.dot_general(both_half, both_all, last_pair, preferred_element_type=floats)
    branch = lax.psum_scatter(branch.astype(halves), TEAM, scatter_dimension=0, tiled=True)
    normal_grad = lax.psum_scatter(normal_grad.astype(halves), TEAM, scatter_dimension=0, tiled=True)
    output = (mixed + branch.astype(floats)).astype(halves)[None]
    both_grad = lax.dot_general(team_normal, both_half, first_pair, preferred_element_type=floats)
    down_grad = lax.dot_general(team_outer, hidden_half, first_pair, preferred_element_type=floats)
    grads = jnp.concatenate([both_grad, down_grad], axis=1).astype(halves)
    grads = grads.reshape(z_count, 2, team // z_count, 2, depth, 3 * share)
    grads = lax.psum_scatter(grads, "c", scatter_dimension=3, tiled=True)
    grads = lax.psum_scatter(grads, "x", scatter_dimension=1, tiled=True)
    grads = grads.reshape(team, depth, 3 * share)
    grads = lax.all_to_all(grads, TEAM, split_axis=0, concat_axis=0, tiled=True)
    grads = grads.reshape(team, depth, 3, share).transpose(2, 1, 0, 3)
    grads = grads.reshape(3, depth, hidden_width).astype(floats)

    normal_grad = normal_grad.astype(floats)
    mixed_part, second_local = norm_back(normal_grad, mixed, scale_second, gain_second)
    mixed_grad = outer_grad.astype(floats) + mixed_part
    mixed_half = mixed_grad.astype(halves)
    merge_local = lax.dot_general(
        mixed_half, attended_half, first_pair, preferred_element_type=floats
    )
    attended_grad = jnp.dot(mixed_half, merge_turned, preferred_element_type=floats).astype(halves)
    grad_group = to_groups(attended_grad.reshape(length, HEADS, HEAD_DIM))
    mass_grad = jnp.einsum("krd,nkd->krn", grad_group, value_all, preferred_element_type=floats)
    row_dots = jnp.sum(shares * mass_grad, axis=-1, keepdims=True)
    score_half = (shares * (mass_grad - row_dots)).astype(halves)
    query_sum = (
        jnp.einsum("krn,nkd->krd", score_half, key_all, preferred_element_type=floats) * SCALE
    )
    key_grad = (
        jnp.einsum("krn,krd->nkd", score_half, query_group, preferred_element_type=floats) * SCALE
    )
    value_grad = jnp.einsum("krn,krd->nkd", shares_half, grad_group, preferred_element_type=floats)
    pair_sums = jnp.concatenate(
        [key_grad.reshape(count, KEY_WIDTH), value_grad.reshape(count, KEY_WIDTH)], axis=1
    )
    pair_mine = lax.psum_scatter(
        pair_sums.astype(halves), SEQ, scatter_dimension=0, tiled=True
    ).astype(floats)
    key_back = pair_mine[:, :KEY_WIDTH].reshape(length, KV_HEADS, HEAD_DIM)
    value_back = pair_mine[:, KEY_WIDTH:]
    query_back = from_groups(query_sum, length).reshape(length, HEADS, HEAD_DIM)
    query_back = query_back * cosine + unturn_half(query_back * sine)
    key_back = key_back * cosine + unturn_half(key_back * sine)
    joint_back = jnp.concatenate(
        [query_back.reshape(length, QUERY_WIDTH), key_back.reshape(length, KEY_WIDTH), value_back],
        axis=1,
    ).astype(halves)
    joint_local = lax.dot_general(
        normal_first, joint_back, first_pair, preferred_element_type=floats
    )
    bias_local = jnp.sum(joint_back.astype(floats), axis=0)
    normal_back = lax.dot_general(joint_back, joint_all, last_pair, preferred_element_type=floats)
    residual_part, first_local = norm_back(normal_back, residual, scale_first, gain_first)
    tokens_grad = (mixed_grad + residual_part)[None]

    small_back = jnp.concatenate(
        [
            bias_local.reshape(-1, bias_depth),
            first_local.reshape(-1, depth),
            second_local.reshape(-1, depth),
        ],
        axis=1,
    )
    small_back = jnp.pad(small_back, ((0, 0), (0, depth * small_width - small_back.shape[1])))
    small_back = small_back.reshape(-1, small_width)
    packed_grad = jnp.concatenate([joint_local, merge_local, small_back], axis=1).astype(halves)
    packed_grad = lax.psum_scatter(packed_grad, AXES, scatter_dimension=0, tiled=True).astype(floats)
    joint_grad = packed_grad[:, :joint_width]
    merge_grad = packed_grad[:, joint_width : joint_width + model].T
    small_back = packed_grad[:, joint_width + model :].reshape(-1)
    bias_grad = small_back[:bias_depth]
    first_grad = small_back[bias_depth : bias_depth + depth]
    second_grad = small_back[bias_depth + depth : bias_depth + 2 * depth]
    return (
        output,
        tokens_grad,
        joint_grad,
        bias_grad,
        merge_grad,
        first_grad,
        second_grad,
        grads[0],
        grads[1],
        grads[2].T,
    )


def solution(mesh):
    seq, row = mesh.shape["seq"], mesh.shape["row"]
    fine = Mesh(mesh.devices.reshape(seq // 2, 2, row // 2, 2), AXES)
    whole = ("z", "x", "y", "c")
    placed = (
        P(ROW, SEQ, None),
        P(ROW, SEQ),
        P(whole, None),
        P(whole),
        P(None, whole),
        P(whole),
        P(whole),
        P(whole, None),
        P(whole, None),
        P(None, whole),
        P(ROW, SEQ, None),
    )
    return jax.shard_map(
        body,
        mesh=fine,
        in_specs=placed,
        out_specs=(
            P(ROW, SEQ, None),
            P(ROW, SEQ, None),
            P(whole, None),
            P(whole),
            P(None, whole),
            P(whole),
            P(whole),
            P(whole, None),
            P(whole, None),
            P(None, whole),
        ),
        check_vma=False,
    )
```

time: 1560 us -> 1020 us (0.65)
  waiting for transfers between devices: 977 us -> 598 us
  blocking collectives: 249 us -> 133 us
  matrix products: 168 us -> 115 us
  other arithmetic: 22.5 us -> 45.3 us
  starting transfers between devices: 23.6 us -> 7.01 us
    all_gather x7 -> x6, waiting for transfers between devices: 471 us -> 194 us  [the longest x1 64.3 us: body(): team_normal = lax.all_gather(normal_half, TEAM, axis=0, tiled=True)]
    all_to_all x5 -> x1, waiting for transfers between devices: 265 us -> 79 us  [body(): grads = lax.all_to_all(grads, TEAM, split_axis=0, concat_axis=0, tiled=True)]
    unnamed x14, waiting for transfers between devices: 4.43 us -> 134 us
    unnamed x2 -> x0, blocking collectives: 80.9 us -> none
    all_gather x3 -> x1, blocking collectives: 84.8 us -> 18.7 us  [body(): labels = lax.all_gather(own_labels, SEQ, axis=0, tiled=True)]
    dot_general x19 -> x15, matrix products: 155 us -> 101 us  [the longest x1 13.9 us: body(): jnp.dot(team_outer, down_turned, preferred_element_type=floats)]
    all_to_all x9 -> x0, local copies, waits for them, and re-layouts: 48.5 us -> none  [the longest x2 12.6 us: body(): lax.all_to_all(gate_part.astype(jnp.bfloat16), 'seq', split_axis=0, conca...]
    reduce_scatter x5 -> x4, waiting for transfers between devices: 237 us -> 191 us  [the longest x1 76 us: body(): lax.psum_scatter(branch.astype(halves), TEAM, scatter_dimension=0, tiled=...]
  transfers between devices with their start and end apart: 18 -> 13, of which waited for: 12 -> 11; matrix products, arithmetic and copies ran while one was open for 16% -> 21% of each run, Pallas kernels for 0% -> 0%
where the time goes in v1:
time: 1020 us; the launch traced here: 1010 us
  waiting for transfers between devices  598 us (59%)
  blocking collectives  133 us (13%)
  matrix products  115 us (11%)
  local copies, waits for them, and re-layouts  93.7 us (9%)
  other arithmetic  45.3 us (4%)
  between operations  15.5 us (2%)
    unnamed x14, waiting for transfers between devices  134 us
    all_to_all x1, blocking collectives, body(): lax.all_to_all(stacked, TEAM, split_axis=0, concat_axis=0, tiled=True)  114 us
    all_to_all x1, waiting for transfers between devices, body(): grads = lax.all_to_all(grads, TEAM, split_axis=0, concat_axis=0, tiled=True)  79 us
    reduce_scatter x1, waiting for transfers between devices, body(): lax.psum_scatter(branch.astype(halves), TEAM, scatter_dimension=0, tiled=...  76 us
    all_gather x1, waiting for transfers between devices, body(): team_normal = lax.all_gather(normal_half, TEAM, axis=0, tiled=True)  64.3 us
    reduce_scatter x1, waiting for transfers between devices, body(): lax.psum_scatter(pair_sums.astype(halves), SEQ, scatter_dimension=0, tile...  54 us
    all_gather x1, waiting for transfers between devices, body(): team_outer = lax.all_gather(outer_grad, TEAM, axis=0, tiled=True)  47.9 us
    reduce_scatter x1, waiting for transfers between devices, body(): lax.psum_scatter(packed_grad, AXES, scatter_dimension=0, tiled=True)  42.2 us
  transfers between devices with their start and end apart: 13, of which 11 were waited for; matrix products, arithmetic and copies ran while one was open for 21% of the time, Pallas kernels for 0%

profile of v1, /device:TPU:0, one launch (start us, length us, event | category | flops | bytes accessed | tf_op | source)
XLA Modules:
  0.0 1007.2 jit_solution(2145119689140950254)
XLA Ops:
  22.6 7.4 maximum_bitcast_fusion
  34.3 113.9 %all_to_all.10 = bf16[8,48,3360]{2,1,0:T(8,128)(2,1)} all-to-all(bf16[8,48,3360]{2,1,0:T(8,128)(2,1)} %reshape.317), channel_id=1, replica_groups=mesh['z'=4,'x'=2,'y'=2,'c'=2] {'z','y'}, dimensions={0} | all-to-all | bytes 5160960 | tf_op jit(solution)/shard_map/all_to_all | solution.py:130
  148.2 18.7 %all-gather = s32[1,1024]{1,0:T(1,128)S(1)} all-gather(s32[1,128]{1,0:T(1,128)S(1)} %copy-done.30), channel_id=2, replica_groups=mesh['z'=4,'x'=2,'y'=2,'c'=2] {'z','x'}, dimensions={1}, use_global_device_ids=true | all-gather | bytes 4608 | tf_op jit(solution)/shard_map/all_gather | solution.py:108
  176.5 40.1 %all-gather.15.cloned.1.call-done = bf16[4,2,2,1,48,3360]{5,4,3,2,1,0:T(8,128)(2,1)} async-done(((bf16[4,1,2,1,48,3360]{5,4,3,2,1,0:T(8,128)(2,1)}), bf16[4,2,2,1,48,3360]{5,4,3,2,1,0:T(8,128)(2,1)}) %all-gather.15.cloned.1.call-update) | async-done | bytes 5160976 | tf_op jit(solution)/shard_map/all_gather | solution.py:132
  217.8 41.7 %all-gather.11.cloned.1.call-done = bf16[1024,512]{1,0:T(8,128)(2,1)} async-done(((bf16[128,512]{1,0:T(8,128)(2,1)}), bf16[1024,512]{1,0:T(8,128)(2,1)}) %all-gather.11.cloned.1.call-update) | async-done | bytes 1048592 | tf_op jit(solution)/shard_map/all_gather | solution.py:148
  261.9 6.5 fusion.123
  268.4 5.3 fusion.48
  273.9 5.6 multiply_reduce_fusion.1
  282.4 64.3 %all-gather.13.cloned.1.call-done = bf16[1024,1536]{1,0:T(8,128)(2,1)} async-done(((bf16[128,1536]{1,0:T(8,128)(2,1)}), bf16[1024,1536]{1,0:T(8,128)(2,1)}) %all-gather.13.cloned.1.call-update) | async-done | bytes 3145744 | tf_op jit(solution)/shard_map/all_gather | solution.py:171
  346.7 13.2 %fusion.4 = f32[1024,2240]{0,1:T(8,128)} fusion(bf16[1024,1536]{1,0:T(8,128)(2,1)} %all-gather.13.cloned.1.call-done, bf16[1536,3360]{1,0:T(8,128)(2,1)} %bitcast.203), kind=kOutput, calls=%fused_computation.14 | convolution fusion | flops 7046430720 | bytes 19398656 | tf_op jit(solution)/shard_map/dot_general | solution.py:172
  359.9 47.9 %all-gather.19.cloned.1.call-done = bf16[1,1024,1536]{2,1,0:T(8,128)(2,1)} async-done(((bf16[1,128,1536]{2,1,0:T(8,128)(2,1)}), bf16[1,1024,1536]{2,1,0:T(8,128)(2,1)}) %all-gather.19.cloned.1.call-update) | async-done | bytes 3145744 | tf_op jit(solution)/shard_map/all_gather | solution.py:137
  407.8 13.9 %fusion.13 = (bf16[1024,1120]{0,1:T(8,128)(2,1)S(1)}, bf16[1024,1120]{0,1:T(8,128)(2,1)S(1)}, bf16[1024,1120]{0,1:T(8,128)(2,1)}) fusion(f32[1024,2240]{0,1:T(8,128)} %fusion.4, bf16[1,1024,1536]{2,1,0:T(8,128)(2,1)} %all-gather.19.cloned.1.call-done, bf16[1536,3360]{1,0:T(8,128)(2,1)} %bitcast.204), kind=kOutput, calls=%fused_computation.26 | convolution fusion | flops 3540418560 | bytes 22740992 | tf_op jit(solution)/shard_map/dot_general | solution.py:178
  423.8 9.3 fusion.20
  433.2 9.9 convolution_convert_fusion.4
  443.2 7.1 fusion.1
  454.6 12.4 %convolution_convert_fusion = bf16[1536,2240]{0,1:T(8,128)(2,1)} fusion(bf16[1024,1536]{1,0:T(8,128)(2,1)} %all-gather.13.cloned.1.call-done, bf16[1024,1120]{0,1:T(8,128)(2,1)} %copy-done.38, bf16[1024,1120]{0,1:T(8,128)(2,1)} %copy-done.37), kind=kOutput, calls=%fused_computation.2 | convolution fusion | flops 7059046400 | bytes 14614528 | tf_op jit(solution)/shard_map/dot_general | solution.py:186
  467.1 10.0 copy.111
  477.1 10.2 %pad_maximum_fusion.1 = bf16[4,2,2,2,48,3360]{5,4,3,2,1,0:T(8,128)(2,1)} fusion(bf16[4,2,2,2,48,1120]{5,4,3,2,1,0:T(8,128)(2,1)S(1)} %bitcast.175, bf16[4,2,2,2,48,2240]{5,4,3,2,1,0:T(8,128)(2,1)} %bitcast.173), kind=kLoop, calls=%fused_computation.3 | loop fusion | flops 20643840 | bytes 20643840 | tf_op jit(solution)/shard_map/concatenate | solution.py:188
  487.4 18.9 %reduce-scatter.9.cloned.1.call-done = bf16[128,1536]{1,0:T(8,128)(2,1)} async-done(((bf16[1024,1536]{1,0:T(8,128)(2,1)}), bf16[128,1536]{1,0:T(8,128)(2,1)}) %reduce-scatter.9.cloned.1.call-update) | async-done | bytes 393232 | tf_op jit(solution)/shard_map/reduce_scatter | solution.py:184
  507.6 76.0 %reduce-scatter.7.cloned.1.call-done = bf16[128,1536]{1,0:T(8,128)(2,1)} async-done(((bf16[1024,1536]{1,0:T(8,128)(2,1)}), bf16[128,1536]{1,0:T(8,128)(2,1)}) %reduce-scatter.7.cloned.1.call-update) | async-done | bytes 393232 | tf_op jit(solution)/shard_map/reduce_scatter | solution.py:183
  590.3 4.9 fusion.44
  596.3 5.0 multiply_reduce_fusion
  611.7 16.6 %all-reduce.7.cloned.1.call-done = bf16[4,2,2,2,48,3360]{5,4,3,2,1,0:T(8,128)(2,1)} async-done(((bf16[4,2,2,2,48,3360]{5,4,3,2,1,0:T(8,128)(2,1)}), bf16[4,2,2,2,48,3360]{5,4,3,2,1,0:T(8,128)(2,1)}) %all-reduce.7.cloned.1.call-update) | async-done | bytes 10321936
  628.4 5.9 constant_dynamic-slice_fusion.1
  642.8 54.0 %reduce-scatter.11.cloned.1.call-done = bf16[128,512]{1,0:T(8,128)(2,1)} async-done(((bf16[1024,512]{1,0:T(8,128)(2,1)}), bf16[128,512]{1,0:T(8,128)(2,1)}) %reduce-scatter.11.cloned.1.call-update) | async-done | bytes 131088 | tf_op jit(solution)/shard_map/reduce_scatter | solution.py:219
  699.5 5.1 fusion.67
  713.9 116.5 %all-reduce.9.cloned.1.call-done = bf16[4,2,2,1,48,3360]{5,4,3,2,1,0:T(8,128)(2,1)} async-done(((bf16[4,2,2,1,48,3360]{5,4,3,2,1,0:T(8,128)(2,1)}), bf16[4,2,2,1,48,3360]{5,4,3,2,1,0:T(8,128)(2,1)}) %all-reduce.9.cloned.1.call-update) | async-done | bytes 5160976
  834.6 5.9 all-to-all-start.1
  841.7 79.0 %all-to-all-done.1 = bf16[8,48,3360]{2,1,0:T(8,128)(2,1)} async-done(((bf16[8,48,3360]{2,1,0:T(8,128)(2,1)}), bf16[8,48,3360]{2,1,0:T(8,128)(2,1)}, u32[]{:S(2)}, u32[]{:S(2)}) %all-to-all-start.1) | async-done | bytes 2580512 | tf_op jit(solution)/shard_map/all_to_all | solution.py:193
  920.7 8.4 reshape.332
  929.1 13.4 %fusion.118 = (f32[1,48,8,1120]{3,0,1,2:T(1,128)S(1)}, f32[1,48,8,1120]{3,0,1,2:T(1,128)}, f32[1,48,8,1120]{3,0,1,2:T(1,128)S(1)}) fusion(f32[3,48,8,1120]{3,0,1,2:T(4,128)} %bitcast.174), kind=kLoop, calls=%fused_computation.173 | loop fusion | bytes 10321920 | tf_op jit(solution)/shard_map/slice | solution.py:267
  950.9 42.2 %reduce-scatter.13.cloned.1.call-done = bf16[48,3588]{1,0:T(8,128)(2,1)} async-done(((bf16[1536,3588]{1,0:T(8,128)(2,1)}), bf16[48,3588]{1,0:T(8,128)(2,1)}) %reduce-scatter.13.cloned.1.call-update) | async-done | bytes 344464 | tf_op jit(solution)/shard_map/reduce_scatter | solution.py:250
  (216 shorter events, 102.2 us)
Async XLA Ops:
  7.2 161.9 %all-gather.9.cloned.1.call-start = ((), (), s32[]{:S(2)}) async-start(), calls=%async_computation.6 | async-start | bytes 11759616 | tf_op jit(solution)/shard_map/all_gather | solution.py:118
  10.0 206.6 %all-gather.15.cloned.1.call-start = ((), (), s32[]{:S(2)}) async-start(), calls=%async_computation.9 | async-start | bytes 7962624 | tf_op jit(solution)/shard_map/all_gather | solution.py:132
  34.3 113.9 %copy-start.30 = (s32[1,128]{1,0:T(1,128)S(1)}, s32[1,128]{1,0:T(1,128)}, u32[]{:S(2)}) copy-start(s32[1,128]{1,0:T(1,128)} %param.12) | copy-start | bytes 1540
  34.3 134.1 %copy-start.4 = (bf16[1,128,1536]{2,1,0:T(8,128)(2,1)S(1)}, bf16[1,128,1536]{2,1,0:T(8,128)(2,1)}, u32[]{:S(2)}) copy-start(bf16[1,128,1536]{2,1,0:T(8,128)(2,1)} %param.11) | copy-start | bytes 1179652
  148.2 111.3 %all-gather.11.cloned.1.call-start = ((), (), s32[]{:S(2)}) async-start(), calls=%async_computation.7 | async-start | bytes 1179648 | tf_op jit(solution)/shard_map/all_gather | solution.py:148
  168.1 49.2 %copy-start.14 = (f32[128,128]{0,1:T(8,128)}, f32[128,128]{0,1:T(8,128)S(1)}, u32[]{:S(2)}) copy-start(f32[128,128]{0,1:T(8,128)S(1)} %get-tuple-element.38) | copy-start | bytes 196612
  168.1 49.2 %copy-start.16 = (f32[128,128]{0,1:T(8,128)}, f32[128,128]{0,1:T(8,128)S(1)}, u32[]{:S(2)}) copy-start(f32[128,128]{0,1:T(8,128)S(1)} %get-tuple-element.39) | copy-start | bytes 196612
  175.7 41.0 %copy-start.12 = (f32[128,2,128]{2,1,0:T(2,128)}, f32[128,2,128]{2,1,0:T(2,128)S(1)}, u32[]{:S(2)}) copy-start(f32[128,2,128]{2,1,0:T(2,128)S(1)} %mul.326) | copy-start | bytes 393220
  176.4 106.0 %all-gather.17.cloned.1.call-start = ((), (), s32[]{:S(2)}) async-start(), calls=%async_computation.10 | async-start | bytes 15925248 | tf_op jit(solution)/shard_map/all_gather | solution.py:133
  216.6 130.1 %all-gather.13.cloned.1.call-start = ((), (), s32[]{:S(2)}) async-start(), calls=%async_computation.8 | async-start | bytes 3538944 | tf_op jit(solution)/shard_map/all_gather | solution.py:171
  217.7 50.7 %copy-start.10 = (bf16[2,6,128,128]{3,2,1,0:T(8,128)(2,1)}, bf16[2,6,128,128]{3,2,1,0:T(8,128)(2,1)S(1)}, u32[]{:S(2)}) copy-start(bf16[2,6,128,128]{3,2,1,0:T(8,128)(2,1)S(1)} %copy.89) | copy-start | bytes 1179652
  280.1 79.8 %copy-start.26 = (f32[128]{0:T(128)}, f32[128]{0:T(128)S(1)}, u32[]{:S(2)}) copy-start(f32[128]{0:T(128)S(1)} %get-tuple-element.43) | copy-start | bytes 1540
  281.3 126.5 %all-gather.19.cloned.1.call-start = ((), (), s32[]{:S(2)}) async-start(), calls=%async_computation.15 | async-start | bytes 3538944 | tf_op jit(solution)/shard_map/all_gather | solution.py:137
  281.9 224.4 %reduce-scatter.9.cloned.1.call-start = ((), (), s32[]{:S(2)}) async-start(), calls=%async_computation.12 | async-start | bytes 3538944 | tf_op jit(solution)/shard_map/reduce_scatter | solution.py:184
  407.8 16.0 %copy-start.33 = (bf16[4,2,2,2,48,3360]{5,4,3,2,1,0:T(8,128)(2,1)S(1)}, bf16[4,2,2,2,48,3360]{5,4,3,2,1,0:T(8,128)(2,1)}, u32[]{:S(2)}) copy-start(bf16[4,2,2,2,48,3360]{5,4,3,2,1,0:T(8,128)(2,1)} %all-gather.17.cloned.1.call-done) | copy-start | bytes 30965764
  433.1 150.5 %reduce-scatter.7.cloned.1.call-start = ((), (), s32[]{:S(2)}) async-start(), calls=%async_computation.11 | async-start | bytes 3538944 | tf_op jit(solution)/shard_map/reduce_scatter | solution.py:183
  433.2 10.0 copy-start.34
  443.1 185.2 %all-reduce.7.cloned.1.call-start = ((), (), s32[]{:S(2)}) async-start(), calls=%async_computation.16 | async-start | bytes 21233664
  487.3 19.0 %copy-start.3 = (f32[128,1536]{1,0:T(8,128)S(1)}, f32[128,1536]{1,0:T(8,128)}, u32[]{:S(2)}) copy-start(f32[128,1536]{1,0:T(8,128)} %copy-done.2) | copy-start | bytes 2359300
  487.3 19.0 %copy-start.27 = (f32[128]{0:T(128)S(1)}, f32[128]{0:T(128)}, u32[]{:S(2)}) copy-start(f32[128]{0:T(128)} %copy-done.26) | copy-start | bytes 1540
  487.3 96.3 %copy-start.9 = (bf16[1,128,1536]{2,1,0:T(8,128)(2,1)S(1)}, bf16[1,128,1536]{2,1,0:T(8,128)(2,1)}, u32[]{:S(2)}) copy-start(bf16[1,128,1536]{2,1,0:T(8,128)(2,1)} %param.21) | copy-start | bytes 1179652
  487.3 96.3 %copy-start.31 = (f32[128]{0:T(128)S(1)}, f32[128]{0:T(128)}, u32[]{:S(2)}) copy-start(f32[128]{0:T(128)} %get-tuple-element.42) | copy-start | bytes 1540
  487.4 209.5 %reduce-scatter.11.cloned.1.call-start = ((), (), s32[]{:S(2)}) async-start(), calls=%async_computation.13 | async-start | bytes 1179648 | tf_op jit(solution)/shard_map/reduce_scatter | solution.py:219
  610.8 219.6 %all-reduce.9.cloned.1.call-start = ((), (), s32[]{:S(2)}) async-start(), calls=%async_computation.17 | async-start | bytes 10616832
  634.3 358.8 %reduce-scatter.13.cloned.1.call-start = ((), (), s32[]{:S(2)}) async-start(), calls=%async_computation.14 | async-start | bytes 11759616 | tf_op jit(solution)/shard_map/reduce_scatter | solution.py:250
  639.2 58.7 %copy-start.21 = (f32[128,128]{1,0:T(8,128)S(1)}, f32[128,128]{1,0:T(8,128)}, u32[]{:S(2)}) copy-start(f32[128,128]{1,0:T(8,128)} %copy-done.20) | copy-start | bytes 196612
  639.2 59.2 %copy-start.13 = (f32[128,2,128]{2,1,0:T(2,128)S(1)}, f32[128,2,128]{2,1,0:T(2,128)}, u32[]{:S(2)}) copy-start(f32[128,2,128]{2,1,0:T(2,128)} %copy-done.12) | copy-start | bytes 393220
  639.2 60.2 %copy-start.5 = (bf16[1,128,1536]{2,1,0:T(8,128)(2,1)S(1)}, bf16[1,128,1536]{2,1,0:T(8,128)(2,1)}, u32[]{:S(2)}) copy-start(bf16[1,128,1536]{2,1,0:T(8,128)(2,1)} %param.11) | copy-start | bytes 1179652
  639.2 60.2 %copy-start.25 = (f32[1536]{0:T(1024)S(1)}, f32[1536]{0:T(1024)}, u32[]{:S(2)}) copy-start(f32[1536]{0:T(1024)} %copy-done.24) | copy-start | bytes 18436
  639.2 60.2 %copy-start.29 = (f32[128]{0:T(128)S(1)}, f32[128]{0:T(128)}, u32[]{:S(2)}) copy-start(f32[128]{0:T(128)} %copy-done.28) | copy-start | bytes 1540
  830.4 10.0 copy-start.32
  834.6 86.1 %all-to-all-start.1 = ((bf16[8,48,3360]{2,1,0:T(8,128)(2,1)}), bf16[8,48,3360]{2,1,0:T(8,128)(2,1)}, u32[]{:S(2)}, u32[]{:S(2)}) async-start(bf16[8,48,3360]{2,1,0:T(8,128)(2,1)} %bitcast.177), calls=%async_computation.5 | async-start | bytes 5308416 | tf_op jit(solution)/shard_map/all_to_all | solution.py:193
  (22 other events, 88.3 us)
Sparse Core Ops, SparseCore 0:
  11.5 136.1 all-gather.8
  149.2 67.3 all-gather.14
  219.3 40.1 all-gather.10
  260.9 21.4 all-gather.16
  285.0 61.6 all-gather.12
  348.7 59.0 all-gather.18
  433.2 73.0 reduce-scatter.8
  509.9 73.6 reduce-scatter.6
  586.2 42.1 all-reduce.6
  632.2 64.6 reduce-scatter.10
  699.5 130.9 all-reduce.8
  837.4 155.7 reduce-scatter.12

commit v2 on v1

--- a/solution.py
+++ b/solution.py
@@ -1,8 +1,11 @@
+import functools
 import math
 
 import jax
 import jax.numpy as jnp
 from jax import lax
+from jax.experimental import pallas as pl
+from jax.experimental.pallas import tpu as pltpu
 from jax.sharding import Mesh, PartitionSpec as P
 
 HEADS = 12
@@ -81,6 +84,353 @@
     part = scale * scaled - values * (scale * scale * scale) * inner
     gain_grad = jnp.sum(upstream * values * scale, axis=0)
     return part, gain_grad
+
+
+MESH = pl.DeviceIdType.MESH
+VMEM_LIMIT = 60 * 2**20
+
+
+def coordinates():
+    return tuple(lax.axis_index(name) for name in AXES)
+
+
+class Courier:
+    def __init__(self, sends, receives):
+        self.sends, self.receives, self.copies, self.settled = sends, receives, [], 0
+
+    def copy(self, source, target, device):
+        place = len(self.copies)
+        made = pltpu.make_async_remote_copy(
+            src_ref=source,
+            dst_ref=target,
+            send_sem=self.sends.at[place],
+            recv_sem=self.receives.at[place],
+            device_id=device,
+            device_id_type=MESH,
+        )
+        made.start()
+        self.copies.append(made)
+        return made
+
+    def finish(self):
+        for made in self.copies[self.settled :]:
+            made.wait_send()
+        self.settled = len(self.copies)
+
+
+def meet(devices):
+    barrier = pltpu.get_barrier_semaphore()
+    for device in devices:
+        pl.semaphore_signal(barrier, inc=1, device_id=device, device_id_type=MESH)
+    pl.semaphore_wait(barrier, len(devices))
+
+
+def cuts_of(width, step):
+    return [(start, min(step, width - start)) for start in range(0, width, step)]
+
+
+def forward_kernel(
+    nz,
+    stack_ref,
+    normal_ref,
+    outer_ref,
+    branch_ref,
+    back_ref,
+    grads_ref,
+    w,
+    xn,
+    ct,
+    hid,
+    gb,
+    ub,
+    part,
+    ybuf,
+    zsend,
+    zbuf,
+    cbuf,
+    xbuf,
+    gbuf,
+    sends,
+    receives,
+    locals_,
+):
+    z, x, y, c = coordinates()
+    length, model = normal_ref.shape
+    share = w.shape[-1]
+    block = model // nz
+    courier = Courier(sends, receives)
+    across_x, across_y, across_c = (z, 1 - x, y, c), (z, x, 1 - y, c), (z, x, y, 1 - c)
+
+    def source(dz):
+        return lax.rem(z + nz - dz, nz)
+
+    team = [(dz, dy) for dz in range(nz) for dy in range(2)]
+    meet(
+        [(lax.rem(z + dz, nz), x, lax.rem(y + dy, 2), c) for dz, dy in team[1:]]
+        + [across_x, across_c]
+    )
+
+    def columns(tz, ty):
+        return pl.ds(pl.multiple_of((tz * 2 + ty) * share, 128), share)
+
+    own = pltpu.make_async_copy(
+        stack_ref.at[:, :, columns(z, y)], w.at[:, z, x * 2 + y, c], locals_.at[0]
+    )
+    own.start()
+    direct = {}
+    for dz, dy in team[1:]:
+        tz, ty = lax.rem(z + dz, nz), lax.rem(y + dy, 2)
+        direct[dz, dy] = courier.copy(
+            stack_ref.at[:, :, columns(tz, ty)], w.at[:, z, x * 2 + y, c], (tz, x, ty, c)
+        )
+
+    rows_mine, rows_other = pl.ds(y * length, length), pl.ds((1 - y) * length, length)
+    arriving = {}
+    for mine, team_buffer, name in ((outer_ref, ct, "outer"), (normal_ref, xn, "normal")):
+        team_buffer[z, rows_mine, :] = mine[...]
+        along = {}
+        for dz in range(1, nz):
+            along[dz] = courier.copy(
+                mine, team_buffer.at[z, rows_mine], (lax.rem(z + dz, nz), x, y, c)
+            )
+        side = {0: courier.copy(mine, team_buffer.at[z, rows_mine], across_y)}
+        arriving[name] = (along, side)
+    for dz in range(1, nz):
+        for team_buffer, name in ((ct, "outer"), (xn, "normal")):
+            along, side = arriving[name]
+            along[dz].wait_recv()
+            spot = team_buffer.at[source(dz), rows_mine]
+            side[dz] = courier.copy(spot, spot, across_y)
+
+    crossed, handed = {}, []
+    own.wait()
+    for dz, dy in team:
+        if (dz, dy) != (0, 0):
+            direct[dz, dy].wait_recv()
+        sy = lax.rem(y + dy, 2)
+        spot = w.at[:, source(dz), x * 2 + sy, c]
+        crossed[dz, dy] = courier.copy(spot, spot, across_x)
+        handed.append(courier.copy(spot, spot, across_c))
+    for dz, dy in team:
+        crossed[dz, dy].wait_recv()
+        sy = lax.rem(y + dy, 2)
+        spot = w.at[:, source(dz), (1 - x) * 2 + sy, c]
+        handed.append(courier.copy(spot, spot, across_c))
+    for made in handed:
+        made.wait_recv()
+    for name in ("outer", "normal"):
+        for made in arriving[name][1].values():
+            made.wait_recv()
+    courier.finish()
+
+    def weight(which, start, size):
+        return w[which, :, :, :, :, start : start + size].reshape(model, size)
+
+    scatter = []
+    for dz in range(nz):
+        group = source(dz)
+        for start, size in cuts_of(share, 256):
+            normal = xn[group]
+            outer = ct[group]
+            gate = jnp.dot(normal, weight(0, start, size), preferred_element_type=floats)
+            upper = jnp.dot(normal, weight(1, start, size), preferred_element_type=floats)
+            hidden_back = jnp.dot(outer, weight(2, start, size), preferred_element_type=floats)
+            sig = 1.0 / (1.0 + jnp.exp(-gate))
+            silu = gate * sig
+            spot = (group, slice(None), slice(start, start + size))
+            hid[spot] = (silu * upper).astype(halves)
+            gb[spot] = (hidden_back * upper * (sig * (1.0 + gate * (1.0 - sig)))).astype(halves)
+            ub[spot] = (hidden_back * silu).astype(halves)
+        half = nz // 2
+
+        @pl.loop(0, 2)
+        def _(step):
+            rows = pl.ds(step * half, half)
+            lanes = pl.ds(pl.multiple_of(step * (model // 2), 128), model // 2)
+
+            def turned(which):
+                return w[which, rows].reshape(model // 2, share)
+
+            part[0, group, :, lanes] = (
+                lax.dot_general(gb[group], turned(0), last_pair, preferred_element_type=floats)
+                + lax.dot_general(ub[group], turned(1), last_pair, preferred_element_type=floats)
+            ).astype(halves)
+            part[1, group, :, lanes] = lax.dot_general(
+                hid[group], turned(2), last_pair, preferred_element_type=floats
+            ).astype(halves)
+
+        for which in range(2):
+            scatter.append(
+                courier.copy(
+                    part.at[which, group, rows_other], ybuf.at[which, group], across_y
+                )
+            )
+
+    final = {}
+    for dz in range(nz):
+        group = source(dz)
+        for which in range(2):
+            scatter[2 * dz + which].wait_recv()
+            total = part[which, group, rows_mine, :].astype(floats) + ybuf[which, group].astype(floats)
+            if dz == 0:
+                (back_ref, branch_ref)[which][...] = total
+            else:
+                zsend[which, dz - 1] = total.astype(halves)
+                final[which, dz] = courier.copy(
+                    zsend.at[which, dz - 1], zbuf.at[which, dz - 1], (group, x, y, c)
+                )
+
+    lines = 2 * length * nz
+    moved = {}
+    orders = [(dz + nz // 2) % nz for dz in range(nz)]
+    for dz in orders:
+        group = lax.rem(z + dz, nz)
+        lanes = pl.ds(pl.multiple_of(group * block, 128), block)
+        normal_turned = xn[:, :, lanes].reshape(lines, block).T
+        outer_turned = ct[:, :, lanes].reshape(lines, block).T
+        for which, left, right in ((0, normal_turned, gb), (1, normal_turned, ub), (2, outer_turned, hid)):
+            for start, size in cuts_of(share, 512):
+                w[which, group, :, :, :, start : start + size] = (
+                    jnp.dot(
+                        left,
+                        right[:, :, start : start + size].reshape(lines, size),
+                        preferred_element_type=floats,
+                    )
+                    .astype(halves)
+                    .reshape(4, 2, -1, size)
+                )
+        moved[dz] = courier.copy(w.at[:, group, :, 1 - c], cbuf.at[dz], across_c)
+    crossing = {}
+    for dz in orders:
+        group = lax.rem(z + dz, nz)
+        moved[dz].wait_recv()
+        for which in range(3):
+            w[which, group, :, c] = (
+                w[which, group, :, c].astype(floats) + cbuf[dz, which].astype(floats)
+            ).astype(halves)
+        crossing[dz] = courier.copy(
+            w.at[:, group, pl.ds((1 - x) * 2, 2), c], xbuf.at[dz], across_x
+        )
+    arrived = []
+    for dz in orders:
+        group = lax.rem(z + dz, nz)
+        crossing[dz].wait_recv()
+        for dy in range(2):
+            ty = lax.rem(y + dy, 2)
+            for which in range(3):
+                total = w[which, group, x * 2 + ty, c].astype(floats) + xbuf[dz, which, ty].astype(floats)
+                if (dz, dy) == (0, 0):
+                    gbuf[z * 2 + y, which] = total.astype(halves)
+                else:
+                    w[which, group, x * 2 + ty, c] = total.astype(halves)
+            if (dz, dy) != (0, 0):
+                arrived.append(
+                    courier.copy(
+                        w.at[:, group, x * 2 + ty, c], gbuf.at[z * 2 + y], (group, x, ty, c)
+                    )
+                )
+    for which, target in ((0, back_ref), (1, branch_ref)):
+        for dz in range(1, nz):
+            final[which, dz].wait_recv()
+            target[...] += zbuf[which, dz - 1].astype(floats)
+    for made in arrived:
+        made.wait_recv()
+    for member in range(2 * nz):
+        for which in range(3):
+            grads_ref[which, :, member * share : (member + 1) * share] = gbuf[member, which]
+    courier.finish()
+
+
+def padded_share(hidden_width, team):
+    return -(-hidden_width // (team * 128)) * 128
+
+
+def feed_forward_kernel(normal_half, outer_grad, gate_matrix, up_matrix, down_matrix):
+    length, model = normal_half.shape
+    depth, hidden_width = gate_matrix.shape
+    nz = lax.axis_size("z")
+    share = padded_share(hidden_width, 2 * nz)
+    stack = jnp.stack([gate_matrix, up_matrix, down_matrix.T])
+    stack = jnp.pad(stack, ((0, 0), (0, 0), (0, 2 * nz * share - hidden_width)))
+    vmem = pl.BlockSpec(memory_space=pltpu.VMEM)
+    lines = 2 * length
+    copies = 31 + 14 + 14 + 15
+    branch, back, grads = pl.pallas_call(
+        functools.partial(forward_kernel, nz),
+        name="feed_forward",
+        out_shape=(
+            jax.ShapeDtypeStruct((length, model), floats),
+            jax.ShapeDtypeStruct((length, model), floats),
+            jax.ShapeDtypeStruct((3, depth, 2 * nz * share), halves),
+        ),
+        in_specs=[pl.BlockSpec(memory_space=pl.ANY), vmem, vmem],
+        out_specs=(vmem, vmem, vmem),
+        scratch_shapes=[
+            pltpu.VMEM((3, nz, 4, 2, depth, share), halves),
+            pltpu.VMEM((nz, lines, model), halves),
+            pltpu.VMEM((nz, lines, model), halves),
+            pltpu.VMEM((nz, lines, share), halves),
+            pltpu.VMEM((nz, lines, share), halves),
+            pltpu.VMEM((nz, lines, share), halves),
+            pltpu.VMEM((2, nz, lines, model), halves),
+            pltpu.VMEM((2, nz, length, model), halves),
+            pltpu.VMEM((2, nz - 1, length, model), halves),
+            pltpu.VMEM((2, nz - 1, length, model), halves),
+            pltpu.VMEM((nz, 3, 4, depth, share), halves),
+            pltpu.VMEM((nz, 3, 2, depth, share), halves),
+            pltpu.VMEM((2 * nz, 3, depth, share), halves),
+            pltpu.SemaphoreType.DMA((copies,)),
+            pltpu.SemaphoreType.DMA((copies,)),
+            pltpu.SemaphoreType.DMA((1,)),
+        ],
+        compiler_params=pltpu.CompilerParams(
+            collective_id=0, has_side_effects=True, vmem_limit_bytes=VMEM_LIMIT
+        ),
+    )(stack, normal_half, outer_grad)
+    return branch, back, grads[:, :, :hidden_width].astype(floats)
+
+
+def feed_forward_plain(normal_half, outer_grad, gate_matrix, up_matrix, down_matrix):
+    model = normal_half.shape[1]
+    depth, hidden_width = gate_matrix.shape
+    z_count = lax.axis_size("z")
+    team = lax.axis_size(TEAM)
+    share = hidden_width // team
+    stacked = jnp.stack([gate_matrix, up_matrix, down_matrix.T], axis=1)
+    stacked = stacked.reshape(depth, 3, team, share).transpose(2, 0, 1, 3)
+    stacked = stacked.reshape(team, depth, 3 * share)
+    stacked = lax.all_to_all(stacked, TEAM, split_axis=0, concat_axis=0, tiled=True)
+    stacked = stacked.reshape(z_count, 1, team // z_count, 1, depth, 3 * share)
+    stacked = lax.all_gather(stacked, "x", axis=1, tiled=True)
+    stacked = lax.all_gather(stacked, "c", axis=3, tiled=True)
+    stacked = stacked.reshape(model, 3 * share)
+    both_all, down_turned = stacked[:, : 2 * share], stacked[:, 2 * share :]
+    team_outer = lax.all_gather(outer_grad, TEAM, axis=0, tiled=True)
+    team_normal = lax.all_gather(normal_half, TEAM, axis=0, tiled=True)
+    both = jnp.dot(team_normal, both_all, preferred_element_type=floats)
+    gate, upper = both[:, :share], both[:, share:]
+    sig = jax.nn.sigmoid(gate)
+    silu = gate * sig
+    hidden_half = (silu * upper).astype(halves)
+    branch = lax.dot_general(hidden_half, down_turned, last_pair, preferred_element_type=floats)
+    hidden_grad = jnp.dot(team_outer, down_turned, preferred_element_type=floats)
+    gate_half = (hidden_grad * upper * sig * (1.0 + gate * (1.0 - sig))).astype(halves)
+    upper_half = (hidden_grad * silu).astype(halves)
+    both_half = jnp.concatenate([gate_half, upper_half], axis=1)
+    normal_grad = lax.dot_general(both_half, both_all, last_pair, preferred_element_type=floats)
+    branch = lax.psum_scatter(branch.astype(halves), TEAM, scatter_dimension=0, tiled=True)
+    normal_grad = lax.psum_scatter(normal_grad.astype(halves), TEAM, scatter_dimension=0, tiled=True)
+    both_grad = lax.dot_general(team_normal, both_half, first_pair, preferred_element_type=floats)
+    down_grad = lax.dot_general(team_outer, hidden_half, first_pair, preferred_element_type=floats)
+    grads = jnp.concatenate([both_grad, down_grad], axis=1).astype(halves)
+    grads = grads.reshape(z_count, 2, team // z_count, 2, depth, 3 * share)
+    grads = lax.psum_scatter(grads, "c", scatter_dimension=3, tiled=True)
+    grads = lax.psum_scatter(grads, "x", scatter_dimension=1, tiled=True)
+    grads = grads.reshape(team, depth, 3 * share)
+    grads = lax.all_to_all(grads, TEAM, split_axis=0, concat_axis=0, tiled=True)
+    grads = grads.reshape(team, depth, 3, share).transpose(2, 1, 0, 3)
+    grads = grads.reshape(3, depth, hidden_width).astype(floats)
+    return branch.astype(floats), normal_grad.astype(floats), grads
 
 
 def body(
@@ -100,10 +450,6 @@
     length, model = residual.shape
     depth = joint_matrix.shape[0]
     joint_width = joint_matrix.shape[1]
-    hidden_width = gate_matrix.shape[1]
-    z_count = lax.axis_size("z")
-    team = lax.axis_size(TEAM)
-    share = hidden_width // team
     own_labels = segments[0]
     labels = lax.all_gather(own_labels, SEQ, axis=0, tiled=True)
     offset = lax.axis_index(SEQ) * length
@@ -124,17 +470,7 @@
     gain_first = small[:, bias_depth : bias_depth + depth].reshape(-1)
     gain_second = small[:, bias_depth + depth : bias_depth + 2 * depth].reshape(-1)
 
-    stacked = jnp.stack([gate_matrix, up_matrix, down_matrix.T], axis=1)
-    stacked = stacked.reshape(depth, 3, team, share).transpose(2, 0, 1, 3)
-    stacked = stacked.reshape(team, depth, 3 * share)
-    stacked = lax.all_to_all(stacked, TEAM, split_axis=0, concat_axis=0, tiled=True)
-    stacked = stacked.reshape(z_count, 1, team // z_count, 1, depth, 3 * share)
-    stacked = lax.all_gather(stacked, "x", axis=1, tiled=True)
-    stacked = lax.all_gather(stacked, "c", axis=3, tiled=True)
-    stacked = stacked.reshape(model, 3 * share)
-    both_all, down_turned = stacked[:, : 2 * share], stacked[:, 2 * share :]
     outer_grad = cotangent[0]
-    team_outer = lax.all_gather(outer_grad, TEAM, axis=0, tiled=True)
 
     scale_first = norm_parts(residual)
     normal_first = (residual * scale_first * gain_first).astype(halves)
@@ -168,33 +504,15 @@
     scale_second = norm_parts(mixed)
     normal_half = (mixed * scale_second * gain_second).astype(halves)
 
-    team_normal = lax.all_gather(normal_half, TEAM, axis=0, tiled=True)
-    both = jnp.dot(team_normal, both_all, preferred_element_type=floats)
-    gate, upper = both[:, :share], both[:, share:]
-    sig = jax.nn.sigmoid(gate)
-    silu = gate * sig
-    hidden_half = (silu * upper).astype(halves)
-    branch = lax.dot_general(hidden_half, down_turned, last_pair, preferred_element_type=floats)
-    hidden_grad = jnp.dot(team_outer, down_turned, preferred_element_type=floats)
-    gate_half = (hidden_grad * upper * sig * (1.0 + gate * (1.0 - sig))).astype(halves)
-    upper_half = (hidden_grad * silu).astype(halves)
-    both_half = jnp.concatenate([gate_half, upper_half], axis=1)
-    normal_grad = lax.dot_general(both_half, both_all, last_pair, preferred_element_type=floats)
-    branch = lax.psum_scatter(branch.astype(halves), TEAM, scatter_dimension=0, tiled=True)
-    normal_grad = lax.psum_scatter(normal_grad.astype(halves), TEAM, scatter_dimension=0, tiled=True)
-    output = (mixed + branch.astype(floats)).astype(halves)[None]
-    both_grad = lax.dot_general(team_normal, both_half, first_pair, preferred_element_type=floats)
-    down_grad = lax.dot_general(team_outer, hidden_half, first_pair, preferred_element_type=floats)
-    grads = jnp.concatenate([both_grad, down_grad], axis=1).astype(halves)
-    grads = grads.reshape(z_count, 2, team // z_count, 2, depth, 3 * share)
-    grads = lax.psum_scatter(grads, "c", scatter_dimension=3, tiled=True)
-    grads = lax.psum_scatter(grads, "x", scatter_dimension=1, tiled=True)
-    grads = grads.reshape(team, depth, 3 * share)
-    grads = lax.all_to_all(grads, TEAM, split_axis=0, concat_axis=0, tiled=True)
-    grads = grads.reshape(team, depth, 3, share).transpose(2, 1, 0, 3)
-    grads = grads.reshape(3, depth, hidden_width).astype(floats)
-
-    normal_grad = normal_grad.astype(floats)
+    if depth % 16 == 0:
+        feed_forward = feed_forward_kernel
+    else:
+        feed_forward = feed_forward_plain
+    branch, normal_grad, grads = feed_forward(
+        normal_half, outer_grad, gate_matrix, up_matrix, down_matrix
+    )
+    output = (mixed + branch).astype(halves)[None]
+
     mixed_part, second_local = norm_back(normal_grad, mixed, scale_second, gain_second)
     mixed_grad = outer_grad.astype(floats) + mixed_part
     mixed_half = mixed_grad.astype(halves)

time: 1020 us -> 797 us (0.78)
  Pallas kernels: 0 us -> 356 us
  waiting for transfers between devices: 598 us -> 296 us
  blocking collectives: 133 us -> 22.3 us
  local copies, waits for them, and re-layouts: 93.7 us -> 20.6 us
  matrix products: 115 us -> 44.3 us
    pallas_call x0 -> x1, Pallas kernels: none -> 356 us  [feed_forward_kernel(): pl.pallas_call(functools.partial(forward_kernel, nz), name='feed_forward'...]
    all_gather x4 -> x0, waiting for transfers between devices: 152 us -> none  [the longest x1 64.3 us: body(): team_normal = lax.all_gather(normal_half, TEAM, axis=0, tiled=True)]
    unnamed x14 -> x4, waiting for transfers between devices: 134 us -> 0.07 us
    all_to_all x1 -> x0, blocking collectives: 114 us -> none  [body(): lax.all_to_all(stacked, TEAM, split_axis=0, concat_axis=0, tiled=True)]
    reduce_scatter x1, waiting for transfers between devices: 42.2 us -> 139 us  [body(): lax.psum_scatter(packed_grad, AXES, scatter_dimension=0, tiled=True)]
    reduce_scatter x2 -> x0, waiting for transfers between devices: 95 us -> none  [the longest x1 76 us: body(): lax.psum_scatter(branch.astype(halves), TEAM, scatter_dimension=0, tiled=...]
    all_to_all x1 -> x0, waiting for transfers between devices: 79 us -> none  [body(): grads = lax.all_to_all(grads, TEAM, split_axis=0, concat_axis=0, tiled=True)]
    all_gather x1, waiting for transfers between devices: 0.01 us -> 69.7 us  [body(): packed = lax.all_gather(packed, AXES, axis=0, tiled=True)]
  transfers between devices with their start and end apart: 13 -> 4, of which waited for: 11 -> 4; matrix products, arithmetic and copies ran while one was open for 21% -> 3% of each run, Pallas kernels for 0% -> 0%
where the time goes in v2:
time: 797 us; the launch traced here: 793 us
  Pallas kernels  356 us (45%)
  waiting for transfers between devices  296 us (37%)
  matrix products  44.3 us (6%)
  other arithmetic  38.6 us (5%)
  blocking collectives  22.3 us (3%)
  local copies, waits for them, and re-layouts  20.6 us (3%)
  between operations  14.6 us (2%)
    pallas_call x1, Pallas kernels, feed_forward_kernel(): pl.pallas_call(functools.partial(forward_kernel, nz), name='feed_forward'...  356 us
    reduce_scatter x1, waiting for transfers between devices, body(): lax.psum_scatter(packed_grad, AXES, scatter_dimension=0, tiled=True)  139 us
    all_gather x1, waiting for transfers between devices, body(): packed = lax.all_gather(packed, AXES, axis=0, tiled=True)  69.7 us
    reduce_scatter x1, waiting for transfers between devices, body(): lax.psum_scatter(pair_sums.astype(halves), SEQ, scatter_dimension=0, tile...  52.3 us
    all_gather x1, waiting for transfers between devices, body(): lax.all_gather(jnp.concatenate([keys, values], axis=1), SEQ, axis=0, tile...  34.3 us
    all_gather x1, blocking collectives, body(): labels = lax.all_gather(own_labels, SEQ, axis=0, tiled=True)  22.3 us
  transfers between devices with their start and end apart: 4, of which 4 were waited for; matrix products, arithmetic and copies ran while one was open for 3% of the time, Pallas kernels for 0%

profile of v2, /device:TPU:0, one launch (start us, length us, event | category | flops | bytes accessed | tf_op | source)
XLA Modules:
  0.0 792.7 jit_solution(1048380825226886331)
XLA Ops:
  8.1 1.8 pad_maximum_fusion.4
  10.0 22.3 %all-gather = s32[1,1024]{1,0:T(1,128)S(1)} all-gather(s32[1,128]{1,0:T(1,128)} %param.12), channel_id=2, replica_groups=mesh['z'=4,'x'=2,'y'=2,'c'=2] {'z','x'}, dimensions={1}, use_global_device_ids=true | all-gather | bytes 4608 | tf_op jit(solution)/shard_map/all_gather | solution.py:454
  35.3 69.7 %all-gather.4.cloned.1.call-done = bf16[1536,3588]{1,0:T(8,128)(2,1)} async-done(((bf16[48,3588]{1,0:T(8,128)(2,1)}), bf16[1536,3588]{1,0:T(8,128)(2,1)}) %all-gather.4.cloned.1.call-update) | async-done | bytes 11022352 | tf_op jit(solution)/shard_map/all_gather | solution.py:464
  106.7 4.0 fusion.21
  112.8 2.7 fusion.17.stack_ref
  116.4 34.3 %all-gather.6.cloned.1.call-done = bf16[1024,512]{1,0:T(8,128)(2,1)} async-done(((bf16[128,512]{1,0:T(8,128)(2,1)}), bf16[1024,512]{1,0:T(8,128)(2,1)}) %all-gather.6.cloned.1.call-update) | async-done | bytes 1048592 | tf_op jit(solution)/shard_map/all_gather | solution.py:484
  150.8 1.4 slice_bitcast_fusion.4
  152.4 5.7 fusion.100
  158.1 3.9 fusion.35
  162.3 4.2 multiply_reduce_fusion.3
  167.4 355.9 %feed_forward.1 = (f32[128,1536]{1,0:T(8,128)}, f32[128,1536]{1,0:T(8,128)}, bf16[3,48,9216]{2,1,0:T(8,128)(2,1)}) custom-call(bf16[3,48,9216]{2,1,0:T(8,128)(2,1)} %fusion.17.stack_ref, bf16[128,1536]{1,0:T(8,128)(2,1)} %multiply_convert_fusion.1.normal_ref, bf16[128,1536]{1,0:T(8,128)(2,1)} %bitcast.142), custom_call_target="tpu_custom_call" | custom-call | tf_op jit(solution)/shard_map/feed_forward/pallas_call | solution.py:358
  523.4 1.4 multiply_reduce_fusion.1
  524.8 2.5 subtract_add_fusion
  528.1 3.1 fusion.24
  532.4 4.1 multiply_reduce_fusion
  536.7 1.7 fusion.31
  538.4 3.4 multiply_convert_fusion
  541.8 1.5 fusion.34
  543.3 2.0 copy.55
  545.3 2.0 copy.56
  547.4 2.2 pad_maximum_fusion.1
  549.7 2.9 convolution_multiply_fusion.1
  552.6 1.5 copy.44
  555.4 3.6 convolution_convert_fusion.1
  559.0 52.3 %reduce-scatter.3.cloned.1.call-done = bf16[128,512]{1,0:T(8,128)(2,1)} async-done(((bf16[1024,512]{1,0:T(8,128)(2,1)}), bf16[128,512]{1,0:T(8,128)(2,1)}) %reduce-scatter.3.cloned.1.call-update) | async-done | bytes 131088 | tf_op jit(solution)/shard_map/reduce_scatter | solution.py:537
  613.9 4.6 convolution_convert_fusion
  618.8 5.1 fusion.47
  624.6 9.7 %pad_maximum_fusion = bf16[1536,3588]{1,0:T(8,128)(2,1)} fusion(bf16[1536,4]{1,0:T(8,128)(2,1)S(1)} %reshape.290, bf16[1536,1536]{1,0:T(8,128)(2,1)} %convolution_convert_fusion.1, bf16[1536,2048]{1,0:T(8,128)(2,1)} %convolution_convert_fusion), kind=kLoop, calls=%fused_computation.1 | loop fusion | flops 33067008 | bytes 22044672 | tf_op jit(solution)/shard_map/concatenate | solution.py:567
  634.3 2.1 slice_convert_fusion
  636.4 2.4 slice_bitcast_fusion
  640.1 139.2 %reduce-scatter.5.cloned.1.call-done = bf16[48,3588]{1,0:T(8,128)(2,1)} async-done(((bf16[1536,3588]{1,0:T(8,128)(2,1)}), bf16[48,3588]{1,0:T(8,128)(2,1)}) %reduce-scatter.5.cloned.1.call-update) | async-done | bytes 344464 | tf_op jit(solution)/shard_map/reduce_scatter | solution.py:568
  784.3 1.7 slice.185
  (132 shorter events, 23.0 us)
Async XLA Ops:
  7.2 97.9 %all-gather.4.cloned.1.call-start = ((), (), s32[]{:S(2)}) async-start(), calls=%async_computation.2 | async-start | bytes 11759616 | tf_op jit(solution)/shard_map/all_gather | solution.py:464
  9.9 140.9 %all-gather.6.cloned.1.call-start = ((), (), s32[]{:S(2)}) async-start(), calls=%async_computation.3 | async-start | bytes 1179648 | tf_op jit(solution)/shard_map/all_gather | solution.py:484
  33.4 82.5 %copy-start.11 = (f32[128,128]{0,1:T(8,128)}, f32[128,128]{0,1:T(8,128)S(1)}, u32[]{:S(2)}) copy-start(f32[128,128]{0,1:T(8,128)S(1)} %get-tuple-element.41) | copy-start | bytes 196612
  33.4 82.5 %copy-start.13 = (f32[128,128]{0,1:T(8,128)}, f32[128,128]{0,1:T(8,128)S(1)}, u32[]{:S(2)}) copy-start(f32[128,128]{0,1:T(8,128)S(1)} %get-tuple-element.42) | copy-start | bytes 196612
  33.5 77.5 %copy-start.15 = (f32[128,128]{1,0:T(8,128)}, f32[128,128]{1,0:T(8,128)S(1)}, u32[]{:S(2)}) copy-start(f32[128,128]{1,0:T(8,128)S(1)} %copy.36) | copy-start | bytes 196612
  106.5 6.1 copy-start.21
  106.5 6.3 copy-start.14
  111.3 4.5 copy-start.9
  112.1 499.3 %reduce-scatter.3.cloned.1.call-start = ((), (), s32[]{:S(2)}) async-start(), calls=%async_computation.4 | async-start | bytes 1179648 | tf_op jit(solution)/shard_map/reduce_scatter | solution.py:537
  116.3 41.8 %copy-start.7 = (bf16[2,6,128,128]{3,2,1,0:T(8,128)(2,1)}, bf16[2,6,128,128]{3,2,1,0:T(8,128)(2,1)S(1)}, u32[]{:S(2)}) copy-start(bf16[2,6,128,128]{3,2,1,0:T(8,128)(2,1)S(1)} %copy.34) | copy-start | bytes 1179652
  152.1 6.0 copy-start.3
  152.1 6.0 copy-start.17
  158.1 378.4 %copy-start.20 = (f32[2,768]{1,0:T(2,128)}, f32[2,768]{1,0:T(2,128)S(1)}, u32[]{:S(2)}) copy-start(f32[2,768]{1,0:T(2,128)S(1)} %get-tuple-element.47) | copy-start | bytes 18436
  158.1 4.1 copy-start.2
  162.3 362.5 %copy-start.4 = (bf16[2,6,128,128]{2,3,1,0:T(8,128)(2,1)}, bf16[2,6,128,128]{2,3,1,0:T(8,128)(2,1)S(1)}, u32[]{:S(2)}) copy-start(bf16[2,6,128,128]{2,3,1,0:T(8,128)(2,1)S(1)} %copy.39) | copy-start | bytes 1179652
  162.3 362.5 %copy-start.6 = (bf16[1,128,1536]{2,1,0:T(8,128)(2,1)S(1)}, bf16[1,128,1536]{2,1,0:T(8,128)(2,1)}, u32[]{:S(2)}) copy-start(bf16[1,128,1536]{2,1,0:T(8,128)(2,1)} %param.21) | copy-start | bytes 1179652
  524.7 7.7 copy-start.18
  527.2 0.9 copy-start
  531.5 5.1 slice-start
  532.4 4.3 slice-start.1
  532.4 4.3 copy-start.19
  538.4 3.5 copy-start.8
  549.6 229.7 %reduce-scatter.5.cloned.1.call-start = ((), (), s32[]{:S(2)}) async-start(), calls=%async_computation.5 | async-start | bytes 11759616 | tf_op jit(solution)/shard_map/reduce_scatter | solution.py:568
  552.6 2.6 copy-start.12
  552.6 2.8 copy-start.1
  552.6 2.8 copy-start.5
  555.2 57.1 %copy-start.16 = (f32[128,128]{1,0:T(8,128)S(1)}, f32[128,128]{1,0:T(8,128)}, u32[]{:S(2)}) copy-start(f32[128,128]{1,0:T(8,128)} %copy-done.15) | copy-start | bytes 196612
  555.3 57.5 %copy-start.10 = (f32[128,2,128]{2,1,0:T(2,128)S(1)}, f32[128,2,128]{2,1,0:T(2,128)}, u32[]{:S(2)}) copy-start(f32[128,2,128]{2,1,0:T(2,128)} %copy-done.9) | copy-start | bytes 393220
  636.4 2.5 copy-start.22
Sparse Core Ops, SparseCore 0:
  11.5 93.5 all-gather.3
  112.2 38.5 all-gather.5
  549.8 61.5 reduce-scatter.2
  634.4 144.8 reduce-scatter.4

commit v3 on v1

--- a/solution.py
+++ b/solution.py
@@ -1,13 +1,17 @@
+import functools
 import math
 
 import jax
 import jax.numpy as jnp
 from jax import lax
+from jax.experimental import pallas as pl
+from jax.experimental.pallas import tpu as pltpu
 from jax.sharding import Mesh, PartitionSpec as P
 
 HEADS = 12
 KV_HEADS = 2
 HEAD_DIM = 128
+MODEL = HEADS * HEAD_DIM
 GROUP = HEADS // KV_HEADS
 QUERY_WIDTH = HEADS * HEAD_DIM
 KEY_WIDTH = KV_HEADS * HEAD_DIM
@@ -79,11 +83,1158 @@
     scaled = upstream * gain
     inner = jnp.mean(scaled * values, axis=-1, keepdims=True)
     part = scale * scaled - values * (scale * scale * scale) * inner
-    gain_grad = jnp.sum(upstream * values * scale, axis=0)
+    gain_grad = jnp.sum(upstream * values * scale, axis=0, keepdims=True)
     return part, gain_grad
 
 
-def body(
+MESH = pl.DeviceIdType.MESH
+VMEM_LIMIT = 60 * 2**20
+
+
+def coordinates():
+    return tuple(lax.axis_index(name) for name in AXES)
+
+
+class Courier:
+    def __init__(self, sends, receives):
+        self.sends, self.receives, self.copies, self.settled = sends, receives, [], 0
+
+    def copy(self, source, target, device):
+        place = len(self.copies)
+        made = pltpu.make_async_remote_copy(
+            src_ref=source,
+            dst_ref=target,
+            send_sem=self.sends.at[place],
+            recv_sem=self.receives.at[place],
+            device_id=device,
+            device_id_type=MESH,
+        )
+        made.start()
+        self.copies.append(made)
+        return made
+
+    def finish(self):
+        for made in self.copies[self.settled :]:
+            made.wait_send()
+        self.settled = len(self.copies)
+
+
+def meet(devices):
+    barrier = pltpu.get_barrier_semaphore()
+    for device in devices:
+        pl.semaphore_signal(barrier, inc=1, device_id=device, device_id_type=MESH)
+    pl.semaphore_wait(barrier, len(devices))
+
+
+def cuts_of(width, step):
+    return [(start, min(step, width - start)) for start in range(0, width, step)]
+
+
+class Gather:
+    def __init__(self, courier, place, source, buffer, order):
+        self.courier, self.place, self.order = courier, place, order
+        self.source, self.buffer = source, buffer
+        self.hops = [{}, {}, {}, {}]
+
+    def line(self, dz):
+        nz = self.place.nz
+        return lax.rem(self.place.z + nz - dz, nz)
+
+    def start(self):
+        p = self.place
+        spot = self.buffer.at[p.z, p.x, p.y, p.c]
+        for dz in range(1, p.nz):
+            device = (lax.rem(p.z + dz, p.nz), p.x, p.y, p.c)
+            self.hops[0][dz] = self.courier.copy(self.source, spot, device)
+
+    def hop(self, number, dz):
+        p, group = self.place, self.line(dz)
+        if dz or number > 1:
+            self.hops[number - 1][dz].wait_recv()
+        if number == 1:
+            spot = self.buffer.at[group, p.x, p.y, p.c]
+            device = p.across[self.order[0]]
+        elif number == 2:
+            if self.order[0] == "y":
+                spot = self.buffer.at[group, p.x, :, p.c]
+            else:
+                spot = self.buffer.at[group, :, p.y, p.c]
+            device = p.across[self.order[1]]
+        else:
+            spot = self.buffer.at[group, :, :, p.c]
+            device = p.across["c"]
+        self.hops[number][dz] = self.courier.copy(spot, spot, device)
+
+    def hop_all(self, number):
+        for dz in range(self.place.nz):
+            self.hop(number, dz)
+
+    def done(self):
+        for made in self.hops[3].values():
+            made.wait_recv()
+
+
+class Place:
+    def __init__(self, nz):
+        self.nz = nz
+        self.z, self.x, self.y, self.c = z, x, y, c = coordinates()
+        self.across = {"x": (z, 1 - x, y, c), "y": (z, x, 1 - y, c), "c": (z, x, y, 1 - c)}
+
+    def line(self, dz, dy=0):
+        y = lax.rem(self.y + dy, 2) if dy else self.y
+        return (lax.rem(self.z + dz, self.nz), self.x, y, self.c)
+
+    def peers(self):
+        team = [self.line(dz, dy) for dz in range(self.nz) for dy in range(2)]
+        return team[1:] + [self.across["x"], self.across["c"]]
+
+
+def spread(values, piece, width):
+    devices, lanes = values.shape
+    at = lax.broadcasted_iota(jnp.int32, (lanes, width), 1)
+    inner = lax.broadcasted_iota(jnp.int32, (lanes, width), 0)
+    chosen = (lax.rem(at, piece) == inner).astype(floats).astype(halves)
+    repeated = jnp.dot(values.astype(halves), chosen, preferred_element_type=floats)
+    owner = lax.div(lax.broadcasted_iota(jnp.int32, (devices, width), 1), piece)
+    mine = owner == lax.broadcasted_iota(jnp.int32, (devices, width), 0)
+    return jnp.sum(jnp.where(mine, repeated, 0.0), axis=0, keepdims=True)
+
+
+def attention_kernel(
+    nz,
+    stack_ref,
+    joint_ref,
+    merge_ref,
+    small_ref,
+    label_ref,
+    inverse_ref,
+    tokens_ref,
+    outer_ref,
+    w_ref,
+    ct_ref,
+    kv_out,
+    query_out,
+    merge_out,
+    xn1_ref,
+    xn2_ref,
+    mixed_ref,
+    gain_ref,
+    turn_ref,
+    query_ref,
+    pair_ref,
+    share_ref,
+    out_ref,
+    joint_kv,
+    joint_q,
+    merge,
+    small,
+    bias_mask,
+    qjoint,
+    pair_own,
+    sends,
+    receives,
+    locals_,
+):
+    place = Place(nz)
+    z, x, y, c = place.z, place.x, place.y, place.c
+    length, model = tokens_ref.shape
+    depth, joint_width = joint_ref.shape
+    share = w_ref.shape[-1]
+    courier = Courier(sends, receives)
+    devices = 8 * nz
+    meet(place.peers())
+
+    own_copies = []
+
+    def keep(source, target):
+        made = pltpu.make_async_copy(source, target, locals_.at[len(own_copies)])
+        made.start()
+        own_copies.append(made)
+        return made
+
+    def columns(tz, ty):
+        return pl.ds(pl.multiple_of((tz * 2 + ty) * share, 128), share)
+
+    half = QUERY_WIDTH // 2
+    blocks = {
+        "small": (small_ref, small, "yx"),
+        "kv": (joint_ref.at[:, QUERY_WIDTH:], joint_kv, "xy"),
+        "q0": (joint_ref.at[:, :half], joint_q.at[0], "yx"),
+        "q1": (joint_ref.at[:, half:QUERY_WIDTH], joint_q.at[1], "xy"),
+        "m0": (merge_ref.at[:, :half], merge.at[0], "yx"),
+        "m1": (merge_ref.at[:, half:], merge.at[1], "xy"),
+    }
+    gathers = {}
+    own_waits = {}
+    for name, (source, buffer, order) in blocks.items():
+        own_waits[name] = keep(source, buffer.at[z, x, y, c])
+        gathers[name] = Gather(courier, place, source, buffer, order)
+    for name in ("small", "kv", "q0", "q1"):
+        gathers[name].start()
+    w_own = keep(stack_ref.at[:, :, columns(z, y)], w_ref.at[:, z, x, y, c])
+    ct_own = keep(outer_ref, ct_ref.at[z, y])
+
+    residual = tokens_ref[...].astype(floats)
+    hat = residual * norm_parts(residual)
+
+    for name in ("small", "kv"):
+        own_waits[name].wait()
+        gathers[name].hop_all(1)
+    direct = {}
+    for dz in list(range(1, nz)) + [0]:
+        for dy in range(2):
+            if dz or dy:
+                ty = lax.rem(y + dy, 2)
+                device = place.line(dz, dy)
+                direct[dz, dy] = courier.copy(
+                    stack_ref.at[:, :, columns(device[0], ty)], w_ref.at[:, z, x, y, c], device
+                )
+    for name in ("small", "kv"):
+        gathers[name].hop_all(2)
+    for name in ("q0", "q1"):
+        own_waits[name].wait()
+        gathers[name].hop_all(1)
+    for name in ("small", "kv"):
+        gathers[name].hop_all(3)
+    for name in ("m0", "m1"):
+        gathers[name].start()
+    ct_along = {
+        dz: courier.copy(outer_ref, ct_ref.at[z, y], place.line(dz)) for dz in range(1, nz)
+    }
+    for name in ("small", "kv"):
+        gathers[name].done()
+
+    pieces = small[...].reshape(devices * 8, 128).astype(halves)
+
+    def row_of(which):
+        at = lax.broadcasted_iota(jnp.int32, (devices, devices * 8), 1)
+        wanted = lax.broadcasted_iota(jnp.int32, (devices, devices * 8), 0) * 8 + which
+        chosen = (at == wanted).astype(floats).astype(halves)
+        return jnp.dot(chosen, pieces, preferred_element_type=floats)
+
+    gain_first = spread(row_of(1), depth, model)
+    gain_second = spread(row_of(2), depth, model)
+    bias = spread(row_of(0), joint_width // devices, joint_width)
+    gain_ref[0:1, :] = gain_first
+    gain_ref[1:2, :] = gain_second
+    label = label_ref[...]
+    start = jnp.zeros((length, 1), floats)
+    block_at = (z * 2 + x) * length
+    rows_at = block_at + lax.broadcasted_iota(jnp.int32, (length, length), 0)
+    lanes_at = lax.broadcasted_iota(jnp.int32, (length, length), 1)
+    for block in range(2 * nz):
+        keys_label = small[block // 2, block % 2, y, c, 3:4, :]
+        start = start + jnp.sum((keys_label < label).astype(floats), axis=1, keepdims=True)
+        allowed = (keys_label == label) & (rows_at >= block * length + lanes_at)
+        bias_mask[:, block * length : (block + 1) * length] = jnp.where(allowed, 0.0, neg)
+    place_at = (block_at + lax.broadcasted_iota(jnp.int32, (length, 1), 0)).astype(floats)
+    angle = (place_at - start) * inverse_ref[...]
+    cosine = jnp.cos(angle)
+    lane = lax.broadcasted_iota(jnp.int32, (length, HEAD_DIM), 1)
+    sine = jnp.where(lane < HEAD_DIM // 2, -1.0, 1.0) * jnp.sin(angle)
+    turn_ref[0] = cosine
+    turn_ref[1] = sine
+
+    def turned(values):
+        return values * cosine + pltpu.roll(values, HEAD_DIM // 2, 1) * sine
+
+    xn1_ref[...] = (hat * gain_first).astype(halves)
+    pair = jnp.dot(
+        xn1_ref[...], joint_kv[...].reshape(model, 2 * KEY_WIDTH), preferred_element_type=floats
+    ) + bias[:, QUERY_WIDTH:]
+    for head in range(KV_HEADS):
+        lanes = slice(head * HEAD_DIM, (head + 1) * HEAD_DIM)
+        pair_own[:, lanes] = turned(pair[:, lanes]).astype(halves)
+    pair_own[:, KEY_WIDTH:] = pair[:, KEY_WIDTH:].astype(halves)
+    pair_ref[z, x] = pair_own[...]
+    pair_along = {
+        dz: courier.copy(pair_own, pair_ref.at[z, x], place.line(dz)) for dz in range(1, nz)
+    }
+    pair_side = {0: courier.copy(pair_own, pair_ref.at[z, x], place.across["x"])}
+    for name in ("q0", "q1"):
+        gathers[name].hop_all(2)
+    for dz in range(1, nz):
+        pair_along[dz].wait_recv()
+        spot = pair_ref.at[lax.rem(z + nz - dz, nz), x]
+        pair_side[dz] = courier.copy(spot, spot, place.across["x"])
+    for name in ("q0", "q1"):
+        gathers[name].hop_all(3)
+    for name in ("m0", "m1"):
+        own_waits[name].wait()
+        gathers[name].hop_all(1)
+    for name in ("q0", "q1"):
+        gathers[name].done()
+
+    for part in range(2):
+        qjoint[:, part * half : (part + 1) * half] = jnp.dot(
+            xn1_ref[...], joint_q[part].reshape(model, half), preferred_element_type=floats
+        ) + bias[:, part * half : (part + 1) * half]
+    for head in range(HEADS):
+        query_ref[head // GROUP, head % GROUP] = turned(
+            qjoint[:, head * HEAD_DIM : (head + 1) * HEAD_DIM]
+        ).astype(halves)
+
+    w_cross, ct_side = {}, {}
+    ct_own.wait()
+    w_own.wait()
+    for dz in range(nz):
+        if dz:
+            ct_along[dz].wait_recv()
+        spot = ct_ref.at[lax.rem(z + nz - dz, nz), y]
+        ct_side[dz] = courier.copy(spot, spot, place.across["y"])
+    for name in ("m0", "m1"):
+        gathers[name].hop_all(2)
+    for made in pair_side.values():
+        made.wait_recv()
+
+    def cross(dz):
+        for dy in range(2):
+            if dz or dy:
+                direct[dz, dy].wait_recv()
+        spot = w_ref.at[:, lax.rem(z + nz - dz, nz), x, :, c]
+        w_cross[dz] = courier.copy(spot, spot, place.across["x"])
+
+    cross(0)
+    cross(1)
+
+    heads = 2
+
+    @pl.loop(0, HEADS // heads)
+    def _(step):
+        kv = lax.div(step, GROUP // heads)
+        pack = lax.rem(step, GROUP // heads)
+        key_lanes = pl.ds(pl.multiple_of(kv * HEAD_DIM, 128), HEAD_DIM)
+        value_lanes = pl.ds(pl.multiple_of(KEY_WIDTH + kv * HEAD_DIM, 128), HEAD_DIM)
+        total_keys = 2 * nz * length
+        query = query_ref[kv, pl.ds(pack * heads, heads)].reshape(heads * length, HEAD_DIM)
+        keys = pair_ref[:, :, :, key_lanes].reshape(total_keys, HEAD_DIM)
+        values = pair_ref[:, :, :, value_lanes].reshape(total_keys, HEAD_DIM)
+        scores = lax.dot_general(query, keys, last_pair, preferred_element_type=floats)
+        scores = scores.reshape(heads, length, total_keys) * SCALE + bias_mask[...][None]
+        top = jnp.max(scores, axis=-1, keepdims=True)
+        raised = jnp.exp(scores - top)
+        shares = raised / jnp.sum(raised, axis=-1, keepdims=True)
+        shares = shares.reshape(heads * length, total_keys).astype(halves)
+        share_ref[kv, pl.ds(pack * heads, heads)] = shares.reshape(heads, length, total_keys)
+        summed = jnp.dot(shares, values, preferred_element_type=floats)
+        for index in range(heads):
+            lanes = pl.ds(pl.multiple_of((step * heads + index) * HEAD_DIM, 128), HEAD_DIM)
+            out_ref[:, lanes] = summed[index * length : (index + 1) * length]
+
+    for name in ("m0", "m1"):
+        gathers[name].hop_all(3)
+    for dz in range(2, nz):
+        cross(dz)
+    for name in ("m0", "m1"):
+        gathers[name].done()
+    saves = [
+        keep(joint_kv, kv_out),
+        keep(joint_q, query_out),
+        keep(merge, merge_out),
+    ]
+    attended = out_ref[...].astype(halves)
+    mixed = tokens_ref[...].astype(floats)
+    for part in range(2):
+        mixed = mixed + lax.dot_general(
+            attended[:, part * half : (part + 1) * half],
+            merge[part].reshape(model, half),
+            last_pair,
+            preferred_element_type=floats,
+        )
+    mixed_ref[...] = mixed
+    xn2_ref[...] = (mixed * norm_parts(mixed) * gain_second).astype(halves)
+
+    hand = []
+    for dz in range(nz):
+        w_cross[dz].wait_recv()
+        spot = w_ref.at[:, lax.rem(z + nz - dz, nz), :, :, c]
+        hand.append(courier.copy(spot, spot, place.across["c"]))
+    for made in hand:
+        made.wait_recv()
+    for made in ct_side.values():
+        made.wait_recv()
+    for made in saves:
+        made.wait()
+    courier.finish()
+
+
+def feed_kernel(
+    nz,
+    w_ref,
+    ct_ref,
+    normal_ref,
+    back_ref,
+    branch_ref,
+    grads_ref,
+    w,
+    xn,
+    ct,
+    hid,
+    gb,
+    ub,
+    part,
+    ybuf,
+    zsend,
+    zbuf,
+    cbuf,
+    sends,
+    receives,
+    locals_,
+):
+    place = Place(nz)
+    z, x, y, c = place.z, place.x, place.y, place.c
+    length, model = normal_ref.shape
+    share = w.shape[-1]
+    block = model // nz
+    lines = 2 * length * nz
+    courier = Courier(sends, receives)
+
+    def source(dz):
+        return lax.rem(z + nz - dz, nz)
+
+    meet([place.line(dz) for dz in range(1, nz)] + [place.across["y"], place.across["c"]])
+    along = {
+        dz: courier.copy(normal_ref, xn.at[z, y], place.line(dz)) for dz in range(1, nz)
+    }
+    side = {0: courier.copy(normal_ref, xn.at[z, y], place.across["y"])}
+    loads = [
+        pltpu.make_async_copy(w_ref.at[which], w.at[which], locals_.at[which])
+        for which in range(3)
+    ] + [pltpu.make_async_copy(ct_ref, ct, locals_.at[3])]
+    for made in loads:
+        made.start()
+    xn[z, y] = normal_ref[...]
+    for made in loads:
+        made.wait()
+
+    def weight(which, start, size):
+        return w[which, :, :, :, :, :, start : start + size].reshape(model, size)
+
+    def pass_on(dz):
+        along[dz].wait_recv()
+        spot = xn.at[source(dz), y]
+        side[dz] = courier.copy(spot, spot, place.across["y"])
+
+    half = nz // 2
+    scatter = []
+    for dz in range(nz):
+        group = source(dz)
+        if dz + 1 < nz:
+            pass_on(dz + 1)
+        side[dz].wait_recv()
+        for start, size in cuts_of(share, 256):
+            normal = xn[group].reshape(2 * length, model)
+            outer = ct[group].reshape(2 * length, model)
+            gate = jnp.dot(normal, weight(0, start, size), preferred_element_type=floats)
+            upper = jnp.dot(normal, weight(1, start, size), preferred_element_type=floats)
+            hidden_back = jnp.dot(outer, weight(2, start, size), preferred_element_type=floats)
+            sig = 1.0 / (1.0 + jnp.exp(-gate))
+            silu = gate * sig
+            spot = (group, slice(None), slice(start, start + size))
+            hid[spot] = (silu * upper).astype(halves)
+            gb[spot] = (hidden_back * upper * (sig * (1.0 + gate * (1.0 - sig)))).astype(halves)
+            ub[spot] = (hidden_back * silu).astype(halves)
+
+        @pl.loop(0, 2)
+        def _(step):
+            rows = pl.ds(step * half, half)
+            lanes = pl.ds(pl.multiple_of(step * (model // 2), 128), model // 2)
+
+            def turned(which):
+                return w[which, rows].reshape(model // 2, share)
+
+            both = lax.dot_general(
+                gb[group], turned(0), last_pair, preferred_element_type=floats
+            ) + lax.dot_general(ub[group], turned(1), last_pair, preferred_element_type=floats)
+            part[group, :, :, lanes] = both.astype(halves).reshape(2, length, model // 2)
+
+        scatter.append(
+            courier.copy(part.at[group, 1 - y], ybuf.at[group], place.across["y"])
+        )
+
+    final = {}
+    for dz in [(dz + nz // 2) % nz for dz in range(nz)]:
+        group = source(dz)
+        scatter[dz].wait_recv()
+        total = part[group, y].astype(floats) + ybuf[group].astype(floats)
+        if dz == 0:
+            back_ref[...] = total
+        else:
+            zsend[dz - 1] = total.astype(halves)
+            final[dz] = courier.copy(zsend.at[dz - 1], zbuf.at[dz - 1], (group, x, y, c))
+
+    for group in range(nz):
+
+        @pl.loop(0, 2)
+        def _(step):
+            rows = pl.ds(step * half, half)
+            lanes = pl.ds(pl.multiple_of(step * (model // 2), 128), model // 2)
+            product = lax.dot_general(
+                hid[group],
+                w[2, rows].reshape(model // 2, share),
+                last_pair,
+                preferred_element_type=floats,
+            )
+            branch_ref[group, :, :, lanes] = product.astype(halves).reshape(2, length, model // 2)
+
+    saves, handed = [], []
+    for group in range(nz):
+        lanes = slice(group * block, (group + 1) * block)
+        normal_turned = xn[:, :, :, lanes].reshape(lines, block).T
+        outer_turned = ct[:, :, :, lanes].reshape(lines, block).T
+        for which, left, right in (
+            (0, normal_turned, gb),
+            (1, normal_turned, ub),
+            (2, outer_turned, hid),
+        ):
+            for start, size in cuts_of(share, 512):
+                w[which, group, :, :, :, :, start : start + size] = (
+                    jnp.dot(
+                        left,
+                        right[:, :, start : start + size].reshape(lines, size),
+                        preferred_element_type=floats,
+                    )
+                    .astype(halves)
+                    .reshape(2, 2, 2, -1, size)
+                )
+        handed.append(
+            courier.copy(w.at[:, group, :, :, 1 - c], cbuf.at[group], place.across["c"])
+        )
+    for group in range(nz):
+        handed[group].wait_recv()
+        for which in range(3):
+            w[which, group, :, :, c] = (
+                w[which, group, :, :, c].astype(floats) + cbuf[group, which].astype(floats)
+            ).astype(halves)
+        made = pltpu.make_async_copy(
+            w.at[:, group, :, :, c], grads_ref.at[:, group], locals_.at[4 + group]
+        )
+        made.start()
+        saves.append(made)
+    for dz in range(1, nz):
+        final[dz].wait_recv()
+        back_ref[...] += zbuf[dz - 1].astype(floats)
+    for made in saves:
+        made.wait()
+    courier.finish()
+
+
+class Scatter:
+    def __init__(self, courier, place, parts, core_in, second_in, first_in, line_in, order):
+        self.courier, self.place, self.order = courier, place, order
+        self.parts, self.line_in = parts, line_in
+        self.arrivals = [core_in, second_in, first_in]
+        self.hops = [{}, {}, {}, {}]
+
+    def spots(self, group):
+        p = self.place
+        if self.order == "xy":
+            second = ((group, p.x, slice(None), p.c), (group, 1 - p.x, slice(None), p.c))
+            first = ((group, p.x, p.y, p.c), (group, p.x, 1 - p.y, p.c))
+        else:
+            second = ((group, slice(None), p.y, p.c), (group, slice(None), 1 - p.y, p.c))
+            first = ((group, p.x, p.y, p.c), (group, 1 - p.x, p.y, p.c))
+        every = slice(None)
+        core = ((group, every, every, p.c), (group, every, every, 1 - p.c))
+        return [core, second, first]
+
+    def hop(self, number, dz):
+        p = self.place
+        group = lax.rem(p.z + dz, p.nz)
+        spots = self.spots(group)
+        if number:
+            self.hops[number - 1][dz].wait_recv()
+            kept = spots[number - 1][0]
+            self.parts[kept] = (
+                self.parts[kept].astype(floats) + self.arrivals[number - 1][dz].astype(floats)
+            ).astype(self.parts.dtype)
+        if number < 3:
+            device = p.across[("c" + self.order)[number]]
+            self.hops[number][dz] = self.courier.copy(
+                self.parts.at[spots[number][1]], self.arrivals[number].at[dz], device
+            )
+        elif dz:
+            self.hops[3][dz] = self.courier.copy(
+                self.parts.at[spots[2][0]], self.line_in.at[dz - 1], p.line(dz)
+            )
+
+    def hop_all(self, number):
+        for dz in [(dz + self.place.nz // 2) % self.place.nz for dz in range(self.place.nz)]:
+            self.hop(number, dz)
+
+    def total(self):
+        p = self.place
+        result = self.parts[p.z, p.x, p.y, p.c].astype(floats)
+        for dz in range(1, p.nz):
+            self.hops[3][dz].wait_recv()
+            result = result + self.line_in[dz - 1].astype(floats)
+        return result
+
+
+def gather_pieces(values, piece, devices):
+    width = values.shape[1]
+    owner = lax.div(lax.broadcasted_iota(jnp.int32, (devices, width), 1), piece)
+    mine = owner == lax.broadcasted_iota(jnp.int32, (devices, width), 0)
+    at = lax.broadcasted_iota(jnp.int32, (width, 128), 0)
+    inner = lax.broadcasted_iota(jnp.int32, (width, 128), 1)
+    chosen = (lax.rem(at, piece) == inner).astype(floats)
+    rows = jnp.where(mine, values, 0.0)
+    return jnp.dot(rows, chosen, preferred_element_type=floats, precision=lax.Precision.HIGHEST)
+
+
+def back_kernel(
+    nz,
+    grads_in,
+    branch_ref,
+    kv_ref,
+    q_ref,
+    m_ref,
+    back_ref,
+    mixed_ref,
+    outer_ref,
+    tokens_ref,
+    xn1_ref,
+    gain_ref,
+    turn_ref,
+    query_ref,
+    pair_ref,
+    share_ref,
+    out_ref,
+    output_ref,
+    tokens_grad_ref,
+    joint_grad_ref,
+    merge_grad_ref,
+    small_grad_ref,
+    grads_ref,
+    weight,
+    weight_kv,
+    gown,
+    gin,
+    branch_own,
+    branch_in,
+    branch_line,
+    merge_part,
+    merge_c,
+    merge_s,
+    merge_f,
+    merge_z,
+    query_part,
+    query_c,
+    query_s,
+    query_f,
+    query_z,
+    kv_part,
+    kv_c,
+    kv_s,
+    kv_f,
+    kv_z,
+    small_part,
+    small_c,
+    small_s,
+    small_f,
+    small_z,
+    pair_sum,
+    pair_half,
+    pair_side,
+    pair_line,
+    joint_back,
+    attended_back,
+    query_back,
+    mixed_grad,
+    sends,
+    receives,
+    locals_,
+):
+    place = Place(nz)
+    z, x, y, c = place.z, place.x, place.y, place.c
+    length, model = tokens_ref.shape
+    share = gown.shape[-1]
+    half = QUERY_WIDTH // 2
+    block = model // nz
+    depth = grads_in.shape[-2]
+    devices = 8 * nz
+    total_keys = 2 * nz * length
+    orders = [(dz + nz // 2) % nz for dz in range(nz)]
+    courier = Courier(sends, receives)
+    meet(place.peers())
+
+    def group_of(dz):
+        return lax.rem(z + dz, nz)
+
+    copies = []
+
+    def load(source, target):
+        made = pltpu.make_async_copy(source, target, locals_.at[len(copies)])
+        made.start()
+        copies.append(made)
+        return made
+
+    merge_load = load(m_ref, weight)
+    kv_load = load(kv_ref, weight_kv)
+    branch_load = load(branch_ref.at[:, y], branch_own)
+    gown_load = load(grads_in.at[:, :, x], gown)
+
+    g_cross = {
+        dz: courier.copy(grads_in.at[:, group_of(dz), 1 - x], gin.at[dz], place.across["x"])
+        for dz in orders
+    }
+    b_cross = {
+        dz: courier.copy(branch_ref.at[group_of(dz), 1 - y], branch_in.at[dz], place.across["y"])
+        for dz in orders
+    }
+
+    mixed = mixed_ref[...]
+    second_scale = norm_parts(mixed)
+    part, second_local = norm_back(back_ref[...], mixed, second_scale, gain_ref[1:2, :])
+    grad = outer_ref[...].astype(floats) + part
+    mixed_grad[...] = grad
+    mixed_half = grad.astype(halves)
+
+    def scatter(arrays, order):
+        return Scatter(courier, place, *arrays, order)
+
+    merges = [
+        scatter([ref.at[i] for ref in (merge_part, merge_c, merge_s, merge_f, merge_z)], order)
+        for i, order in ((0, "xy"), (1, "yx"))
+    ]
+    attended = out_ref[...].astype(halves)
+    mixed_turned = mixed_half.T
+    for group in range(nz):
+        for i in range(2):
+            merge_part[i, group] = (
+                jnp.dot(
+                    mixed_turned[group * block : (group + 1) * block],
+                    attended[:, i * half : (i + 1) * half],
+                    preferred_element_type=floats,
+                )
+                .astype(halves)
+                .reshape(2, 2, 2, depth, half)
+            )
+    for made in merges:
+        made.hop_all(0)
+    merge_load.wait()
+    for i in range(2):
+        attended_back[:, i * half : (i + 1) * half] = jnp.dot(
+            mixed_half, weight[i].reshape(model, half), preferred_element_type=floats
+        ).astype(halves)
+    query_load = load(q_ref, weight)
+
+    branch_load.wait()
+    gown_load.wait()
+    b_line, g_line = {}, []
+    for dz in orders:
+        group = group_of(dz)
+        b_cross[dz].wait_recv()
+        branch_own[group] = (
+            branch_own[group].astype(floats) + branch_in[dz].astype(floats)
+        ).astype(halves)
+        if dz:
+            b_line[dz] = courier.copy(
+                branch_own.at[group], branch_line.at[dz - 1], place.line(dz)
+            )
+    mine = pl.ds(pl.multiple_of((z * 2 + y) * share, 128), share)
+    kept = []
+
+    def grads_on(dz):
+        group = group_of(dz)
+        g_cross[dz].wait_recv()
+        for which in range(3):
+            gown[which, group] = (
+                gown[which, group].astype(floats) + gin[dz, which].astype(floats)
+            ).astype(halves)
+        for dy in range(2):
+            ty = lax.rem(y + dy, 2)
+            if dz or dy:
+                g_line.append(
+                    courier.copy(
+                        gown.at[:, group, ty], grads_ref.at[:, :, mine], (group, x, ty, c)
+                    )
+                )
+            else:
+                kept.append(load(gown.at[:, group, ty], grads_ref.at[:, :, mine]))
+
+    grads_on(orders[0])
+    for made in merges:
+        made.hop_all(1)
+
+    heads = 2
+    pair_sum[...] = jnp.zeros_like(pair_sum)
+
+    @pl.loop(0, HEADS // heads)
+    def _(step):
+        kv = lax.div(step, GROUP // heads)
+        pack = lax.rem(step, GROUP // heads)
+        key_lanes = pl.ds(pl.multiple_of(kv * HEAD_DIM, 128), HEAD_DIM)
+        value_lanes = pl.ds(pl.multiple_of(KEY_WIDTH + kv * HEAD_DIM, 128), HEAD_DIM)
+        rows = heads * length
+        query = query_ref[kv, pl.ds(pack * heads, heads)].reshape(rows, HEAD_DIM)
+        keys = pair_ref[:, :, :, key_lanes].reshape(total_keys, HEAD_DIM)
+        values = pair_ref[:, :, :, value_lanes].reshape(total_keys, HEAD_DIM)
+        lanes = [
+            pl.ds(pl.multiple_of((step * heads + index) * HEAD_DIM, 128), HEAD_DIM)
+            for index in range(heads)
+        ]
+        upstream = jnp.concatenate([attended_back[:, at] for at in lanes], axis=0)
+        summed = jnp.concatenate([out_ref[:, at] for at in lanes], axis=0)
+        delta = jnp.sum(upstream.astype(floats) * summed, axis=-1, keepdims=True)
+        mass = lax.dot_general(upstream, values, last_pair, preferred_element_type=floats)
+        shares = share_ref[kv, pl.ds(pack * heads, heads)].reshape(rows, total_keys)
+        scores = (shares.astype(floats) * (mass - delta)).astype(halves)
+        query_sum = jnp.dot(scores, keys, preferred_element_type=floats) * SCALE
+        for index in range(heads):
+            query_back[:, lanes[index]] = query_sum[index * length : (index + 1) * length]
+        pair_sum[:, key_lanes] += jnp.dot(scores.T, query, preferred_element_type=floats) * SCALE
+        pair_sum[:, value_lanes] += jnp.dot(shares.T, upstream, preferred_element_type=floats)
+
+    pair_half[...] = pair_sum[...].astype(halves).reshape(nz, 2, length, 2 * KEY_WIDTH)
+    p_cross = {
+        dz: courier.copy(pair_half.at[group_of(dz), 1 - x], pair_side.at[dz], place.across["x"])
+        for dz in orders
+    }
+    grads_on(orders[1])
+    cosine, sine = turn_ref[0], turn_ref[1]
+
+    def unturned(values):
+        return values * cosine + pltpu.roll(values * sine, HEAD_DIM // 2, 1)
+
+    for head in range(HEADS):
+        lanes = slice(head * HEAD_DIM, (head + 1) * HEAD_DIM)
+        joint_back[:, lanes] = unturned(query_back[:, lanes]).astype(halves)
+    p_line = {}
+    for dz in orders:
+        group = group_of(dz)
+        p_cross[dz].wait_recv()
+        pair_half[group, x] = (
+            pair_half[group, x].astype(floats) + pair_side[dz].astype(floats)
+        ).astype(halves)
+        if dz:
+            p_line[dz] = courier.copy(
+                pair_half.at[group, x], pair_line.at[dz - 1], place.line(dz)
+            )
+    queries = [
+        scatter([ref.at[i] for ref in (query_part, query_c, query_s, query_f, query_z)], order)
+        for i, order in ((0, "xy"), (1, "yx"))
+    ]
+    keys_values = scatter([kv_part, kv_c, kv_s, kv_f, kv_z], "yx")
+    smalls = scatter([small_part, small_c, small_s, small_f, small_z], "xy")
+    turned = xn1_ref[...].T
+    for group in range(nz):
+        for i in range(2):
+            query_part[i, group] = (
+                jnp.dot(
+                    turned[group * block : (group + 1) * block],
+                    joint_back[:, i * half : (i + 1) * half],
+                    preferred_element_type=floats,
+                )
+                .astype(halves)
+                .reshape(2, 2, 2, depth, half)
+            )
+    for made in queries:
+        made.hop_all(0)
+    for made in merges:
+        made.hop_all(2)
+    total = pair_half[z, x].astype(floats)
+    for dz in range(1, nz):
+        p_line[dz].wait_recv()
+        total = total + pair_line[dz - 1].astype(floats)
+    for head in range(KV_HEADS):
+        lanes = slice(head * HEAD_DIM, (head + 1) * HEAD_DIM)
+        joint_back[:, QUERY_WIDTH + head * HEAD_DIM : QUERY_WIDTH + (head + 1) * HEAD_DIM] = (
+            unturned(total[:, lanes]).astype(halves)
+        )
+    joint_back[:, QUERY_WIDTH + KEY_WIDTH :] = total[:, KEY_WIDTH:].astype(halves)
+    for group in range(nz):
+        kv_part[group] = (
+            jnp.dot(
+                turned[group * block : (group + 1) * block],
+                joint_back[:, QUERY_WIDTH:],
+                preferred_element_type=floats,
+            )
+            .astype(halves)
+            .reshape(2, 2, 2, depth, 2 * KEY_WIDTH)
+        )
+    keys_values.hop_all(0)
+    for made in queries:
+        made.hop_all(1)
+    grads_on(orders[2])
+
+    query_load.wait()
+    kv_load.wait()
+    normal_back = lax.dot_general(
+        joint_back[:, QUERY_WIDTH:],
+        weight_kv[...].reshape(model, 2 * KEY_WIDTH),
+        last_pair,
+        preferred_element_type=floats,
+    )
+    for i in range(2):
+        normal_back = normal_back + lax.dot_general(
+            joint_back[:, i * half : (i + 1) * half],
+            weight[i].reshape(model, half),
+            last_pair,
+            preferred_element_type=floats,
+        )
+    residual = tokens_ref[...].astype(floats)
+    part, first_local = norm_back(normal_back, residual, norm_parts(residual), gain_ref[0:1, :])
+    tokens_grad_ref[...] = mixed_grad[...] + part
+    bias_local = jnp.sum(joint_back[...].astype(floats), axis=0, keepdims=True)
+
+    pieces = jnp.zeros((devices * 8, 128), floats)
+    for which, values in ((0, bias_local), (1, first_local), (2, second_local)):
+        mine_rows = gather_pieces(values, values.shape[1] // devices, devices)
+        at = lax.broadcasted_iota(jnp.int32, (devices * 8, devices), 0)
+        wanted = lax.broadcasted_iota(jnp.int32, (devices * 8, devices), 1) * 8 + which
+        pieces = pieces + jnp.dot(
+            (at == wanted).astype(floats),
+            mine_rows,
+            preferred_element_type=floats,
+            precision=lax.Precision.HIGHEST,
+        )
+    small_part[...] = pieces.reshape(nz, 2, 2, 2, 8, 128)
+    smalls.hop_all(0)
+    keys_values.hop_all(1)
+    smalls.hop_all(1)
+    for made in queries:
+        made.hop_all(2)
+    keys_values.hop_all(2)
+    smalls.hop_all(2)
+    for dz in orders[3:]:
+        grads_on(dz)
+    for made in merges + queries + [keys_values, smalls]:
+        made.hop_all(3)
+    total = mixed_ref[...] + branch_own[z].astype(floats)
+    for dz in range(1, nz):
+        b_line[dz].wait_recv()
+        total = total + branch_line[dz - 1].astype(floats)
+    output_ref[...] = total.astype(halves)
+    for i in range(2):
+        merge_grad_ref[:, i * half : (i + 1) * half] = merges[i].total()
+        joint_grad_ref[:, i * half : (i + 1) * half] = queries[i].total()
+    joint_grad_ref[:, QUERY_WIDTH:] = keys_values.total()
+    small_grad_ref[...] = smalls.total()
+    for made in g_line:
+        made.wait_recv()
+    for made in kept:
+        made.wait()
+    courier.finish()
+
+
+def padded_share(hidden_width, team):
+    return -(-hidden_width // (team * 128)) * 128
+
+
+def body_kernels(
+    tokens,
+    segments,
+    joint_matrix,
+    joint_bias,
+    merge_matrix,
+    norm_first,
+    norm_second,
+    gate_matrix,
+    up_matrix,
+    down_matrix,
+    cotangent,
+):
+    length, model = tokens.shape[1:]
+    depth, joint_width = joint_matrix.shape
+    hidden_width = gate_matrix.shape[1]
+    nz = lax.axis_size("z")
+    share = padded_share(hidden_width, 2 * nz)
+    half = QUERY_WIDTH // 2
+    pair_width = 2 * KEY_WIDTH
+    keys = 2 * nz * length
+    vmem = pl.BlockSpec(memory_space=pltpu.VMEM)
+    anywhere = pl.BlockSpec(memory_space=pl.ANY)
+    blocks = (nz, 2, 2, 2)
+
+    def shape(dims, kind=halves):
+        return jax.ShapeDtypeStruct(dims, kind)
+
+    def semaphores(count, loads):
+        return [
+            pltpu.SemaphoreType.DMA((count,)),
+            pltpu.SemaphoreType.DMA((count,)),
+            pltpu.SemaphoreType.DMA((loads,)),
+        ]
+
+    def params(number):
+        return pltpu.CompilerParams(
+            collective_id=number, has_side_effects=True, vmem_limit_bytes=VMEM_LIMIT
+        )
+
+    stack = jnp.stack([gate_matrix, up_matrix, down_matrix.T])
+    stack = jnp.pad(stack, ((0, 0), (0, 0), (0, 2 * nz * share - hidden_width)))
+
+    def lane_row(values):
+        return jnp.pad(values.astype(floats), (0, 128 - values.shape[0]))
+
+    own_labels = segments[0]
+    empty = jnp.zeros((128,), floats)
+    small = jnp.stack(
+        [lane_row(v) for v in (joint_bias, norm_first, norm_second, own_labels)] + [empty] * 4
+    )
+    inverse = jnp.power(floats(theta), -(jnp.arange(HEAD_DIM // 2, dtype=floats) * (2.0 / HEAD_DIM)))
+    inverse = jnp.concatenate([inverse, inverse])[None]
+    labels = own_labels.astype(floats)[:, None]
+    outer = cotangent[0]
+    (
+        w,
+        team_outer,
+        kv_all,
+        q_all,
+        m_all,
+        xn1,
+        xn2,
+        mixed,
+        gains,
+        turns,
+        queries,
+        pair,
+        shares,
+        summed,
+    ) = pl.pallas_call(
+        functools.partial(attention_kernel, nz),
+        name="attention_forward",
+        out_shape=(
+            shape((3,) + blocks + (depth, share)),
+            shape((nz, 2, length, model)),
+            shape(blocks + (depth, pair_width)),
+            shape((2,) + blocks + (depth, half)),
+            shape((2,) + blocks + (depth, half)),
+            shape((length, model)),
+            shape((length, model)),
+            shape((length, model), floats),
+            shape((8, model), floats),
+            shape((2, length, HEAD_DIM), floats),
+            shape((KV_HEADS, GROUP, length, HEAD_DIM)),
+            shape((nz, 2, length, pair_width)),
+            shape((KV_HEADS, GROUP, length, keys)),
+            shape((length, QUERY_WIDTH), floats),
+        ),
+        in_specs=[anywhere] * 3 + [vmem] * 5,
+        out_specs=(anywhere,) * 5 + (vmem,) * 9,
+        scratch_shapes=[
+            pltpu.VMEM(blocks + (depth, pair_width), halves),
+            pltpu.VMEM((2,) + blocks + (depth, half), halves),
+            pltpu.VMEM((2,) + blocks + (depth, half), halves),
+            pltpu.VMEM(blocks + (8, 128), floats),
+            pltpu.VMEM((length, keys), floats),
+            pltpu.VMEM((length, QUERY_WIDTH), floats),
+            pltpu.VMEM((length, pair_width), halves),
+        ]
+        + semaphores(119, 11),
+        compiler_params=params(0),
+    )(stack, joint_matrix, merge_matrix.T, small, labels, inverse, tokens[0], outer)
+
+    lines = 2 * length
+    back, branch, grads = pl.pallas_call(
+        functools.partial(feed_kernel, nz),
+        name="feed_forward",
+        out_shape=(
+            shape((length, model), floats),
+            shape((nz, 2, length, model)),
+            shape((3, nz, 2, 2, depth, share)),
+        ),
+        in_specs=[anywhere, anywhere, vmem],
+        out_specs=(vmem, vmem, anywhere),
+        scratch_shapes=[
+            pltpu.VMEM((3,) + blocks + (depth, share), halves),
+            pltpu.VMEM((nz, 2, length, model), halves),
+            pltpu.VMEM((nz, 2, length, model), halves),
+            pltpu.VMEM((nz, lines, share), halves),
+            pltpu.VMEM((nz, lines, share), halves),
+            pltpu.VMEM((nz, lines, share), halves),
+            pltpu.VMEM((nz, 2, length, model), halves),
+            pltpu.VMEM((nz, length, model), halves),
+            pltpu.VMEM((nz - 1, length, model), halves),
+            pltpu.VMEM((nz - 1, length, model), halves),
+            pltpu.VMEM((nz, 3, 2, 2, depth, share), halves),
+        ]
+        + semaphores(18, 8),
+        compiler_params=params(1),
+    )(w, team_outer, xn2)
+
+    def sums(rows, width, kind=halves, lead=()):
+        return [
+            pltpu.VMEM(lead + blocks + (rows, width), kind),
+            pltpu.VMEM(lead + (nz, 2, 2, rows, width), kind),
+            pltpu.VMEM(lead + (nz, 2, rows, width), kind),
+            pltpu.VMEM(lead + (nz, rows, width), kind),
+            pltpu.VMEM(lead + (nz - 1, rows, width), kind),
+        ]
+
+    output, tokens_grad, joint_grad, merge_grad, small_grad, grads = pl.pallas_call(
+        functools.partial(back_kernel, nz),
+        name="attention_backward",
+        out_shape=(
+            shape((length, model)),
+            shape((length, model), floats),
+            shape((depth, joint_width), floats),
+            shape((depth, QUERY_WIDTH), floats),
+            shape((8, 128), floats),
+            shape((3, depth, 2 * nz * share)),
+        ),
+        in_specs=[anywhere] * 5 + [vmem] * 11,
+        out_specs=(vmem,) * 5 + (anywhere,),
+        scratch_shapes=[
+            pltpu.VMEM((2,) + blocks + (depth, half), halves),
+            pltpu.VMEM(blocks + (depth, pair_width), halves),
+            pltpu.VMEM((3, nz, 2, depth, share), halves),
+            pltpu.VMEM((nz, 3, 2, depth, share), halves),
+            pltpu.VMEM((nz, length, model), halves),
+            pltpu.VMEM((nz, length, model), halves),
+            pltpu.VMEM((nz - 1, length, model), halves),
+        ]
+        + sums(depth, half, lead=(2,))
+        + sums(depth, half, lead=(2,))
+        + sums(depth, pair_width)
+        + sums(8, 128, floats)
+        + [
+            pltpu.VMEM((keys, pair_width), floats),
+            pltpu.VMEM((nz, 2, length, pair_width), halves),
+            pltpu.VMEM((nz, length, pair_width), halves),
+            pltpu.VMEM((nz - 1, length, pair_width), halves),
+            pltpu.VMEM((length, joint_width), halves),
+            pltpu.VMEM((length, QUERY_WIDTH), halves),
+            pltpu.VMEM((length, QUERY_WIDTH), floats),
+            pltpu.VMEM((length, model), floats),
+        ]
+        + semaphores(115, 6),
+        compiler_params=params(2),
+    )(
+        grads,
+        branch,
+        kv_all,
+        q_all,
+        m_all,
+        back,
+        mixed,
+        outer,
+        tokens[0],
+        xn1,
+        gains,
+        turns,
+        queries,
+        pair,
+        shares,
+        summed,
+    )
+    grads = grads[:, :, :hidden_width].astype(floats)
+    return (
+        output[None],
+        tokens_grad[None],
+        joint_grad,
+        small_grad[0, : joint_bias.shape[0]],
+        merge_grad.T,
+        small_grad[1, :depth],
+        small_grad[2, :depth],
+        grads[0],
+        grads[1],
+        grads[2].T,
+    )
+
+
+def body_plain(
     tokens,
     segments,
     joint_matrix,
@@ -285,8 +1436,9 @@
         P(None, whole),
         P(ROW, SEQ, None),
     )
+    depth = MODEL // mesh.size
     return jax.shard_map(
-        body,
+        body_kernels if depth % 16 == 0 else body_plain,
         mesh=fine,
         in_specs=placed,
         out_specs=(

time: 1020 us -> 556 us (0.55)
  waiting for transfers between devices: 598 us -> 0 us
  Pallas kernels: 0 us -> 529 us
  blocking collectives: 133 us -> 0 us
  matrix products: 115 us -> 0 us
  local copies, waits for them, and re-layouts: 93.7 us -> 9.36 us
  other arithmetic: 45.3 us -> 7.64 us
  between operations: 15.5 us -> 0.9 us
    pallas_call x0 -> x3, Pallas kernels: none -> 529 us  [the longest x1 231 us: body_kernels(): pl.pallas_call(functools.partial(attention_kernel, nz), name='attention_f...]
    all_gather x6 -> x0, waiting for transfers between devices: 194 us -> none  [the longest x1 64.3 us: body(): team_normal = lax.all_gather(normal_half, TEAM, axis=0, tiled=True)]
    reduce_scatter x4 -> x0, waiting for transfers between devices: 191 us -> none  [the longest x1 76 us: body(): lax.psum_scatter(branch.astype(halves), TEAM, scatter_dimension=0, tiled=...]
    unnamed x14 -> x0, waiting for transfers between devices: 134 us -> none
    all_to_all x1 -> x0, blocking collectives: 114 us -> none  [body(): lax.all_to_all(stacked, TEAM, split_axis=0, concat_axis=0, tiled=True)]
    dot_general x17 -> x0, matrix products: 108 us -> none  [the longest x1 13.9 us: body(): jnp.dot(team_outer, down_turned, preferred_element_type=floats)]
    all_to_all x1 -> x0, waiting for transfers between devices: 79 us -> none  [body(): grads = lax.all_to_all(grads, TEAM, split_axis=0, concat_axis=0, tiled=True)]
    another operation x10 -> x2, local copies, waits for them, and re-layouts: 23 us -> 0.61 us  [body_kernels(): jnp.stack([lane_row(v) for v in (joint_bias, norm_first, norm_second, own...]
  transfers between devices with their start and end apart: 13 -> 0, of which waited for: 11 -> 0; matrix products, arithmetic and copies ran while one was open for 21% -> 0% of each run, Pallas kernels for 0% -> 0%
where the time goes in v3:
time: 556 us; the launch traced here: 547 us
  Pallas kernels  529 us (95%)
  local copies, waits for them, and re-layouts  9.36 us (2%)
  other arithmetic  7.64 us (1%)
    pallas_call x1, Pallas kernels, body_kernels(): pl.pallas_call(functools.partial(attention_kernel, nz), name='attention_f...  231 us
    pallas_call x1, Pallas kernels, body_kernels(): pl.pallas_call(functools.partial(back_kernel, nz), name='attention_backwa...  196 us
    pallas_call x1, Pallas kernels, body_kernels(): pl.pallas_call(functools.partial(feed_kernel, nz), name='feed_forward', o...  103 us

profile of v3, /device:TPU:0, one launch (start us, length us, event | category | flops | bytes accessed | tf_op | source)
XLA Modules:
  0.0 547.3 jit_solution(297372631564820541)
XLA Ops:
  0.6 0.7 bitcast_convert_fusion.2
  1.3 0.6 maximum_bitcast_fusion.inverse_ref
  1.9 0.7 convert_bitcast_fusion
  2.6 0.7 bitcast_convert_fusion
  3.2 0.6 stack.48.small_ref
  3.8 0.7 copy.21.label_ref
  4.6 2.9 fusion.4.stack_ref
  7.5 230.8 %attention_forward.1 = (bf16[3,4,2,2,2,48,1152]{6,5,4,3,2,1,0:T(8,128)(2,1)}, bf16[4,2,128,1536]{3,2,1,0:T(8,128)(2,1)}, bf16[4,2,2,2,48,512]{5,4,3,2,1,0:T(8,12...) custom-call(bf16[3,48,9216]{2,1,0:T(8,128)(2,1)} %fusion.4.stack_ref, ...), custom_call_target="tpu_custom_call" | custom-call | tf_op jit(solution)/shard_map/attention_forward/pallas_call | solution.py:1095
  238.4 102.7 %feed_forward.1 = (f32[128,1536]{1,0:T(8,128)}, bf16[4,2,128,1536]{3,2,1,0:T(8,128)(2,1)}, bf16[3,4,2,2,48,1152]{5,4,3,2,1,0:T(8,128)(2,1)}) custom-call(bf16[3,4,2,2,2,48,1152]{6,5,4,3,2,1,0:T(8,128)(2,1)} %get-tuple-element.33.w_ref, bf16[4,2,128,1536]{3,2,1,0:T(8,128)(2,1)} %get-tuple-element.34.ct_ref, bf16[128,1536]{1,0:T(8,128)(2,1)} %get-tuple-element.35.normal_ref), custom_call_target="tpu_custom_call" | custom-call | tf_op jit(solution)/shard_map/feed_forward/pallas_call | solution.py:1130
  341.1 195.8 %attention_backward.1 = (bf16[128,1536]{1,0:T(8,128)(2,1)}, f32[128,1536]{1,0:T(8,128)}, f32[48,2048]{1,0:T(8,128)}, f32[48,1536]{1,0:T(8,128)}, f32[8,128]{1,0:T(8,128)}, /*index=5*/bf16[3,48,9216]{2,1,0:T(8,128)(2,1)}) custom-call(bf16[3,4,2,2,48,1152]{5,4,3,2,1,0:T(8,128)(2,1)} %get-tuple-element.36.grads_in, ...), custom_call_target="tpu_custom_call" | custom-call | tf_op jit(solution)/shard_map/attention_backward/pallas_call | solution.py:1166
  536.9 1.2 slice_bitcast_fusion.5
  538.1 1.3 slice_bitcast_fusion.3
  539.4 2.1 slice_convert_fusion
  541.5 0.0 copy-start.2
  541.5 0.0 copy-start
  541.5 0.0 copy-start.1
  541.5 2.4 slice_bitcast_fusion
  544.0 0.0 copy-start.3
  544.0 0.0 copy-done.2
  544.0 0.7 copy.26
  544.7 0.0 copy-done
  544.7 0.9 copy.27
  545.6 0.0 copy-done.1
  545.6 0.7 copy.28
  546.4 0.0 copy-done.3
  546.4 0.7 copy.29
  (2 shorter events, 0.0 us)
Async XLA Ops:
  541.5 2.5 copy-start.2
  541.5 3.2 copy-start
  541.5 4.1 copy-start.1
  544.0 2.4 copy-start.3

commit v4 on v3

--- a/solution.py
+++ b/solution.py
@@ -95,13 +95,33 @@
     return tuple(lax.axis_index(name) for name in AXES)
 
 
+class Sent:
+    def __init__(self, raw, when):
+        self.raw, self.when = raw, when
+
+    def under(self, act):
+        if self.when is None:
+            act()
+        else:
+            pl.when(self.when)(act)
+
+    def start(self):
+        self.under(self.raw.start)
+
+    def wait_recv(self):
+        self.under(self.raw.wait_recv)
+
+    def wait_send(self):
+        self.under(self.raw.wait_send)
+
+
 class Courier:
     def __init__(self, sends, receives):
-        self.sends, self.receives, self.copies, self.settled = sends, receives, [], 0
-
-    def copy(self, source, target, device):
+        self.sends, self.receives, self.copies = sends, receives, []
+
+    def make(self, source, target, device, when=None):
         place = len(self.copies)
-        made = pltpu.make_async_remote_copy(
+        raw = pltpu.make_async_remote_copy(
             src_ref=source,
             dst_ref=target,
             send_sem=self.sends.at[place],
@@ -109,14 +129,18 @@
             device_id=device,
             device_id_type=MESH,
         )
-        made.start()
+        made = Sent(raw, when)
         self.copies.append(made)
         return made
 
+    def copy(self, source, target, device, when=None):
+        made = self.make(source, target, device, when)
+        made.start()
+        return made
+
     def finish(self):
-        for made in self.copies[self.settled :]:
+        for made in self.copies:
             made.wait_send()
-        self.settled = len(self.copies)
 
 
 def meet(devices):
@@ -130,47 +154,82 @@
     return [(start, min(step, width - start)) for start in range(0, width, step)]
 
 
+class Line:
+    def __init__(self, courier, place, spot):
+        self.courier, self.place, self.spot = courier, place, spot
+        self.sent = {}
+
+    def items(self):
+        p = self.place
+        found = [(0, 0, p.z, None)]
+        for step in range(1, p.nz):
+            found.append((step, 1, lax.max(p.z - step, 0), p.z >= step))
+            found.append((step, -1, lax.min(p.z + step, p.nz - 1), p.z + step < p.nz))
+        return found
+
+    def send(self, step, way, group, also=None):
+        p = self.place
+        inside = p.z < p.nz - 1 if way == 1 else p.z > 0
+        if also is not None:
+            inside = inside & also
+        spot = self.spot(group)
+        self.sent[step, way] = self.courier.copy(spot, spot, p.line_at(way), inside)
+
+    def start(self):
+        self.send(0, 1, self.place.z)
+        self.send(0, -1, self.place.z)
+
+    def arrive(self, step, way, group, exists):
+        made = self.sent[step - 1, way]
+
+        @pl.when(exists)
+        def _():
+            made.raw.wait_recv()
+
+        if step < self.place.nz - 1:
+            self.send(step, way, group, exists)
+
+
 class Gather:
-    def __init__(self, courier, place, source, buffer, order):
-        self.courier, self.place, self.order = courier, place, order
+    def __init__(self, courier, place, source, buffer):
+        self.courier, self.place = courier, place
         self.source, self.buffer = source, buffer
-        self.hops = [{}, {}, {}, {}]
-
-    def line(self, dz):
-        nz = self.place.nz
-        return lax.rem(self.place.z + nz - dz, nz)
+        self.line = Line(courier, place, lambda group: buffer.at[group, :, place.y, place.c])
+        self.side, self.core = {}, {}
 
     def start(self):
         p = self.place
-        spot = self.buffer.at[p.z, p.x, p.y, p.c]
-        for dz in range(1, p.nz):
-            device = (lax.rem(p.z + dz, p.nz), p.x, p.y, p.c)
-            self.hops[0][dz] = self.courier.copy(self.source, spot, device)
-
-    def hop(self, number, dz):
-        p, group = self.place, self.line(dz)
-        if dz or number > 1:
-            self.hops[number - 1][dz].wait_recv()
-        if number == 1:
-            spot = self.buffer.at[group, p.x, p.y, p.c]
-            device = p.across[self.order[0]]
-        elif number == 2:
-            if self.order[0] == "y":
-                spot = self.buffer.at[group, p.x, :, p.c]
-            else:
-                spot = self.buffer.at[group, :, p.y, p.c]
-            device = p.across[self.order[1]]
-        else:
+        self.cross = self.courier.copy(
+            self.source, self.buffer.at[p.z, p.x, p.y, p.c], p.across["x"]
+        )
+
+    def along(self):
+        self.cross.wait_recv()
+        self.line.start()
+        self.sideways(self.line.items()[0])
+
+    def sideways(self, item):
+        step, way, group, exists = item
+        p = self.place
+        spot = self.buffer.at[group, :, p.y, p.c]
+        self.side[step, way] = self.courier.copy(spot, spot, p.across["y"], exists)
+
+    def pass_on(self, step):
+        for item in self.line.items():
+            if item[0] == step:
+                self.line.arrive(*item)
+                self.sideways(item)
+
+    def to_core(self):
+        p = self.place
+        for item in self.line.items():
+            step, way, group, exists = item
+            self.side[step, way].wait_recv()
             spot = self.buffer.at[group, :, :, p.c]
-            device = p.across["c"]
-        self.hops[number][dz] = self.courier.copy(spot, spot, device)
-
-    def hop_all(self, number):
-        for dz in range(self.place.nz):
-            self.hop(number, dz)
+            self.core[step, way] = self.courier.copy(spot, spot, p.across["c"], exists)
 
     def done(self):
-        for made in self.hops[3].values():
+        for made in self.core.values():
             made.wait_recv()
 
 
@@ -183,6 +242,9 @@
     def line(self, dz, dy=0):
         y = lax.rem(self.y + dy, 2) if dy else self.y
         return (lax.rem(self.z + dz, self.nz), self.x, y, self.c)
+
+    def line_at(self, way):
+        return (lax.rem(self.z + self.nz + way, self.nz), self.x, self.y, self.c)
 
     def peers(self):
         team = [self.line(dz, dy) for dz in range(self.nz) for dy in range(2)]
@@ -206,7 +268,6 @@
     joint_ref,
     merge_ref,
     small_ref,
-    label_ref,
     inverse_ref,
     tokens_ref,
     outer_ref,
@@ -229,8 +290,9 @@
     merge,
     small,
     bias_mask,
-    qjoint,
-    pair_own,
+    tokens_all,
+    mixed_send,
+    mixed_in,
     sends,
     receives,
     locals_,
@@ -238,10 +300,14 @@
     place = Place(nz)
     z, x, y, c = place.z, place.x, place.y, place.c
     length, model = tokens_ref.shape
-    depth, joint_width = joint_ref.shape
+    depth = joint_ref.shape[1]
     share = w_ref.shape[-1]
+    half = GROUP * HEAD_DIM
+    both = 2 * length
+    total_keys = nz * both
     courier = Courier(sends, receives)
     devices = 8 * nz
+    joint_width = 2 * joint_ref.shape[2]
     meet(place.peers())
 
     own_copies = []
@@ -255,54 +321,71 @@
     def columns(tz, ty):
         return pl.ds(pl.multiple_of((tz * 2 + ty) * share, 128), share)
 
-    half = QUERY_WIDTH // 2
-    blocks = {
-        "small": (small_ref, small, "yx"),
-        "kv": (joint_ref.at[:, QUERY_WIDTH:], joint_kv, "xy"),
-        "q0": (joint_ref.at[:, :half], joint_q.at[0], "yx"),
-        "q1": (joint_ref.at[:, half:QUERY_WIDTH], joint_q.at[1], "xy"),
-        "m0": (merge_ref.at[:, :half], merge.at[0], "yx"),
-        "m1": (merge_ref.at[:, half:], merge.at[1], "xy"),
-    }
-    gathers = {}
-    own_waits = {}
-    for name, (source, buffer, order) in blocks.items():
-        own_waits[name] = keep(source, buffer.at[z, x, y, c])
-        gathers[name] = Gather(courier, place, source, buffer, order)
-    for name in ("small", "kv", "q0", "q1"):
+    gathers, own_waits = {}, {}
+
+    def begin(name, own, other, buffer):
+        own_waits[name] = keep(own, buffer.at[z, x, y, c])
+        gathers[name] = Gather(courier, place, other, buffer)
         gathers[name].start()
+
+    begin("small", small_ref, small_ref, small)
+    begin("kv", joint_ref.at[x, :, half:], joint_ref.at[1 - x, :, half:], joint_kv)
+    token_cross = courier.copy(tokens_ref, tokens_all.at[x], place.across["x"])
+    begin("q", joint_ref.at[x, :, :half], joint_ref.at[1 - x, :, :half], joint_q)
+    begin("m", merge_ref.at[x], merge_ref.at[1 - x], merge)
+    tokens_all[x] = tokens_ref[...]
     w_own = keep(stack_ref.at[:, :, columns(z, y)], w_ref.at[:, z, x, y, c])
     ct_own = keep(outer_ref, ct_ref.at[z, y])
 
-    residual = tokens_ref[...].astype(floats)
-    hat = residual * norm_parts(residual)
-
+    direct, w_cross, w_hand = {}, {}, {}
+
+    def give(dz, dy):
+        device = place.line(dz, dy)
+        direct[dz, dy] = courier.copy(
+            stack_ref.at[:, :, columns(device[0], device[2])], w_ref.at[:, z, x, y, c], device
+        )
+
+    def w_spot(dz, dy, side):
+        return w_ref.at[:, lax.rem(z + nz - dz, nz), side, lax.rem(y + dy, 2), c]
+
+    def take(dz, dy):
+        if dz or dy:
+            direct[dz, dy].wait_recv()
+        spot = w_spot(dz, dy, x)
+        w_cross[dz, dy] = courier.copy(spot, spot, place.across["x"])
+        w_hand[dz, dy, 0] = courier.copy(spot, spot, place.across["c"])
+
+    def hand(dz, dy):
+        w_cross[dz, dy].wait_recv()
+        spot = w_spot(dz, dy, 1 - x)
+        w_hand[dz, dy, 1] = courier.copy(spot, spot, place.across["c"])
+
+    give(0, 1)
+    give(2, 0)
     for name in ("small", "kv"):
         own_waits[name].wait()
-        gathers[name].hop_all(1)
-    direct = {}
-    for dz in list(range(1, nz)) + [0]:
-        for dy in range(2):
-            if dz or dy:
-                ty = lax.rem(y + dy, 2)
-                device = place.line(dz, dy)
-                direct[dz, dy] = courier.copy(
-                    stack_ref.at[:, :, columns(device[0], ty)], w_ref.at[:, z, x, y, c], device
-                )
+        gathers[name].along()
+    token_cross.wait_recv()
+    tokens_both = tokens_all[...].reshape(both, model).astype(floats)
+    hat = tokens_both * norm_parts(tokens_both)
     for name in ("small", "kv"):
-        gathers[name].hop_all(2)
-    for name in ("q0", "q1"):
-        own_waits[name].wait()
-        gathers[name].hop_all(1)
+        gathers[name].pass_on(1)
+    own_waits["q"].wait()
+    gathers["q"].along()
+    for step in range(2, nz):
+        for name in ("small", "kv"):
+            gathers[name].pass_on(step)
     for name in ("small", "kv"):
-        gathers[name].hop_all(3)
-    for name in ("m0", "m1"):
-        gathers[name].start()
-    ct_along = {
-        dz: courier.copy(outer_ref, ct_ref.at[z, y], place.line(dz)) for dz in range(1, nz)
-    }
+        gathers[name].to_core()
+    w_own.wait()
+    take(0, 0)
+    for step in range(1, nz):
+        gathers["q"].pass_on(step)
     for name in ("small", "kv"):
         gathers[name].done()
+    take(0, 1)
+    give(2, 1)
+    own_waits["m"].wait()
 
     pieces = small[...].reshape(devices * 8, 128).astype(halves)
 
@@ -317,20 +400,26 @@
     bias = spread(row_of(0), joint_width // devices, joint_width)
     gain_ref[0:1, :] = gain_first
     gain_ref[1:2, :] = gain_second
-    label = label_ref[...]
-    start = jnp.zeros((length, 1), floats)
-    block_at = (z * 2 + x) * length
-    rows_at = block_at + lax.broadcasted_iota(jnp.int32, (length, length), 0)
-    lanes_at = lax.broadcasted_iota(jnp.int32, (length, length), 1)
+
+    def mine(first, width):
+        return jnp.where(x == 0, bias[:, first : first + width], bias[:, first + width : first + 2 * width])
+
+    bias_query = mine(0, half)
+    bias_key = mine(QUERY_WIDTH, HEAD_DIM)
+    bias_value = mine(QUERY_WIDTH + KEY_WIDTH, HEAD_DIM)
+    label = jnp.concatenate([small[z, side, y, c].T[:, 3:4] for side in range(2)], axis=0)
+    start = jnp.zeros((both, 1), floats)
+    rows_at = z * both + lax.broadcasted_iota(jnp.int32, (both, length), 0)
+    lanes_at = lax.broadcasted_iota(jnp.int32, (both, length), 1)
     for block in range(2 * nz):
         keys_label = small[block // 2, block % 2, y, c, 3:4, :]
         start = start + jnp.sum((keys_label < label).astype(floats), axis=1, keepdims=True)
         allowed = (keys_label == label) & (rows_at >= block * length + lanes_at)
         bias_mask[:, block * length : (block + 1) * length] = jnp.where(allowed, 0.0, neg)
-    place_at = (block_at + lax.broadcasted_iota(jnp.int32, (length, 1), 0)).astype(floats)
+    place_at = (z * both + lax.broadcasted_iota(jnp.int32, (both, 1), 0)).astype(floats)
     angle = (place_at - start) * inverse_ref[...]
     cosine = jnp.cos(angle)
-    lane = lax.broadcasted_iota(jnp.int32, (length, HEAD_DIM), 1)
+    lane = lax.broadcasted_iota(jnp.int32, (both, HEAD_DIM), 1)
     sine = jnp.where(lane < HEAD_DIM // 2, -1.0, 1.0) * jnp.sin(angle)
     turn_ref[0] = cosine
     turn_ref[1] = sine
@@ -340,116 +429,99 @@
 
     xn1_ref[...] = (hat * gain_first).astype(halves)
     pair = jnp.dot(
-        xn1_ref[...], joint_kv[...].reshape(model, 2 * KEY_WIDTH), preferred_element_type=floats
-    ) + bias[:, QUERY_WIDTH:]
-    for head in range(KV_HEADS):
-        lanes = slice(head * HEAD_DIM, (head + 1) * HEAD_DIM)
-        pair_own[:, lanes] = turned(pair[:, lanes]).astype(halves)
-    pair_own[:, KEY_WIDTH:] = pair[:, KEY_WIDTH:].astype(halves)
-    pair_ref[z, x] = pair_own[...]
-    pair_along = {
-        dz: courier.copy(pair_own, pair_ref.at[z, x], place.line(dz)) for dz in range(1, nz)
-    }
-    pair_side = {0: courier.copy(pair_own, pair_ref.at[z, x], place.across["x"])}
-    for name in ("q0", "q1"):
-        gathers[name].hop_all(2)
-    for dz in range(1, nz):
-        pair_along[dz].wait_recv()
-        spot = pair_ref.at[lax.rem(z + nz - dz, nz), x]
-        pair_side[dz] = courier.copy(spot, spot, place.across["x"])
-    for name in ("q0", "q1"):
-        gathers[name].hop_all(3)
-    for name in ("m0", "m1"):
-        own_waits[name].wait()
-        gathers[name].hop_all(1)
-    for name in ("q0", "q1"):
-        gathers[name].done()
-
-    for part in range(2):
-        qjoint[:, part * half : (part + 1) * half] = jnp.dot(
-            xn1_ref[...], joint_q[part].reshape(model, half), preferred_element_type=floats
-        ) + bias[:, part * half : (part + 1) * half]
-    for head in range(HEADS):
-        query_ref[head // GROUP, head % GROUP] = turned(
-            qjoint[:, head * HEAD_DIM : (head + 1) * HEAD_DIM]
-        ).astype(halves)
-
-    w_cross, ct_side = {}, {}
+        xn1_ref[...], joint_kv[...].reshape(model, 2 * HEAD_DIM), preferred_element_type=floats
+    )
+    pair_ref[z, :, :HEAD_DIM] = turned(pair[:, :HEAD_DIM] + bias_key).astype(halves)
+    pair_ref[z, :, HEAD_DIM:] = (pair[:, HEAD_DIM:] + bias_value).astype(halves)
+    pairs = Line(courier, place, lambda group: pair_ref.at[group])
+    pairs.start()
+    gathers["q"].to_core()
+    gathers["m"].along()
+    for item in pairs.items()[1:3]:
+        pairs.arrive(*item)
+    take(2, 0)
+    give(1, 0)
+    for item in pairs.items()[3:]:
+        pairs.arrive(*item)
+    gathers["m"].pass_on(1)
+    gathers["q"].done()
+
+    query = jnp.dot(xn1_ref[...], joint_q[...].reshape(model, half), preferred_element_type=floats)
+    query = query + bias_query
+    for head in range(GROUP):
+        query_ref[head] = turned(query[:, head * HEAD_DIM : (head + 1) * HEAD_DIM]).astype(halves)
+    for step in range(2, nz):
+        gathers["m"].pass_on(step)
+    take(2, 1)
+    give(1, 1)
+    give(3, 0)
+    outers = Line(courier, place, lambda group: ct_ref.at[group, y])
+    ct_side = {}
+
+    def ct_on(item):
+        step, way, group, exists = item
+        if step:
+            outers.arrive(*item)
+        spot = ct_ref.at[group, y]
+        ct_side[step, way] = courier.copy(spot, spot, place.across["y"], exists)
+
     ct_own.wait()
-    w_own.wait()
-    for dz in range(nz):
-        if dz:
-            ct_along[dz].wait_recv()
-        spot = ct_ref.at[lax.rem(z + nz - dz, nz), y]
-        ct_side[dz] = courier.copy(spot, spot, place.across["y"])
-    for name in ("m0", "m1"):
-        gathers[name].hop_all(2)
-    for made in pair_side.values():
-        made.wait_recv()
-
-    def cross(dz):
-        for dy in range(2):
-            if dz or dy:
-                direct[dz, dy].wait_recv()
-        spot = w_ref.at[:, lax.rem(z + nz - dz, nz), x, :, c]
-        w_cross[dz] = courier.copy(spot, spot, place.across["x"])
-
-    cross(0)
-    cross(1)
-
-    heads = 2
-
-    @pl.loop(0, HEADS // heads)
-    def _(step):
-        kv = lax.div(step, GROUP // heads)
-        pack = lax.rem(step, GROUP // heads)
-        key_lanes = pl.ds(pl.multiple_of(kv * HEAD_DIM, 128), HEAD_DIM)
-        value_lanes = pl.ds(pl.multiple_of(KEY_WIDTH + kv * HEAD_DIM, 128), HEAD_DIM)
-        total_keys = 2 * nz * length
-        query = query_ref[kv, pl.ds(pack * heads, heads)].reshape(heads * length, HEAD_DIM)
-        keys = pair_ref[:, :, :, key_lanes].reshape(total_keys, HEAD_DIM)
-        values = pair_ref[:, :, :, value_lanes].reshape(total_keys, HEAD_DIM)
-        scores = lax.dot_general(query, keys, last_pair, preferred_element_type=floats)
-        scores = scores.reshape(heads, length, total_keys) * SCALE + bias_mask[...][None]
-        top = jnp.max(scores, axis=-1, keepdims=True)
-        raised = jnp.exp(scores - top)
-        shares = raised / jnp.sum(raised, axis=-1, keepdims=True)
-        shares = shares.reshape(heads * length, total_keys).astype(halves)
-        share_ref[kv, pl.ds(pack * heads, heads)] = shares.reshape(heads, length, total_keys)
-        summed = jnp.dot(shares, values, preferred_element_type=floats)
-        for index in range(heads):
-            lanes = pl.ds(pl.multiple_of((step * heads + index) * HEAD_DIM, 128), HEAD_DIM)
-            out_ref[:, lanes] = summed[index * length : (index + 1) * length]
-
-    for name in ("m0", "m1"):
-        gathers[name].hop_all(3)
-    for dz in range(2, nz):
-        cross(dz)
-    for name in ("m0", "m1"):
-        gathers[name].done()
-    saves = [
-        keep(joint_kv, kv_out),
-        keep(joint_q, query_out),
-        keep(merge, merge_out),
-    ]
-    attended = out_ref[...].astype(halves)
-    mixed = tokens_ref[...].astype(floats)
-    for part in range(2):
-        mixed = mixed + lax.dot_general(
-            attended[:, part * half : (part + 1) * half],
-            merge[part].reshape(model, half),
-            last_pair,
-            preferred_element_type=floats,
-        )
+    ct_on(outers.items()[0])
+    gathers["m"].to_core()
+    hand(0, 0)
+    hand(0, 1)
+
+    def attend(first, last):
+        @pl.loop(first, last)
+        def _(head):
+            keys = pair_ref[:, :, :HEAD_DIM].reshape(total_keys, HEAD_DIM)
+            values = pair_ref[:, :, HEAD_DIM:].reshape(total_keys, HEAD_DIM)
+            scores = lax.dot_general(
+                query_ref[head], keys, last_pair, preferred_element_type=floats
+            )
+            scores = scores * SCALE + bias_mask[...]
+            top = jnp.max(scores, axis=-1, keepdims=True)
+            raised = jnp.exp(scores - top)
+            shares = (raised / jnp.sum(raised, axis=-1, keepdims=True)).astype(halves)
+            share_ref[head] = shares
+            lanes = pl.ds(pl.multiple_of(head * HEAD_DIM, 128), HEAD_DIM)
+            out_ref[:, lanes] = jnp.dot(shares, values, preferred_element_type=floats)
+
+    attend(0, GROUP // 2)
+    take(1, 0)
+    give(3, 1)
+    attend(GROUP // 2, GROUP)
+    outers.start()
+    gathers["m"].done()
+    saves = [keep(joint_kv, kv_out), keep(joint_q, query_out), keep(merge, merge_out)]
+    merged = lax.dot_general(
+        out_ref[...].astype(halves),
+        merge[...].reshape(model, half),
+        last_pair,
+        preferred_element_type=floats,
+    )
+    mixed_ref[...] = jnp.where(x == 0, merged[:length], merged[length:])
+    mixed_send[...] = jnp.where(x == 0, merged[length:], merged[:length]).astype(halves)
+    mixed_cross = courier.copy(mixed_send, mixed_in, place.across["x"])
+    take(1, 1)
+    hand(2, 0)
+    for item in outers.items()[1:3]:
+        ct_on(item)
+    mixed_cross.wait_recv()
+    mixed = tokens_ref[...].astype(floats) + (mixed_ref[...] + mixed_in[...].astype(floats))
     mixed_ref[...] = mixed
     xn2_ref[...] = (mixed * norm_parts(mixed) * gain_second).astype(halves)
-
-    hand = []
-    for dz in range(nz):
-        w_cross[dz].wait_recv()
-        spot = w_ref.at[:, lax.rem(z + nz - dz, nz), :, :, c]
-        hand.append(courier.copy(spot, spot, place.across["c"]))
-    for made in hand:
+    take(3, 0)
+    hand(2, 1)
+    for item in outers.items()[3:5]:
+        ct_on(item)
+    hand(1, 0)
+    take(3, 1)
+    for item in outers.items()[5:]:
+        ct_on(item)
+    for spot in ((1, 1), (3, 0), (3, 1)):
+        hand(*spot)
+    for made in w_hand.values():
         made.wait_recv()
     for made in ct_side.values():
         made.wait_recv()
@@ -619,56 +691,111 @@
     courier.finish()
 
 
+class LineSum:
+    def __init__(self, courier, place, parts, spot, above, below):
+        self.courier, self.place, self.parts, self.spot = courier, place, parts, spot
+        self.arrivals = {1: above, -1: below}
+        self.sent = {}
+
+    def add(self, target, way):
+        nz = self.place.nz
+        spot = self.spot(target)
+        arrived = self.arrivals[way][target - 1 if way == 1 else target]
+        self.parts[spot] = (self.parts[spot].astype(floats) + arrived.astype(floats)).astype(
+            self.parts.dtype
+        )
+
+    def forward(self, target, way):
+        p = self.place
+        moving = p.z < target if way == 1 else p.z > target
+        fed = p.z > 0 if way == 1 else p.z < p.nz - 1
+        made = self.courier.make(
+            self.parts.at[self.spot(target)],
+            self.arrivals[way].at[target - 1 if way == 1 else target],
+            p.line_at(way),
+            moving,
+        )
+        self.sent[target, way] = made
+
+        @pl.when(moving & fed)
+        def _():
+            made.raw.wait_recv()
+            self.add(target, way)
+
+        made.start()
+
+    def forward_all(self):
+        nz = self.place.nz
+        for step in range(nz - 1):
+            self.forward(nz - 1 - step, 1)
+            self.forward(step, -1)
+
+    def finish(self):
+        p = self.place
+        for (target, way), made in self.sent.items():
+            fed = p.z > 0 if way == 1 else p.z < p.nz - 1
+
+            @pl.when((p.z == target) & fed)
+            def _(target=target, way=way, made=made):
+                made.raw.wait_recv()
+                self.add(target, way)
+
+
 class Scatter:
-    def __init__(self, courier, place, parts, core_in, second_in, first_in, line_in, order):
-        self.courier, self.place, self.order = courier, place, order
-        self.parts, self.line_in = parts, line_in
-        self.arrivals = [core_in, second_in, first_in]
-        self.hops = [{}, {}, {}, {}]
-
-    def spots(self, group):
+    def __init__(self, courier, place, parts, core_in, side_in, above, below, last_in):
+        self.courier, self.place, self.parts = courier, place, parts
+        self.core_in, self.side_in, self.last_in = core_in, side_in, last_in
+        every = slice(None)
+        self.line = LineSum(
+            courier, place, parts, lambda group: (group, every, place.y, place.c), above, below
+        )
+        self.groups = []
+        for step in range((place.nz + 1) // 2):
+            self.groups += [place.nz - 1 - step, step]
+        self.core, self.side = {}, {}
+
+    def to_core(self, group):
         p = self.place
-        if self.order == "xy":
-            second = ((group, p.x, slice(None), p.c), (group, 1 - p.x, slice(None), p.c))
-            first = ((group, p.x, p.y, p.c), (group, p.x, 1 - p.y, p.c))
-        else:
-            second = ((group, slice(None), p.y, p.c), (group, slice(None), 1 - p.y, p.c))
-            first = ((group, p.x, p.y, p.c), (group, 1 - p.x, p.y, p.c))
+        self.core[group] = self.courier.copy(
+            self.parts.at[group, :, :, 1 - p.c], self.core_in.at[group], p.across["c"]
+        )
+
+    def add(self, spot, arrived):
+        self.parts[spot] = (self.parts[spot].astype(floats) + arrived.astype(floats)).astype(
+            self.parts.dtype
+        )
+
+    def sideways(self):
+        p = self.place
         every = slice(None)
-        core = ((group, every, every, p.c), (group, every, every, 1 - p.c))
-        return [core, second, first]
-
-    def hop(self, number, dz):
+        for group in self.groups:
+            self.core[group].wait_recv()
+            self.add((group, every, every, p.c), self.core_in[group])
+            self.side[group] = self.courier.copy(
+                self.parts.at[group, :, 1 - p.y, p.c], self.side_in.at[group], p.across["y"]
+            )
+
+    def along(self):
         p = self.place
-        group = lax.rem(p.z + dz, p.nz)
-        spots = self.spots(group)
-        if number:
-            self.hops[number - 1][dz].wait_recv()
-            kept = spots[number - 1][0]
-            self.parts[kept] = (
-                self.parts[kept].astype(floats) + self.arrivals[number - 1][dz].astype(floats)
-            ).astype(self.parts.dtype)
-        if number < 3:
-            device = p.across[("c" + self.order)[number]]
-            self.hops[number][dz] = self.courier.copy(
-                self.parts.at[spots[number][1]], self.arrivals[number].at[dz], device
-            )
-        elif dz:
-            self.hops[3][dz] = self.courier.copy(
-                self.parts.at[spots[2][0]], self.line_in.at[dz - 1], p.line(dz)
-            )
-
-    def hop_all(self, number):
-        for dz in [(dz + self.place.nz // 2) % self.place.nz for dz in range(self.place.nz)]:
-            self.hop(number, dz)
-
-    def total(self):
+        for group in self.groups:
+            self.side[group].wait_recv()
+            self.add((group, slice(None), p.y, p.c), self.side_in[group])
+        self.line.forward_all()
+
+    def across(self):
         p = self.place
-        result = self.parts[p.z, p.x, p.y, p.c].astype(floats)
-        for dz in range(1, p.nz):
-            self.hops[3][dz].wait_recv()
-            result = result + self.line_in[dz - 1].astype(floats)
-        return result
+        self.line.finish()
+        self.last = self.courier.copy(
+            self.parts.at[p.z, 1 - p.x, p.y, p.c], self.last_in, p.across["x"]
+        )
+
+    def own(self):
+        p = self.place
+        return self.parts[p.z, p.x, p.y, p.c].astype(floats)
+
+    def other(self):
+        self.last.wait_recv()
+        return self.last_in[...].astype(floats)
 
 
 def gather_pieces(values, piece, devices):
@@ -706,54 +833,42 @@
     merge_grad_ref,
     small_grad_ref,
     grads_ref,
-    weight,
+    weight_m,
+    weight_q,
     weight_kv,
     gown,
     gin,
     branch_own,
     branch_in,
-    branch_line,
-    merge_part,
-    merge_c,
-    merge_s,
-    merge_f,
-    merge_z,
-    query_part,
-    query_c,
-    query_s,
-    query_f,
-    query_z,
-    kv_part,
-    kv_c,
-    kv_s,
-    kv_f,
-    kv_z,
-    small_part,
-    small_c,
-    small_s,
-    small_f,
-    small_z,
-    pair_sum,
-    pair_half,
-    pair_side,
-    pair_line,
-    joint_back,
-    attended_back,
-    query_back,
-    mixed_grad,
-    sends,
-    receives,
-    locals_,
+    branch_above,
+    branch_below,
+    *rest,
 ):
+    merge_bufs, query_bufs, kv_bufs, small_bufs = (rest[6 * i : 6 * i + 6] for i in range(4))
+    (
+        pair_sum,
+        pair_half,
+        pair_above,
+        pair_below,
+        joint_back,
+        attended_back,
+        mixed_both,
+        back_send,
+        back_in,
+        sends,
+        receives,
+        locals_,
+    ) = rest[24:]
     place = Place(nz)
     z, x, y, c = place.z, place.x, place.y, place.c
     length, model = tokens_ref.shape
     share = gown.shape[-1]
-    half = QUERY_WIDTH // 2
+    half = GROUP * HEAD_DIM
+    both = 2 * length
     block = model // nz
     depth = grads_in.shape[-2]
     devices = 8 * nz
-    total_keys = 2 * nz * length
+    total_keys = nz * both
     orders = [(dz + nz // 2) % nz for dz in range(nz)]
     courier = Courier(sends, receives)
     meet(place.peers())
@@ -769,71 +884,84 @@
         copies.append(made)
         return made
 
-    merge_load = load(m_ref, weight)
-    kv_load = load(kv_ref, weight_kv)
+    merge_load = load(m_ref, weight_m)
     branch_load = load(branch_ref.at[:, y], branch_own)
     gown_load = load(grads_in.at[:, :, x], gown)
-
-    g_cross = {
-        dz: courier.copy(grads_in.at[:, group_of(dz), 1 - x], gin.at[dz], place.across["x"])
-        for dz in orders
+    query_load = load(q_ref, weight_q)
+    kv_load = load(kv_ref, weight_kv)
+
+    b_cross = {
+        group: courier.copy(branch_ref.at[group, 1 - y], branch_in.at[group], place.across["y"])
+        for group in range(nz)
     }
-    b_cross = {
-        dz: courier.copy(branch_ref.at[group_of(dz), 1 - y], branch_in.at[dz], place.across["y"])
-        for dz in orders
-    }
+    g_cross, g_line, kept = {}, [], []
+
+    def grads_across(dz):
+        g_cross[dz] = courier.copy(
+            grads_in.at[:, group_of(dz), 1 - x], gin.at[dz], place.across["x"]
+        )
 
     mixed = mixed_ref[...]
     second_scale = norm_parts(mixed)
     part, second_local = norm_back(back_ref[...], mixed, second_scale, gain_ref[1:2, :])
     grad = outer_ref[...].astype(floats) + part
-    mixed_grad[...] = grad
-    mixed_half = grad.astype(halves)
-
-    def scatter(arrays, order):
-        return Scatter(courier, place, *arrays, order)
-
-    merges = [
-        scatter([ref.at[i] for ref in (merge_part, merge_c, merge_s, merge_f, merge_z)], order)
-        for i, order in ((0, "xy"), (1, "yx"))
-    ]
-    attended = out_ref[...].astype(halves)
-    mixed_turned = mixed_half.T
-    for group in range(nz):
-        for i in range(2):
-            merge_part[i, group] = (
+    tokens_grad_ref[...] = grad
+    mixed_both[x] = grad.astype(halves)
+    mixed_cross = courier.copy(mixed_both.at[x], mixed_both.at[x], place.across["x"])
+    grads_across(orders[0])
+    mixed_cross.wait_recv()
+    grads_across(orders[1])
+
+    merge_load.wait()
+    upstream_both = mixed_both[...].reshape(both, model)
+    attended_back[...] = jnp.dot(
+        upstream_both, weight_m[...].reshape(model, half), preferred_element_type=floats
+    ).astype(halves)
+    merges = Scatter(courier, place, *merge_bufs)
+    queries = Scatter(courier, place, *query_bufs)
+    keys_values = Scatter(courier, place, *kv_bufs)
+    smalls = Scatter(courier, place, *small_bufs)
+
+    def product_rows(scatter, left, right):
+        for group in scatter.groups:
+            scatter.parts[group] = (
                 jnp.dot(
-                    mixed_turned[group * block : (group + 1) * block],
-                    attended[:, i * half : (i + 1) * half],
-                    preferred_element_type=floats,
+                    left[group * block : (group + 1) * block], right, preferred_element_type=floats
                 )
                 .astype(halves)
-                .reshape(2, 2, 2, depth, half)
+                .reshape(2, 2, 2, depth, right.shape[1])
             )
-    for made in merges:
-        made.hop_all(0)
-    merge_load.wait()
-    for i in range(2):
-        attended_back[:, i * half : (i + 1) * half] = jnp.dot(
-            mixed_half, weight[i].reshape(model, half), preferred_element_type=floats
-        ).astype(halves)
-    query_load = load(q_ref, weight)
-
-    branch_load.wait()
+            scatter.to_core(group)
+
+    product_rows(merges, upstream_both.T, out_ref[...].astype(halves))
+
+    def attend(first, last):
+        @pl.loop(first, last)
+        def _(head):
+            query = query_ref[head]
+            keys = pair_ref[:, :, :HEAD_DIM].reshape(total_keys, HEAD_DIM)
+            values = pair_ref[:, :, HEAD_DIM:].reshape(total_keys, HEAD_DIM)
+            lanes = pl.ds(pl.multiple_of(head * HEAD_DIM, 128), HEAD_DIM)
+            upstream = attended_back[:, lanes]
+            delta = jnp.sum(upstream.astype(floats) * out_ref[:, lanes], axis=-1, keepdims=True)
+            mass = lax.dot_general(upstream, values, last_pair, preferred_element_type=floats)
+            shares = share_ref[head]
+            scores = (shares.astype(floats) * (mass - delta)).astype(halves)
+            query_sum = jnp.dot(scores, keys, preferred_element_type=floats) * SCALE
+            cosine, sine = turn_ref[0], turn_ref[1]
+            joint_back[:, lanes] = (
+                query_sum * cosine + pltpu.roll(query_sum * sine, HEAD_DIM // 2, 1)
+            ).astype(halves)
+            pair_sum[:, :HEAD_DIM] += (
+                jnp.dot(scores.T, query, preferred_element_type=floats) * SCALE
+            )
+            pair_sum[:, HEAD_DIM:] += jnp.dot(shares.T, upstream, preferred_element_type=floats)
+
+    pair_sum[...] = jnp.zeros_like(pair_sum)
+    attend(0, GROUP // 2)
+
     gown_load.wait()
-    b_line, g_line = {}, []
-    for dz in orders:
-        group = group_of(dz)
-        b_cross[dz].wait_recv()
-        branch_own[group] = (
-            branch_own[group].astype(floats) + branch_in[dz].astype(floats)
-        ).astype(halves)
-        if dz:
-            b_line[dz] = courier.copy(
-                branch_own.at[group], branch_line.at[dz - 1], place.line(dz)
-            )
     mine = pl.ds(pl.multiple_of((z * 2 + y) * share, 128), share)
-    kept = []
 
     def grads_on(dz):
         group = group_of(dz)
@@ -854,130 +982,67 @@
                 kept.append(load(gown.at[:, group, ty], grads_ref.at[:, :, mine]))
 
     grads_on(orders[0])
-    for made in merges:
-        made.hop_all(1)
-
-    heads = 2
-    pair_sum[...] = jnp.zeros_like(pair_sum)
-
-    @pl.loop(0, HEADS // heads)
-    def _(step):
-        kv = lax.div(step, GROUP // heads)
-        pack = lax.rem(step, GROUP // heads)
-        key_lanes = pl.ds(pl.multiple_of(kv * HEAD_DIM, 128), HEAD_DIM)
-        value_lanes = pl.ds(pl.multiple_of(KEY_WIDTH + kv * HEAD_DIM, 128), HEAD_DIM)
-        rows = heads * length
-        query = query_ref[kv, pl.ds(pack * heads, heads)].reshape(rows, HEAD_DIM)
-        keys = pair_ref[:, :, :, key_lanes].reshape(total_keys, HEAD_DIM)
-        values = pair_ref[:, :, :, value_lanes].reshape(total_keys, HEAD_DIM)
-        lanes = [
-            pl.ds(pl.multiple_of((step * heads + index) * HEAD_DIM, 128), HEAD_DIM)
-            for index in range(heads)
-        ]
-        upstream = jnp.concatenate([attended_back[:, at] for at in lanes], axis=0)
-        summed = jnp.concatenate([out_ref[:, at] for at in lanes], axis=0)
-        delta = jnp.sum(upstream.astype(floats) * summed, axis=-1, keepdims=True)
-        mass = lax.dot_general(upstream, values, last_pair, preferred_element_type=floats)
-        shares = share_ref[kv, pl.ds(pack * heads, heads)].reshape(rows, total_keys)
-        scores = (shares.astype(floats) * (mass - delta)).astype(halves)
-        query_sum = jnp.dot(scores, keys, preferred_element_type=floats) * SCALE
-        for index in range(heads):
-            query_back[:, lanes[index]] = query_sum[index * length : (index + 1) * length]
-        pair_sum[:, key_lanes] += jnp.dot(scores.T, query, preferred_element_type=floats) * SCALE
-        pair_sum[:, value_lanes] += jnp.dot(shares.T, upstream, preferred_element_type=floats)
-
-    pair_half[...] = pair_sum[...].astype(halves).reshape(nz, 2, length, 2 * KEY_WIDTH)
-    p_cross = {
-        dz: courier.copy(pair_half.at[group_of(dz), 1 - x], pair_side.at[dz], place.across["x"])
-        for dz in orders
-    }
-    grads_on(orders[1])
-    cosine, sine = turn_ref[0], turn_ref[1]
-
-    def unturned(values):
-        return values * cosine + pltpu.roll(values * sine, HEAD_DIM // 2, 1)
-
-    for head in range(HEADS):
-        lanes = slice(head * HEAD_DIM, (head + 1) * HEAD_DIM)
-        joint_back[:, lanes] = unturned(query_back[:, lanes]).astype(halves)
-    p_line = {}
-    for dz in orders:
-        group = group_of(dz)
-        p_cross[dz].wait_recv()
-        pair_half[group, x] = (
-            pair_half[group, x].astype(floats) + pair_side[dz].astype(floats)
+    grads_across(orders[2])
+    merges.sideways()
+    attend(GROUP // 2, GROUP)
+
+    pair_half[...] = pair_sum[...].astype(halves).reshape(nz, both, 2 * HEAD_DIM)
+    pairs = LineSum(courier, place, pair_half, lambda group: (group,), pair_above, pair_below)
+    pairs.forward(nz - 1, 1)
+    pairs.forward(0, -1)
+    turned = xn1_ref[...].T
+    product_rows(queries, turned, joint_back[:, :half])
+    for step in range(1, nz - 1):
+        pairs.forward(nz - 1 - step, 1)
+        pairs.forward(step, -1)
+    branch_load.wait()
+    for group in range(nz):
+        b_cross[group].wait_recv()
+        branch_own[group] = (
+            branch_own[group].astype(floats) + branch_in[group].astype(floats)
         ).astype(halves)
-        if dz:
-            p_line[dz] = courier.copy(
-                pair_half.at[group, x], pair_line.at[dz - 1], place.line(dz)
-            )
-    queries = [
-        scatter([ref.at[i] for ref in (query_part, query_c, query_s, query_f, query_z)], order)
-        for i, order in ((0, "xy"), (1, "yx"))
-    ]
-    keys_values = scatter([kv_part, kv_c, kv_s, kv_f, kv_z], "yx")
-    smalls = scatter([small_part, small_c, small_s, small_f, small_z], "xy")
-    turned = xn1_ref[...].T
-    for group in range(nz):
-        for i in range(2):
-            query_part[i, group] = (
-                jnp.dot(
-                    turned[group * block : (group + 1) * block],
-                    joint_back[:, i * half : (i + 1) * half],
-                    preferred_element_type=floats,
-                )
-                .astype(halves)
-                .reshape(2, 2, 2, depth, half)
-            )
-    for made in queries:
-        made.hop_all(0)
-    for made in merges:
-        made.hop_all(2)
-    total = pair_half[z, x].astype(floats)
-    for dz in range(1, nz):
-        p_line[dz].wait_recv()
-        total = total + pair_line[dz - 1].astype(floats)
-    for head in range(KV_HEADS):
-        lanes = slice(head * HEAD_DIM, (head + 1) * HEAD_DIM)
-        joint_back[:, QUERY_WIDTH + head * HEAD_DIM : QUERY_WIDTH + (head + 1) * HEAD_DIM] = (
-            unturned(total[:, lanes]).astype(halves)
-        )
-    joint_back[:, QUERY_WIDTH + KEY_WIDTH :] = total[:, KEY_WIDTH:].astype(halves)
-    for group in range(nz):
-        kv_part[group] = (
-            jnp.dot(
-                turned[group * block : (group + 1) * block],
-                joint_back[:, QUERY_WIDTH:],
-                preferred_element_type=floats,
-            )
-            .astype(halves)
-            .reshape(2, 2, 2, depth, 2 * KEY_WIDTH)
-        )
-    keys_values.hop_all(0)
-    for made in queries:
-        made.hop_all(1)
-    grads_on(orders[2])
-
+    pairs.finish()
+    total = pair_half[z].astype(floats)
+    key_total = total[:, :HEAD_DIM]
+    joint_back[:, half : half + HEAD_DIM] = (
+        key_total * turn_ref[0] + pltpu.roll(key_total * turn_ref[1], HEAD_DIM // 2, 1)
+    ).astype(halves)
+    joint_back[:, half + HEAD_DIM :] = total[:, HEAD_DIM:].astype(halves)
+    product_rows(keys_values, turned, joint_back[:, half:])
     query_load.wait()
     kv_load.wait()
     normal_back = lax.dot_general(
-        joint_back[:, QUERY_WIDTH:],
-        weight_kv[...].reshape(model, 2 * KEY_WIDTH),
+        joint_back[:, :half],
+        weight_q[...].reshape(model, half),
         last_pair,
         preferred_element_type=floats,
-    )
-    for i in range(2):
-        normal_back = normal_back + lax.dot_general(
-            joint_back[:, i * half : (i + 1) * half],
-            weight[i].reshape(model, half),
-            last_pair,
-            preferred_element_type=floats,
-        )
+    ) + lax.dot_general(
+        joint_back[:, half:],
+        weight_kv[...].reshape(model, 2 * HEAD_DIM),
+        last_pair,
+        preferred_element_type=floats,
+    )
+    back_send[...] = jnp.where(x == 0, normal_back[length:], normal_back[:length]).astype(halves)
+    back_cross = courier.copy(back_send, back_in, place.across["x"])
+    normal_own = jnp.where(x == 0, normal_back[:length], normal_back[length:])
+    queries.sideways()
+    keys_values.sideways()
+    grads_on(orders[1])
+    grads_across(orders[3])
+    merges.along()
+
+    back_cross.wait_recv()
+    normal_own = normal_own + back_in[...].astype(floats)
     residual = tokens_ref[...].astype(floats)
-    part, first_local = norm_back(normal_back, residual, norm_parts(residual), gain_ref[0:1, :])
-    tokens_grad_ref[...] = mixed_grad[...] + part
-    bias_local = jnp.sum(joint_back[...].astype(floats), axis=0, keepdims=True)
-
+    part, first_local = norm_back(normal_own, residual, norm_parts(residual), gain_ref[0:1, :])
+    tokens_grad_ref[...] += part
+
+    local = jnp.sum(joint_back[...].astype(floats), axis=0, keepdims=True)
+    pieces_of = []
+    for first, width in ((0, half), (half, HEAD_DIM), (half + HEAD_DIM, HEAD_DIM)):
+        for side in range(2):
+            pieces_of.append(jnp.where(x == side, local[:, first : first + width], 0.0))
+    bias_local = jnp.concatenate(pieces_of, axis=1)
     pieces = jnp.zeros((devices * 8, 128), floats)
     for which, values in ((0, bias_local), (1, first_local), (2, second_local)):
         mine_rows = gather_pieces(values, values.shape[1] // devices, devices)
@@ -989,28 +1054,32 @@
             preferred_element_type=floats,
             precision=lax.Precision.HIGHEST,
         )
-    small_part[...] = pieces.reshape(nz, 2, 2, 2, 8, 128)
-    smalls.hop_all(0)
-    keys_values.hop_all(1)
-    smalls.hop_all(1)
-    for made in queries:
-        made.hop_all(2)
-    keys_values.hop_all(2)
-    smalls.hop_all(2)
-    for dz in orders[3:]:
-        grads_on(dz)
-    for made in merges + queries + [keys_values, smalls]:
-        made.hop_all(3)
-    total = mixed_ref[...] + branch_own[z].astype(floats)
-    for dz in range(1, nz):
-        b_line[dz].wait_recv()
-        total = total + branch_line[dz - 1].astype(floats)
-    output_ref[...] = total.astype(halves)
-    for i in range(2):
-        merge_grad_ref[:, i * half : (i + 1) * half] = merges[i].total()
-        joint_grad_ref[:, i * half : (i + 1) * half] = queries[i].total()
-    joint_grad_ref[:, QUERY_WIDTH:] = keys_values.total()
-    small_grad_ref[...] = smalls.total()
+    smalls.parts[...] = pieces.reshape(nz, 2, 2, 2, 8, 128)
+    for group in smalls.groups:
+        smalls.to_core(group)
+    keys_values.along()
+    queries.along()
+    smalls.sideways()
+    grads_on(orders[2])
+    branches = LineSum(
+        courier, place, branch_own, lambda group: (group,), branch_above, branch_below
+    )
+    branches.forward_all()
+    smalls.along()
+    merges.across()
+    grads_on(orders[3])
+    keys_values.across()
+    queries.across()
+    smalls.across()
+    branches.finish()
+    output_ref[...] = (mixed_ref[...] + branch_own[z].astype(floats)).astype(halves)
+    merge_grad_ref[x] = merges.own()
+    merge_grad_ref[1 - x] = merges.other()
+    joint_grad_ref[x, :, :half] = queries.own()
+    joint_grad_ref[1 - x, :, :half] = queries.other()
+    joint_grad_ref[x, :, half:] = keys_values.own()
+    joint_grad_ref[1 - x, :, half:] = keys_values.other()
+    small_grad_ref[...] = smalls.own() + smalls.other()
     for made in g_line:
         made.wait_recv()
     for made in kept:
@@ -1040,9 +1109,10 @@
     hidden_width = gate_matrix.shape[1]
     nz = lax.axis_size("z")
     share = padded_share(hidden_width, 2 * nz)
-    half = QUERY_WIDTH // 2
-    pair_width = 2 * KEY_WIDTH
-    keys = 2 * nz * length
+    half = GROUP * HEAD_DIM
+    pair_width = 2 * HEAD_DIM
+    both = 2 * length
+    keys = nz * both
     vmem = pl.BlockSpec(memory_space=pltpu.VMEM)
     anywhere = pl.BlockSpec(memory_space=pl.ANY)
     blocks = (nz, 2, 2, 2)
@@ -1075,7 +1145,20 @@
     )
     inverse = jnp.power(floats(theta), -(jnp.arange(HEAD_DIM // 2, dtype=floats) * (2.0 / HEAD_DIM)))
     inverse = jnp.concatenate([inverse, inverse])[None]
-    labels = own_labels.astype(floats)[:, None]
+    joint_halves = jnp.stack(
+        [
+            jnp.concatenate(
+                [
+                    joint_matrix[:, side * half : (side + 1) * half],
+                    joint_matrix[:, QUERY_WIDTH + side * HEAD_DIM :][:, :HEAD_DIM],
+                    joint_matrix[:, QUERY_WIDTH + KEY_WIDTH + side * HEAD_DIM :][:, :HEAD_DIM],
+                ],
+                axis=1,
+            )
+            for side in range(2)
+        ]
+    )
+    merge_halves = merge_matrix.T.reshape(depth, 2, half).transpose(1, 0, 2)
     outer = cotangent[0]
     (
         w,
@@ -1099,32 +1182,33 @@
             shape((3,) + blocks + (depth, share)),
             shape((nz, 2, length, model)),
             shape(blocks + (depth, pair_width)),
-            shape((2,) + blocks + (depth, half)),
-            shape((2,) + blocks + (depth, half)),
-            shape((length, model)),
+            shape(blocks + (depth, half)),
+            shape(blocks + (depth, half)),
+            shape((both, model)),
             shape((length, model)),
             shape((length, model), floats),
             shape((8, model), floats),
-            shape((2, length, HEAD_DIM), floats),
-            shape((KV_HEADS, GROUP, length, HEAD_DIM)),
-            shape((nz, 2, length, pair_width)),
-            shape((KV_HEADS, GROUP, length, keys)),
-            shape((length, QUERY_WIDTH), floats),
+            shape((2, both, HEAD_DIM), floats),
+            shape((GROUP, both, HEAD_DIM)),
+            shape((nz, both, pair_width)),
+            shape((GROUP, both, keys)),
+            shape((both, half), floats),
         ),
-        in_specs=[anywhere] * 3 + [vmem] * 5,
+        in_specs=[anywhere] * 3 + [vmem] * 4,
         out_specs=(anywhere,) * 5 + (vmem,) * 9,
         scratch_shapes=[
             pltpu.VMEM(blocks + (depth, pair_width), halves),
-            pltpu.VMEM((2,) + blocks + (depth, half), halves),
-            pltpu.VMEM((2,) + blocks + (depth, half), halves),
+            pltpu.VMEM(blocks + (depth, half), halves),
+            pltpu.VMEM(blocks + (depth, half), halves),
             pltpu.VMEM(blocks + (8, 128), floats),
-            pltpu.VMEM((length, keys), floats),
-            pltpu.VMEM((length, QUERY_WIDTH), floats),
-            pltpu.VMEM((length, pair_width), halves),
+            pltpu.VMEM((both, keys), floats),
+            pltpu.VMEM((2, length, model), halves),
+            pltpu.VMEM((length, model), halves),
+            pltpu.VMEM((length, model), halves),
         ]
-        + semaphores(119, 11),
+        + semaphores(136, 9),
         compiler_params=params(0),
-    )(stack, joint_matrix, merge_matrix.T, small, labels, inverse, tokens[0], outer)
+    )(stack, joint_halves, merge_halves, small, inverse, tokens[0], outer)
 
     lines = 2 * length
     back, branch, grads = pl.pallas_call(
@@ -1154,13 +1238,14 @@
         compiler_params=params(1),
     )(w, team_outer, xn2)
 
-    def sums(rows, width, kind=halves, lead=()):
+    def sums(rows, width, kind=halves):
         return [
-            pltpu.VMEM(lead + blocks + (rows, width), kind),
-            pltpu.VMEM(lead + (nz, 2, 2, rows, width), kind),
-            pltpu.VMEM(lead + (nz, 2, rows, width), kind),
-            pltpu.VMEM(lead + (nz, rows, width), kind),
-            pltpu.VMEM(lead + (nz - 1, rows, width), kind),
+            pltpu.VMEM(blocks + (rows, width), kind),
+            pltpu.VMEM((nz, 2, 2, rows, width), kind),
+            pltpu.VMEM((nz, 2, rows, width), kind),
+            pltpu.VMEM((nz - 1, 2, rows, width), kind),
+            pltpu.VMEM((nz - 1, 2, rows, width), kind),
+            pltpu.VMEM((rows, width), kind),
         ]
 
     output, tokens_grad, joint_grad, merge_grad, small_grad, grads = pl.pallas_call(
@@ -1169,37 +1254,40 @@
         out_shape=(
             shape((length, model)),
             shape((length, model), floats),
-            shape((depth, joint_width), floats),
-            shape((depth, QUERY_WIDTH), floats),
+            shape((2, depth, half + pair_width), floats),
+            shape((2, depth, half), floats),
             shape((8, 128), floats),
             shape((3, depth, 2 * nz * share)),
         ),
         in_specs=[anywhere] * 5 + [vmem] * 11,
         out_specs=(vmem,) * 5 + (anywhere,),
         scratch_shapes=[
-            pltpu.VMEM((2,) + blocks + (depth, half), halves),
+            pltpu.VMEM(blocks + (depth, half), halves),
+            pltpu.VMEM(blocks + (depth, half), halves),
             pltpu.VMEM(blocks + (depth, pair_width), halves),
             pltpu.VMEM((3, nz, 2, depth, share), halves),
             pltpu.VMEM((nz, 3, 2, depth, share), halves),
             pltpu.VMEM((nz, length, model), halves),
             pltpu.VMEM((nz, length, model), halves),
             pltpu.VMEM((nz - 1, length, model), halves),
+            pltpu.VMEM((nz - 1, length, model), halves),
         ]
-        + sums(depth, half, lead=(2,))
-        + sums(depth, half, lead=(2,))
+        + sums(depth, half)
+        + sums(depth, half)
         + sums(depth, pair_width)
         + sums(8, 128, floats)
         + [
             pltpu.VMEM((keys, pair_width), floats),
-            pltpu.VMEM((nz, 2, length, pair_width), halves),
-            pltpu.VMEM((nz, length, pair_width), halves),
-            pltpu.VMEM((nz - 1, length, pair_width), halves),
-            pltpu.VMEM((length, joint_width), halves),
-            pltpu.VMEM((length, QUERY_WIDTH), halves),
-            pltpu.VMEM((length, QUERY_WIDTH), floats),
-            pltpu.VMEM((length, model), floats),
+            pltpu.VMEM((nz, both, pair_width), halves),
+            pltpu.VMEM((nz - 1, both, pair_width), halves),
+            pltpu.VMEM((nz - 1, both, pair_width), halves),
+            pltpu.VMEM((both, half + pair_width), halves),
+            pltpu.VMEM((both, half), halves),
+            pltpu.VMEM((2, length, model), halves),
+            pltpu.VMEM((length, model), halves),
+            pltpu.VMEM((length, model), halves),
         ]
-        + semaphores(115, 6),
+        + semaphores(89, 6),
         compiler_params=params(2),
     )(
         grads,
@@ -1219,6 +1307,15 @@
         shares,
         summed,
     )
+    joint_grad = jnp.concatenate(
+        [
+            joint_grad[side, :, first : first + width]
+            for first, width in ((0, half), (half, HEAD_DIM), (half + HEAD_DIM, HEAD_DIM))
+            for side in range(2)
+        ],
+        axis=1,
+    )
+    merge_grad = merge_grad.transpose(1, 0, 2).reshape(depth, QUERY_WIDTH)
     grads = grads[:, :, :hidden_width].astype(floats)
     return (
         output[None],

time: 556 us -> 469 us (0.84)
  the two profiles are of different devices: /device:TPU:0 before, /device:TPU:22 now
where the time goes in v4:
time: 469 us; the launch traced here: 460 us
  Pallas kernels  434 us (93%)
  local copies, waits for them, and re-layouts  16.9 us (4%)
  other arithmetic  8.46 us (2%)
    pallas_call x1, Pallas kernels, body_kernels(): pl.pallas_call(functools.partial(back_kernel, nz), name='attention_backwa...  193 us
    pallas_call x1, Pallas kernels, body_kernels(): pl.pallas_call(functools.partial(attention_kernel, nz), name='attention_f...  135 us
    pallas_call x1, Pallas kernels, body_kernels(): pl.pallas_call(functools.partial(feed_kernel, nz), name='feed_forward', o...  106 us

profile of v4, /device:TPU:22, one launch (start us, length us, event | category | flops | bytes accessed | tf_op | source)
XLA Modules:
  0.0 460.5 jit_solution(2894845876324169931)
XLA Ops:
  0.6 0.7 convert_element_type.17
  1.3 0.7 bitcast_convert_fusion.2
  2.0 0.6 maximum_bitcast_fusion.2.inverse_ref
  2.6 0.7 bitcast_convert_fusion
  3.2 0.6 stack.60.small_ref
  3.8 0.8 fusion.6
  4.6 1.6 copy.26
  6.2 0.9 fusion.5
  7.2 0.7 pad_maximum_fusion.joint_ref
  7.8 2.9 fusion.4.stack_ref
  10.8 135.4 %attention_forward.1 = (bf16[3,4,2,2,2,48,1152]{6,5,4,3,2,1,0:T(8,128)(2,1)}, bf16[4,2,128,1536]{3,2,1,0:T(8,128)(2,1)}, bf16[4,2,2,2,48,256]{5,4,3,2,1,0:T(8,12...) custom-call(bf16[3,48,9216]{2,1,0:T(8,128)(2,1)} %fusion.4.stack_ref, ...), custom_call_target="tpu_custom_call" | custom-call | tf_op jit(solution)/shard_map/attention_forward/pallas_call | solution.py:1178
  146.2 106.0 %feed_forward.1 = (f32[128,1536]{1,0:T(8,128)}, bf16[4,2,128,1536]{3,2,1,0:T(8,128)(2,1)}, bf16[3,4,2,2,48,1152]{5,4,3,2,1,0:T(8,128)(2,1)}) custom-call(bf16[3,4,2,2,2,48,1152]{6,5,4,3,2,1,0:T(8,128)(2,1)} %get-tuple-element.33.w_ref, bf16[4,2,128,1536]{3,2,1,0:T(8,128)(2,1)} %get-tuple-element.34.ct_ref, bf16[128,1536]{1,0:T(8,128)(2,1)} %get-tuple-element.35.normal_ref), custom_call_target="tpu_custom_call" | custom-call | tf_op jit(solution)/shard_map/feed_forward/pallas_call | solution.py:1214
  252.2 192.8 %attention_backward.1 = (bf16[128,1536]{1,0:T(8,128)(2,1)}, f32[128,1536]{1,0:T(8,128)}, f32[2,48,1024]{2,1,0:T(8,128)}, f32[2,48,768]{2,1,0:T(8,128)}, f32[8,128]{1,0:T(8,128)}, /*index=5*/bf16[3,48,9216]{2,1,0:T(8,128)(2,1)}) custom-call(bf16[3,4,2,2,48,1152]{5,4,3,2,1,0:T(8,128)(2,1)} %get-tuple-element.36.grads_in, ...), custom_call_target="tpu_custom_call" | custom-call | tf_op jit(solution)/shard_map/attention_backward/pallas_call | solution.py:1251
  445.0 1.2 slice_bitcast_fusion.5
  446.2 1.3 slice_bitcast_fusion.3
  447.4 1.7 copy.24
  449.1 0.9 bitcast_dynamic-update-slice_fusion.1
  450.0 0.9 bitcast_dynamic-update-slice_fusion
  451.0 0.7 bitcast_dynamic-update-slice_fusion.5
  451.7 0.7 bitcast_dynamic-update-slice_fusion.4
  452.5 0.7 bitcast_dynamic-update-slice_fusion.3
  453.2 0.7 bitcast_dynamic-update-slice_fusion.2
  453.9 0.0 copy-start.2
  453.9 2.2 slice_convert_fusion
  456.2 0.0 copy-done.2
  456.2 0.0 copy-start.1
  456.2 0.0 copy-start
  456.2 2.4 slice_bitcast_fusion
  458.6 0.0 copy-done.1
  458.6 0.7 copy.34
  459.4 0.0 copy-done
  459.4 0.9 copy.35
  (3 shorter events, 0.0 us)
Async XLA Ops:
  453.9 2.2 copy-start.2
  456.2 2.5 copy-start.1
  456.2 3.2 copy-start

commit v5 on v4

--- a/solution.py
+++ b/solution.py
@@ -3,6 +3,7 @@
 
 import jax
 import jax.numpy as jnp
+import numpy as np
 from jax import lax
 from jax.experimental import pallas as pl
 from jax.experimental.pallas import tpu as pltpu
@@ -15,6 +16,7 @@
 GROUP = HEADS // KV_HEADS
 QUERY_WIDTH = HEADS * HEAD_DIM
 KEY_WIDTH = KV_HEADS * HEAD_DIM
+KV_PIECES = [(QUERY_WIDTH, HEAD_DIM), (QUERY_WIDTH + KEY_WIDTH, HEAD_DIM)]
 SCALE = 1.0 / math.sqrt(HEAD_DIM)
 
 eps = 1e-06
@@ -150,6 +152,10 @@
     pl.semaphore_wait(barrier, len(devices))
 
 
+def far_first(nz):
+    return sorted(range(nz), key=lambda dz: (dz == 0, abs(2 * dz - nz)))
+
+
 def cuts_of(width, step):
     return [(start, min(step, width - start)) for start in range(0, width, step)]
 
@@ -199,12 +205,15 @@
 
     def start(self):
         p = self.place
-        self.cross = self.courier.copy(
-            self.source, self.buffer.at[p.z, p.x, p.y, p.c], p.across["x"]
-        )
+        spot = self.buffer.at[p.z, p.x, p.y, p.c]
+        self.cross = [
+            self.courier.copy(source, spot.at[:, lanes], p.across["x"])
+            for source, lanes in self.source
+        ]
 
     def along(self):
-        self.cross.wait_recv()
+        for made in self.cross:
+            made.wait_recv()
         self.line.start()
         self.sideways(self.line.items()[0])
 
@@ -300,14 +309,13 @@
     place = Place(nz)
     z, x, y, c = place.z, place.x, place.y, place.c
     length, model = tokens_ref.shape
-    depth = joint_ref.shape[1]
+    depth, joint_width = joint_ref.shape
     share = w_ref.shape[-1]
     half = GROUP * HEAD_DIM
     both = 2 * length
     total_keys = nz * both
     courier = Courier(sends, receives)
     devices = 8 * nz
-    joint_width = 2 * joint_ref.shape[2]
     meet(place.peers())
 
     own_copies = []
@@ -323,16 +331,28 @@
 
     gathers, own_waits = {}, {}
 
-    def begin(name, own, other, buffer):
-        own_waits[name] = keep(own, buffer.at[z, x, y, c])
-        gathers[name] = Gather(courier, place, other, buffer)
+    def begin(name, ref, pieces, buffer):
+        def from_side(side):
+            found = []
+            at = 0
+            for first, width in pieces:
+                lanes = pl.ds(pl.multiple_of(first + side * width, 128), width)
+                found.append((ref.at[:, lanes], slice(at, at + width)))
+                at += width
+            return found
+
+        spot = buffer.at[z, x, y, c]
+        own_waits[name] = [keep(own, spot.at[:, lanes]) for own, lanes in from_side(x)]
+        gathers[name] = Gather(courier, place, from_side(1 - x), buffer)
         gathers[name].start()
 
-    begin("small", small_ref, small_ref, small)
-    begin("kv", joint_ref.at[x, :, half:], joint_ref.at[1 - x, :, half:], joint_kv)
+    own_waits["small"] = [keep(small_ref, small.at[z, x, y, c])]
+    gathers["small"] = Gather(courier, place, [(small_ref, slice(None))], small)
+    gathers["small"].start()
+    begin("kv", joint_ref, KV_PIECES, joint_kv)
     token_cross = courier.copy(tokens_ref, tokens_all.at[x], place.across["x"])
-    begin("q", joint_ref.at[x, :, :half], joint_ref.at[1 - x, :, :half], joint_q)
-    begin("m", merge_ref.at[x], merge_ref.at[1 - x], merge)
+    begin("q", joint_ref, [(0, half)], joint_q)
+    begin("m", merge_ref, [(0, half)], merge)
     tokens_all[x] = tokens_ref[...]
     w_own = keep(stack_ref.at[:, :, columns(z, y)], w_ref.at[:, z, x, y, c])
     ct_own = keep(outer_ref, ct_ref.at[z, y])
@@ -363,14 +383,16 @@
     give(0, 1)
     give(2, 0)
     for name in ("small", "kv"):
-        own_waits[name].wait()
+        for made in own_waits[name]:
+            made.wait()
         gathers[name].along()
     token_cross.wait_recv()
     tokens_both = tokens_all[...].reshape(both, model).astype(floats)
     hat = tokens_both * norm_parts(tokens_both)
     for name in ("small", "kv"):
         gathers[name].pass_on(1)
-    own_waits["q"].wait()
+    for made in own_waits["q"] + own_waits["m"]:
+        made.wait()
     gathers["q"].along()
     for step in range(2, nz):
         for name in ("small", "kv"):
@@ -385,7 +407,6 @@
         gathers[name].done()
     take(0, 1)
     give(2, 1)
-    own_waits["m"].wait()
 
     pieces = small[...].reshape(devices * 8, 128).astype(halves)
 
@@ -537,6 +558,7 @@
     normal_ref,
     back_ref,
     branch_ref,
+    done_ref,
     grads_ref,
     w,
     xn,
@@ -549,6 +571,7 @@
     zsend,
     zbuf,
     cbuf,
+    xbuf,
     sends,
     receives,
     locals_,
@@ -564,7 +587,7 @@
     def source(dz):
         return lax.rem(z + nz - dz, nz)
 
-    meet([place.line(dz) for dz in range(1, nz)] + [place.across["y"], place.across["c"]])
+    meet([place.line(dz) for dz in range(1, nz)] + [place.across[name] for name in "xyc"])
     along = {
         dz: courier.copy(normal_ref, xn.at[z, y], place.line(dz)) for dz in range(1, nz)
     }
@@ -625,7 +648,8 @@
         )
 
     final = {}
-    for dz in [(dz + nz // 2) % nz for dz in range(nz)]:
+
+    def sum_on(dz):
         group = source(dz)
         scatter[dz].wait_recv()
         total = part[group, y].astype(floats) + ybuf[group].astype(floats)
@@ -649,9 +673,18 @@
             )
             branch_ref[group, :, :, lanes] = product.astype(halves).reshape(2, length, model // 2)
 
-    saves, handed = [], []
-    for group in range(nz):
-        lanes = slice(group * block, (group + 1) * block)
+    orders = far_first(nz)
+    early = 2
+    handed, crossed, saves = {}, {}, []
+
+    def save(source, target):
+        made = pltpu.make_async_copy(source, target, locals_.at[4 + len(saves)])
+        made.start()
+        saves.append(made)
+
+    def product(dz):
+        group = lax.rem(z + dz, nz)
+        lanes = pl.ds(pl.multiple_of(group * block, 128), block)
         normal_turned = xn[:, :, :, lanes].reshape(lines, block).T
         outer_turned = ct[:, :, :, lanes].reshape(lines, block).T
         for which, left, right in (
@@ -669,20 +702,39 @@
                     .astype(halves)
                     .reshape(2, 2, 2, -1, size)
                 )
-        handed.append(
-            courier.copy(w.at[:, group, :, :, 1 - c], cbuf.at[group], place.across["c"])
+        handed[dz] = courier.copy(
+            w.at[:, group, :, :, 1 - c], cbuf.at[dz], place.across["c"]
         )
-    for group in range(nz):
-        handed[group].wait_recv()
+
+    def settle(position):
+        dz = orders[position]
+        group = lax.rem(z + dz, nz)
+        handed[dz].wait_recv()
         for which in range(3):
             w[which, group, :, :, c] = (
-                w[which, group, :, :, c].astype(floats) + cbuf[group, which].astype(floats)
+                w[which, group, :, :, c].astype(floats) + cbuf[dz, which].astype(floats)
             ).astype(halves)
-        made = pltpu.make_async_copy(
-            w.at[:, group, :, :, c], grads_ref.at[:, group], locals_.at[4 + group]
-        )
-        made.start()
-        saves.append(made)
+        if position < early:
+            crossed[position] = courier.copy(
+                w.at[:, group, 1 - x, :, c], xbuf.at[position], place.across["x"]
+            )
+        else:
+            save(w.at[:, group, :, :, c], grads_ref.at[:, position - early])
+
+    for position in range(nz):
+        product(orders[position])
+        sum_on(position)
+        if position:
+            settle(position - 1)
+    settle(nz - 1)
+    for position in range(early):
+        group = lax.rem(z + orders[position], nz)
+        crossed[position].wait_recv()
+        for which in range(3):
+            w[which, group, x, :, c] = (
+                w[which, group, x, :, c].astype(floats) + xbuf[position, which].astype(floats)
+            ).astype(halves)
+        save(w.at[:, group, x, :, c], done_ref.at[:, position])
     for dz in range(1, nz):
         final[dz].wait_recv()
         back_ref[...] += zbuf[dz - 1].astype(floats)
@@ -724,11 +776,9 @@
 
         made.start()
 
-    def forward_all(self):
-        nz = self.place.nz
-        for step in range(nz - 1):
-            self.forward(nz - 1 - step, 1)
-            self.forward(step, -1)
+    def forward_step(self, step):
+        self.forward(self.place.nz - 1 - step, 1)
+        self.forward(step, -1)
 
     def finish(self):
         p = self.place
@@ -780,7 +830,6 @@
         for group in self.groups:
             self.side[group].wait_recv()
             self.add((group, slice(None), p.y, p.c), self.side_in[group])
-        self.line.forward_all()
 
     def across(self):
         p = self.place
@@ -811,6 +860,7 @@
 
 def back_kernel(
     nz,
+    done_ref,
     grads_in,
     branch_ref,
     kv_ref,
@@ -869,7 +919,7 @@
     depth = grads_in.shape[-2]
     devices = 8 * nz
     total_keys = nz * both
-    orders = [(dz + nz // 2) % nz for dz in range(nz)]
+    orders = far_first(nz)
     courier = Courier(sends, receives)
     meet(place.peers())
 
@@ -887,6 +937,8 @@
     merge_load = load(m_ref, weight_m)
     branch_load = load(branch_ref.at[:, y], branch_own)
     gown_load = load(grads_in.at[:, :, x], gown)
+    early = 2
+    late = orders[early:]
     query_load = load(q_ref, weight_q)
     kv_load = load(kv_ref, weight_kv)
 
@@ -898,8 +950,25 @@
 
     def grads_across(dz):
         g_cross[dz] = courier.copy(
-            grads_in.at[:, group_of(dz), 1 - x], gin.at[dz], place.across["x"]
+            grads_in.at[:, late.index(dz), 1 - x], gin.at[late.index(dz)], place.across["x"]
         )
+
+    mine = pl.ds(pl.multiple_of((z * 2 + y) * share, 128), share)
+
+    def grads_line(dz, rows):
+        for dy in range(2):
+            ty = lax.rem(y + dy, 2)
+            if dz or dy:
+                g_line.append(
+                    courier.copy(
+                        rows.at[:, ty], grads_ref.at[:, :, mine], (group_of(dz), x, ty, c)
+                    )
+                )
+            else:
+                kept.append(load(rows.at[:, ty], grads_ref.at[:, :, mine]))
+
+    for position in range(early):
+        grads_line(orders[position], done_ref.at[:, position])
 
     mixed = mixed_ref[...]
     second_scale = norm_parts(mixed)
@@ -908,9 +977,9 @@
     tokens_grad_ref[...] = grad
     mixed_both[x] = grad.astype(halves)
     mixed_cross = courier.copy(mixed_both.at[x], mixed_both.at[x], place.across["x"])
-    grads_across(orders[0])
     mixed_cross.wait_recv()
-    grads_across(orders[1])
+    for dz in late:
+        grads_across(dz)
 
     merge_load.wait()
     upstream_both = mixed_both[...].reshape(both, model)
@@ -957,33 +1026,19 @@
             )
             pair_sum[:, HEAD_DIM:] += jnp.dot(shares.T, upstream, preferred_element_type=floats)
 
+    def grads_on(dz):
+        at = late.index(dz)
+        g_cross[dz].wait_recv()
+        for which in range(3):
+            gown[which, at] = (
+                gown[which, at].astype(floats) + gin[at, which].astype(floats)
+            ).astype(halves)
+        grads_line(dz, gown.at[:, at])
+
     pair_sum[...] = jnp.zeros_like(pair_sum)
     attend(0, GROUP // 2)
-
-    gown_load.wait()
-    mine = pl.ds(pl.multiple_of((z * 2 + y) * share, 128), share)
-
-    def grads_on(dz):
-        group = group_of(dz)
-        g_cross[dz].wait_recv()
-        for which in range(3):
-            gown[which, group] = (
-                gown[which, group].astype(floats) + gin[dz, which].astype(floats)
-            ).astype(halves)
-        for dy in range(2):
-            ty = lax.rem(y + dy, 2)
-            if dz or dy:
-                g_line.append(
-                    courier.copy(
-                        gown.at[:, group, ty], grads_ref.at[:, :, mine], (group, x, ty, c)
-                    )
-                )
-            else:
-                kept.append(load(gown.at[:, group, ty], grads_ref.at[:, :, mine]))
-
-    grads_on(orders[0])
-    grads_across(orders[2])
     merges.sideways()
+
     attend(GROUP // 2, GROUP)
 
     pair_half[...] = pair_sum[...].astype(halves).reshape(nz, both, 2 * HEAD_DIM)
@@ -1027,9 +1082,9 @@
     normal_own = jnp.where(x == 0, normal_back[:length], normal_back[length:])
     queries.sideways()
     keys_values.sideways()
-    grads_on(orders[1])
-    grads_across(orders[3])
-    merges.along()
+    gown_load.wait()
+    for dz in late[:1]:
+        grads_on(dz)
 
     back_cross.wait_recv()
     normal_own = normal_own + back_in[...].astype(floats)
@@ -1057,28 +1112,33 @@
     smalls.parts[...] = pieces.reshape(nz, 2, 2, 2, 8, 128)
     for group in smalls.groups:
         smalls.to_core(group)
-    keys_values.along()
-    queries.along()
+    for dz in late[1:]:
+        grads_on(dz)
     smalls.sideways()
-    grads_on(orders[2])
+    for made in (merges, queries, keys_values):
+        made.along()
     branches = LineSum(
         courier, place, branch_own, lambda group: (group,), branch_above, branch_below
     )
-    branches.forward_all()
     smalls.along()
-    merges.across()
-    grads_on(orders[3])
-    keys_values.across()
-    queries.across()
-    smalls.across()
+    for step in range(nz - 1):
+        for line in (smalls.line, keys_values.line, queries.line, merges.line, branches):
+            line.forward_step(step)
+    for made in (merges, queries, keys_values, smalls):
+        made.across()
     branches.finish()
     output_ref[...] = (mixed_ref[...] + branch_own[z].astype(floats)).astype(halves)
-    merge_grad_ref[x] = merges.own()
-    merge_grad_ref[1 - x] = merges.other()
-    joint_grad_ref[x, :, :half] = queries.own()
-    joint_grad_ref[1 - x, :, :half] = queries.other()
-    joint_grad_ref[x, :, half:] = keys_values.own()
-    joint_grad_ref[1 - x, :, half:] = keys_values.other()
+    for ref, made, pieces in (
+        (merge_grad_ref, merges, [(0, half)]),
+        (joint_grad_ref, queries, [(0, half)]),
+        (joint_grad_ref, keys_values, KV_PIECES),
+    ):
+        for side, values in ((x, made.own()), (1 - x, made.other())):
+            at = 0
+            for first, width in pieces:
+                lanes = pl.ds(pl.multiple_of(first + side * width, 128), width)
+                ref[:, lanes] = values[:, at : at + width]
+                at += width
     small_grad_ref[...] = smalls.own() + smalls.other()
     for made in g_line:
         made.wait_recv()
@@ -1143,22 +1203,8 @@
     small = jnp.stack(
         [lane_row(v) for v in (joint_bias, norm_first, norm_second, own_labels)] + [empty] * 4
     )
-    inverse = jnp.power(floats(theta), -(jnp.arange(HEAD_DIM // 2, dtype=floats) * (2.0 / HEAD_DIM)))
-    inverse = jnp.concatenate([inverse, inverse])[None]
-    joint_halves = jnp.stack(
-        [
-            jnp.concatenate(
-                [
-                    joint_matrix[:, side * half : (side + 1) * half],
-                    joint_matrix[:, QUERY_WIDTH + side * HEAD_DIM :][:, :HEAD_DIM],
-                    joint_matrix[:, QUERY_WIDTH + KEY_WIDTH + side * HEAD_DIM :][:, :HEAD_DIM],
-                ],
-                axis=1,
-            )
-            for side in range(2)
-        ]
-    )
-    merge_halves = merge_matrix.T.reshape(depth, 2, half).transpose(1, 0, 2)
+    inverse = theta ** -(np.arange(HEAD_DIM // 2) * (2.0 / HEAD_DIM))
+    inverse = jnp.asarray(np.tile(inverse, 2)[None], floats)
     outer = cotangent[0]
     (
         w,
@@ -1206,21 +1252,22 @@
             pltpu.VMEM((length, model), halves),
             pltpu.VMEM((length, model), halves),
         ]
-        + semaphores(136, 9),
+        + semaphores(137, 10),
         compiler_params=params(0),
-    )(stack, joint_halves, merge_halves, small, inverse, tokens[0], outer)
+    )(stack, joint_matrix, merge_matrix.T, small, inverse, tokens[0], outer)
 
     lines = 2 * length
-    back, branch, grads = pl.pallas_call(
+    back, branch, done, grads = pl.pallas_call(
         functools.partial(feed_kernel, nz),
         name="feed_forward",
         out_shape=(
             shape((length, model), floats),
             shape((nz, 2, length, model)),
-            shape((3, nz, 2, 2, depth, share)),
+            shape((3, 2, 2, depth, share)),
+            shape((3, nz - 2, 2, 2, depth, share)),
         ),
         in_specs=[anywhere, anywhere, vmem],
-        out_specs=(vmem, vmem, anywhere),
+        out_specs=(vmem, vmem, anywhere, anywhere),
         scratch_shapes=[
             pltpu.VMEM((3,) + blocks + (depth, share), halves),
             pltpu.VMEM((nz, 2, length, model), halves),
@@ -1233,8 +1280,9 @@
             pltpu.VMEM((nz - 1, length, model), halves),
             pltpu.VMEM((nz - 1, length, model), halves),
             pltpu.VMEM((nz, 3, 2, 2, depth, share), halves),
+            pltpu.VMEM((2, 3, 2, depth, share), halves),
         ]
-        + semaphores(18, 8),
+        + semaphores(22, 8),
         compiler_params=params(1),
     )(w, team_outer, xn2)
 
@@ -1254,19 +1302,19 @@
         out_shape=(
             shape((length, model)),
             shape((length, model), floats),
-            shape((2, depth, half + pair_width), floats),
-            shape((2, depth, half), floats),
+            shape((depth, joint_width), floats),
+            shape((depth, QUERY_WIDTH), floats),
             shape((8, 128), floats),
             shape((3, depth, 2 * nz * share)),
         ),
-        in_specs=[anywhere] * 5 + [vmem] * 11,
+        in_specs=[anywhere] * 6 + [vmem] * 11,
         out_specs=(vmem,) * 5 + (anywhere,),
         scratch_shapes=[
             pltpu.VMEM(blocks + (depth, half), halves),
             pltpu.VMEM(blocks + (depth, half), halves),
             pltpu.VMEM(blocks + (depth, pair_width), halves),
-            pltpu.VMEM((3, nz, 2, depth, share), halves),
-            pltpu.VMEM((nz, 3, 2, depth, share), halves),
+            pltpu.VMEM((3, nz - 2, 2, depth, share), halves),
+            pltpu.VMEM((nz - 2, 3, 2, depth, share), halves),
             pltpu.VMEM((nz, length, model), halves),
             pltpu.VMEM((nz, length, model), halves),
             pltpu.VMEM((nz - 1, length, model), halves),
@@ -1287,9 +1335,10 @@
             pltpu.VMEM((length, model), halves),
             pltpu.VMEM((length, model), halves),
         ]
-        + semaphores(89, 6),
+        + semaphores(90, 6),
         compiler_params=params(2),
     )(
+        done,
         grads,
         branch,
         kv_all,
@@ -1307,16 +1356,7 @@
         shares,
         summed,
     )
-    joint_grad = jnp.concatenate(
-        [
-            joint_grad[side, :, first : first + width]
-            for first, width in ((0, half), (half, HEAD_DIM), (half + HEAD_DIM, HEAD_DIM))
-            for side in range(2)
-        ],
-        axis=1,
-    )
-    merge_grad = merge_grad.transpose(1, 0, 2).reshape(depth, QUERY_WIDTH)
-    grads = grads[:, :, :hidden_width].astype(floats)
+    grads = [grads[which, :, :hidden_width].astype(floats) for which in range(3)]
     return (
         output[None],
         tokens_grad[None],

time: 469 us -> 450 us (0.959)
  the two profiles are of different devices: /device:TPU:22 before, /device:TPU:20 now
where the time goes in v5:
time: 450 us; the launch traced here: 442 us
  Pallas kernels  426 us (95%)
  other arithmetic  9.07 us (2%)
  local copies, waits for them, and re-layouts  6.16 us (1%)
    pallas_call x1, Pallas kernels, body_kernels(): pl.pallas_call(functools.partial(back_kernel, nz), name='attention_backwa...  166 us
    pallas_call x1, Pallas kernels, body_kernels(): pl.pallas_call(functools.partial(attention_kernel, nz), name='attention_f...  133 us
    pallas_call x1, Pallas kernels, body_kernels(): pl.pallas_call(functools.partial(feed_kernel, nz), name='feed_forward', o...  127 us

profile of v5, /device:TPU:20, one launch (start us, length us, event | category | flops | bytes accessed | tf_op | source)
XLA Modules:
  0.0 441.8 jit_solution(12223977308973525303)
XLA Ops:
  0.6 0.7 convert_element_type.30
  1.3 0.7 bitcast_convert_fusion.4
  2.0 0.7 bitcast_convert_fusion.2
  2.6 0.6 stack.48.small_ref
  3.2 2.8 fusion.4.stack_ref
  6.1 133.2 %attention_forward.1 = (bf16[3,4,2,2,2,48,1152]{6,5,4,3,2,1,0:T(8,128)(2,1)}, bf16[4,2,128,1536]{3,2,1,0:T(8,128)(2,1)}, bf16[4,2,2,2,48,256]{5,4,3,2,1,0:T(8,12...) custom-call(bf16[3,48,9216]{2,1,0:T(8,128)(2,1)} %fusion.4.stack_ref, ...), custom_call_target="tpu_custom_call" | custom-call | tf_op jit(solution)/shard_map/attention_forward/pallas_call | solution.py:1224
  139.3 126.9 %feed_forward.1 = (f32[128,1536]{1,0:T(8,128)}, bf16[4,2,128,1536]{3,2,1,0:T(8,128)(2,1)}, bf16[3,2,2,48,1152]{4,3,2,1,0:T(8,128)(2,1)}, bf16[3,2,2,2,48,1152]{5,4,3,2,1,0:T(8,128)(2,1)}) custom-call(bf16[3,4,2,2,2,48,1152]{6,5,4,3,2,1,0:T(8,128)(2,1)} %get-tuple-element.34.w_ref, bf16[4,2,128,1536]{3,2,1,0:T(8,128)(2,1)} %get-tuple-element.35.ct_ref, ...), custom_call_target="tpu_custom_call" | custom-call | tf_op jit(solution)/shard_map/feed_forward/pallas_call | solution.py:1260
  266.2 165.6 %attention_backward.1 = (bf16[128,1536]{1,0:T(8,128)(2,1)}, f32[128,1536]{1,0:T(8,128)}, f32[48,2048]{1,0:T(8,128)}, f32[48,1536]{1,0:T(8,128)}, f32[8,128]{1,0:T(8,128)}, /*index=5*/bf16[3,48,9216]{2,1,0:T(8,128)(2,1)}) custom-call(bf16[3,2,2,48,1152]{4,3,2,1,0:T(8,128)(2,1)} %get-tuple-element.37.done_ref, ...), custom_call_target="tpu_custom_call" | custom-call | tf_op jit(solution)/shard_map/attention_backward/pallas_call | solution.py:1299
  431.9 1.2 slice_bitcast_fusion.2
  433.0 1.3 slice_bitcast_fusion
  434.3 0.0 copy-start.2
  434.3 0.0 copy-start
  434.3 0.0 copy-start.1
  434.3 4.2 convert_bitcast_fusion
  438.5 0.0 copy-start.3
  438.5 0.0 copy-done.2
  438.5 0.7 copy.26
  439.3 0.0 copy-done
  439.3 0.9 copy.27
  440.2 0.0 copy-done.1
  440.2 0.7 copy.28
  440.9 0.0 copy-done.3
  440.9 0.7 copy.29
  (1 shorter events, 0.0 us)
Async XLA Ops:
  434.3 4.2 copy-start.2
  434.3 5.0 %copy-start = (f32[128,1536]{1,0:T(8,128)S(1)}, f32[128,1536]{1,0:T(8,128)}, u32[]{:S(2)}) copy-start(f32[128,1536]{1,0:T(8,128)} %get-tuple-element.53) | copy-start | bytes 2359300
  434.3 5.9 %copy-start.1 = (f32[48,2048]{1,0:T(8,128)S(1)}, f32[48,2048]{1,0:T(8,128)}, u32[]{:S(2)}) copy-start(f32[48,2048]{1,0:T(8,128)} %get-tuple-element.77) | copy-start | bytes 1179652
  438.5 2.4 copy-start.3

commit v6 on v5

--- a/solution.py
+++ b/solution.py
@@ -154,6 +154,10 @@
 
 def far_first(nz):
     return sorted(range(nz), key=lambda dz: (dz == 0, abs(2 * dz - nz)))
+
+
+def near_first(nz):
+    return [sorted(range(nz), key=lambda group: (abs(group - at), -group)) for at in range(nz)]
 
 
 def cuts_of(width, step):
@@ -588,35 +592,57 @@
         return lax.rem(z + nz - dz, nz)
 
     meet([place.line(dz) for dz in range(1, nz)] + [place.across[name] for name in "xyc"])
-    along = {
-        dz: courier.copy(normal_ref, xn.at[z, y], place.line(dz)) for dz in range(1, nz)
-    }
-    side = {0: courier.copy(normal_ref, xn.at[z, y], place.across["y"])}
+    xn[z, y] = normal_ref[...]
+    blocks = Line(courier, place, lambda group: xn.at[group, y])
+    blocks.start()
+    side = {}
+
+    def pass_on(step):
+        for item in blocks.items():
+            if item[0] == step:
+                way, group, exists = item[1:]
+                if step:
+                    blocks.arrive(*item)
+                spot = xn.at[group, y]
+                side[step, way] = courier.copy(spot, spot, place.across["y"], exists)
+
+    pass_on(0)
+    groups = near_first(nz)
+
+    def group_at(number):
+        return sum(jnp.where(z == at, groups[at][number], 0) for at in range(nz))
+
+    def wait_for(number):
+        for at in range(nz):
+            gap = groups[at][number] - at
+            made = side[abs(gap), 0 if gap == 0 else (1 if gap < 0 else -1)]
+            pl.when(z == at)(made.raw.wait_recv)
+
     loads = [
         pltpu.make_async_copy(w_ref.at[which], w.at[which], locals_.at[which])
         for which in range(3)
     ] + [pltpu.make_async_copy(ct_ref, ct, locals_.at[3])]
     for made in loads:
         made.start()
-    xn[z, y] = normal_ref[...]
+    pass_on(1)
     for made in loads:
         made.wait()
 
     def weight(which, start, size):
         return w[which, :, :, :, :, :, start : start + size].reshape(model, size)
 
-    def pass_on(dz):
-        along[dz].wait_recv()
-        spot = xn.at[source(dz), y]
-        side[dz] = courier.copy(spot, spot, place.across["y"])
-
     half = nz // 2
-    scatter = []
+    scatter = {}
+
+    def scatter_on(dz):
+        group = group_at(dz)
+        scatter[dz] = courier.copy(
+            part.at[group, 1 - y], ybuf.at[group], place.across["y"]
+        )
+
     for dz in range(nz):
-        group = source(dz)
-        if dz + 1 < nz:
-            pass_on(dz + 1)
-        side[dz].wait_recv()
+        group = group_at(dz)
+        wait_for(dz)
         for start, size in cuts_of(share, 256):
             normal = xn[group].reshape(2 * length, model)
             outer = ct[group].reshape(2 * length, model)
@@ -643,21 +669,30 @@
             ) + lax.dot_general(ub[group], turned(1), last_pair, preferred_element_type=floats)
             part[group, :, :, lanes] = both.astype(halves).reshape(2, length, model // 2)
 
-        scatter.append(
-            courier.copy(part.at[group, 1 - y], ybuf.at[group], place.across["y"])
+        if dz:
+            scatter_on(dz)
+        if dz + 2 < nz:
+            pass_on(dz + 2)
+
+    scatter_on(0)
+
+    final = {
+        dz: courier.make(
+            zsend.at[source(dz)], zbuf.at[dz - 1], (source(dz), x, y, c)
         )
-
-    final = {}
+        for dz in range(1, nz)
+    }
 
     def sum_on(dz):
-        group = source(dz)
+        group = group_at(dz)
         scatter[dz].wait_recv()
         total = part[group, y].astype(floats) + ybuf[group].astype(floats)
         if dz == 0:
             back_ref[...] = total
         else:
-            zsend[dz - 1] = total.astype(halves)
-            final[dz] = courier.copy(zsend.at[dz - 1], zbuf.at[dz - 1], (group, x, y, c))
+            zsend[group] = total.astype(halves)
+            for apart, made in final.items():
+                pl.when(source(apart) == group)(made.raw.start)
 
     for group in range(nz):
 
@@ -723,7 +758,7 @@
 
     for position in range(nz):
         product(orders[position])
-        sum_on(position)
+        sum_on((position + 1) % nz)
         if position:
             settle(position - 1)
     settle(nz - 1)
@@ -1277,12 +1312,12 @@
             pltpu.VMEM((nz, lines, share), halves),
             pltpu.VMEM((nz, 2, length, model), halves),
             pltpu.VMEM((nz, length, model), halves),
-            pltpu.VMEM((nz - 1, length, model), halves),
+            pltpu.VMEM((nz, length, model), halves),
             pltpu.VMEM((nz - 1, length, model), halves),
             pltpu.VMEM((nz, 3, 2, 2, depth, share), halves),
             pltpu.VMEM((2, 3, 2, depth, share), halves),
         ]
-        + semaphores(22, 8),
+        + semaphores(30, 8),
         compiler_params=params(1),
     )(w, team_outer, xn2)
 

time: 450 us -> 434 us (0.964)
  the two profiles are of different devices: /device:TPU:20 before, /device:TPU:16 now
where the time goes in v6:
time: 434 us; the launch traced here: 426 us
  Pallas kernels  410 us (94%)
  other arithmetic  9.07 us (2%)
  local copies, waits for them, and re-layouts  6.16 us (1%)
    pallas_call x1, Pallas kernels, body_kernels(): pl.pallas_call(functools.partial(back_kernel, nz), name='attention_backwa...  170 us
    pallas_call x1, Pallas kernels, body_kernels(): pl.pallas_call(functools.partial(attention_kernel, nz), name='attention_f...  131 us
    pallas_call x1, Pallas kernels, body_kernels(): pl.pallas_call(functools.partial(feed_kernel, nz), name='feed_forward', o...  109 us

profile of v6, /device:TPU:16, one launch (start us, length us, event | category | flops | bytes accessed | tf_op | source)
XLA Modules:
  0.0 425.8 jit_solution(4794692529950076929)
XLA Ops:
  0.6 0.7 convert_element_type.30
  1.3 0.7 bitcast_convert_fusion.4
  2.0 0.7 bitcast_convert_fusion.2
  2.6 0.6 stack.48.small_ref
  3.2 2.8 fusion.4.stack_ref
  6.1 130.6 %attention_forward.1 = (bf16[3,4,2,2,2,48,1152]{6,5,4,3,2,1,0:T(8,128)(2,1)}, bf16[4,2,128,1536]{3,2,1,0:T(8,128)(2,1)}, bf16[4,2,2,2,48,256]{5,4,3,2,1,0:T(8,12...) custom-call(bf16[3,48,9216]{2,1,0:T(8,128)(2,1)} %fusion.4.stack_ref, ...), custom_call_target="tpu_custom_call" | custom-call | tf_op jit(solution)/shard_map/attention_forward/pallas_call | solution.py:1259
  136.7 108.6 %feed_forward.1 = (f32[128,1536]{1,0:T(8,128)}, bf16[4,2,128,1536]{3,2,1,0:T(8,128)(2,1)}, bf16[3,2,2,48,1152]{4,3,2,1,0:T(8,128)(2,1)}, bf16[3,2,2,2,48,1152]{5,4,3,2,1,0:T(8,128)(2,1)}) custom-call(bf16[3,4,2,2,2,48,1152]{6,5,4,3,2,1,0:T(8,128)(2,1)} %get-tuple-element.34.w_ref, bf16[4,2,128,1536]{3,2,1,0:T(8,128)(2,1)} %get-tuple-element.35.ct_ref, ...), custom_call_target="tpu_custom_call" | custom-call | tf_op jit(solution)/shard_map/feed_forward/pallas_call | solution.py:1295
  245.3 170.5 %attention_backward.1 = (bf16[128,1536]{1,0:T(8,128)(2,1)}, f32[128,1536]{1,0:T(8,128)}, f32[48,2048]{1,0:T(8,128)}, f32[48,1536]{1,0:T(8,128)}, f32[8,128]{1,0:T(8,128)}, /*index=5*/bf16[3,48,9216]{2,1,0:T(8,128)(2,1)}) custom-call(bf16[3,2,2,48,1152]{4,3,2,1,0:T(8,128)(2,1)} %get-tuple-element.37.done_ref, ...), custom_call_target="tpu_custom_call" | custom-call | tf_op jit(solution)/shard_map/attention_backward/pallas_call | solution.py:1334
  415.8 1.2 slice_bitcast_fusion.2
  417.0 1.3 slice_bitcast_fusion
  418.3 0.0 copy-start.2
  418.3 0.0 copy-start
  418.3 0.0 copy-start.1
  418.3 4.2 convert_bitcast_fusion
  422.5 0.0 copy-start.3
  422.5 0.0 copy-done.2
  422.5 0.7 copy.26
  423.3 0.0 copy-done
  423.3 0.9 copy.27
  424.2 0.0 copy-done.1
  424.2 0.7 copy.28
  424.9 0.0 copy-done.3
  424.9 0.7 copy.29
  (1 shorter events, 0.0 us)
Async XLA Ops:
  418.3 4.2 copy-start.2
  418.3 5.0 %copy-start = (f32[128,1536]{1,0:T(8,128)S(1)}, f32[128,1536]{1,0:T(8,128)}, u32[]{:S(2)}) copy-start(f32[128,1536]{1,0:T(8,128)} %get-tuple-element.53) | copy-start | bytes 2359300
  418.3 5.9 %copy-start.1 = (f32[48,2048]{1,0:T(8,128)S(1)}, f32[48,2048]{1,0:T(8,128)}, u32[]{:S(2)}) copy-start(f32[48,2048]{1,0:T(8,128)} %get-tuple-element.77) | copy-start | bytes 1179652
  422.5 2.4 copy-start.3

commit v7 on v6

--- a/solution.py
+++ b/solution.py
@@ -385,7 +385,7 @@
         w_hand[dz, dy, 1] = courier.copy(spot, spot, place.across["c"])
 
     give(0, 1)
-    give(2, 0)
+    give(1, 0)
     for name in ("small", "kv"):
         for made in own_waits[name]:
             made.wait()
@@ -410,7 +410,7 @@
     for name in ("small", "kv"):
         gathers[name].done()
     take(0, 1)
-    give(2, 1)
+    give(1, 1)
 
     pieces = small[...].reshape(devices * 8, 128).astype(halves)
 
@@ -464,8 +464,8 @@
     gathers["m"].along()
     for item in pairs.items()[1:3]:
         pairs.arrive(*item)
-    take(2, 0)
-    give(1, 0)
+    take(1, 0)
+    give(3, 0)
     for item in pairs.items()[3:]:
         pairs.arrive(*item)
     gathers["m"].pass_on(1)
@@ -477,9 +477,9 @@
         query_ref[head] = turned(query[:, head * HEAD_DIM : (head + 1) * HEAD_DIM]).astype(halves)
     for step in range(2, nz):
         gathers["m"].pass_on(step)
-    take(2, 1)
-    give(1, 1)
-    give(3, 0)
+    take(1, 1)
+    give(3, 1)
+    give(2, 0)
     outers = Line(courier, place, lambda group: ct_ref.at[group, y])
     ct_side = {}
 
@@ -513,8 +513,8 @@
             out_ref[:, lanes] = jnp.dot(shares, values, preferred_element_type=floats)
 
     attend(0, GROUP // 2)
-    take(1, 0)
-    give(3, 1)
+    take(3, 0)
+    give(2, 1)
     attend(GROUP // 2, GROUP)
     outers.start()
     gathers["m"].done()
@@ -528,23 +528,23 @@
     mixed_ref[...] = jnp.where(x == 0, merged[:length], merged[length:])
     mixed_send[...] = jnp.where(x == 0, merged[length:], merged[:length]).astype(halves)
     mixed_cross = courier.copy(mixed_send, mixed_in, place.across["x"])
-    take(1, 1)
-    hand(2, 0)
+    take(3, 1)
+    hand(1, 0)
     for item in outers.items()[1:3]:
         ct_on(item)
     mixed_cross.wait_recv()
     mixed = tokens_ref[...].astype(floats) + (mixed_ref[...] + mixed_in[...].astype(floats))
     mixed_ref[...] = mixed
     xn2_ref[...] = (mixed * norm_parts(mixed) * gain_second).astype(halves)
-    take(3, 0)
-    hand(2, 1)
+    take(2, 0)
+    hand(1, 1)
     for item in outers.items()[3:5]:
         ct_on(item)
-    hand(1, 0)
-    take(3, 1)
+    hand(3, 0)
+    take(2, 1)
     for item in outers.items()[5:]:
         ct_on(item)
-    for spot in ((1, 1), (3, 0), (3, 1)):
+    for spot in ((3, 1), (2, 0), (2, 1)):
         hand(*spot)
     for made in w_hand.values():
         made.wait_recv()
@@ -1121,44 +1121,51 @@
     for dz in late[:1]:
         grads_on(dz)
 
-    back_cross.wait_recv()
-    normal_own = normal_own + back_in[...].astype(floats)
-    residual = tokens_ref[...].astype(floats)
-    part, first_local = norm_back(normal_own, residual, norm_parts(residual), gain_ref[0:1, :])
-    tokens_grad_ref[...] += part
-
     local = jnp.sum(joint_back[...].astype(floats), axis=0, keepdims=True)
     pieces_of = []
     for first, width in ((0, half), (half, HEAD_DIM), (half + HEAD_DIM, HEAD_DIM)):
         for side in range(2):
             pieces_of.append(jnp.where(x == side, local[:, first : first + width], 0.0))
     bias_local = jnp.concatenate(pieces_of, axis=1)
-    pieces = jnp.zeros((devices * 8, 128), floats)
-    for which, values in ((0, bias_local), (1, first_local), (2, second_local)):
+    def piece_rows(which, values):
         mine_rows = gather_pieces(values, values.shape[1] // devices, devices)
         at = lax.broadcasted_iota(jnp.int32, (devices * 8, devices), 0)
         wanted = lax.broadcasted_iota(jnp.int32, (devices * 8, devices), 1) * 8 + which
-        pieces = pieces + jnp.dot(
+        return jnp.dot(
             (at == wanted).astype(floats),
             mine_rows,
             preferred_element_type=floats,
             precision=lax.Precision.HIGHEST,
         )
+
+    pieces = piece_rows(0, bias_local) + piece_rows(2, second_local)
+    branches = LineSum(
+        courier, place, branch_own, lambda group: (group,), branch_above, branch_below
+    )
+    back_cross.wait_recv()
+    normal_own = normal_own + back_in[...].astype(floats)
+    residual = tokens_ref[...].astype(floats)
+    part, first_local = norm_back(normal_own, residual, norm_parts(residual), gain_ref[0:1, :])
+    tokens_grad_ref[...] += part
+
+    pieces = pieces + piece_rows(1, first_local)
     smalls.parts[...] = pieces.reshape(nz, 2, 2, 2, 8, 128)
     for group in smalls.groups:
         smalls.to_core(group)
+    for made in (merges, queries, keys_values):
+        made.along()
+    for line in (keys_values.line, queries.line, merges.line, branches):
+        line.forward_step(0)
+    for line in (keys_values.line, queries.line, merges.line, branches):
+        line.forward_step(1)
     for dz in late[1:]:
         grads_on(dz)
     smalls.sideways()
-    for made in (merges, queries, keys_values):
-        made.along()
-    branches = LineSum(
-        courier, place, branch_own, lambda group: (group,), branch_above, branch_below
-    )
+    for line in (keys_values.line, queries.line, merges.line, branches):
+        line.forward_step(2)
     smalls.along()
     for step in range(nz - 1):
-        for line in (smalls.line, keys_values.line, queries.line, merges.line, branches):
-            line.forward_step(step)
+        smalls.line.forward_step(step)
     for made in (merges, queries, keys_values, smalls):
         made.across()
     branches.finish()

time: 434 us -> 423 us (0.975)
  the two profiles are of different devices: /device:TPU:16 before, /device:TPU:0 now
where the time goes in v7:
time: 423 us; the launch traced here: 415 us
  Pallas kernels  399 us (94%)
  other arithmetic  9.07 us (2%)
  local copies, waits for them, and re-layouts  6.16 us (1%)
    pallas_call x1, Pallas kernels, body_kernels(): pl.pallas_call(functools.partial(back_kernel, nz), name='attention_backwa...  160 us
    pallas_call x1, Pallas kernels, body_kernels(): pl.pallas_call(functools.partial(attention_kernel, nz), name='attention_f...  135 us
    pallas_call x1, Pallas kernels, body_kernels(): pl.pallas_call(functools.partial(feed_kernel, nz), name='feed_forward', o...  104 us

profile of v7, /device:TPU:0, one launch (start us, length us, event | category | flops | bytes accessed | tf_op | source)
XLA Modules:
  0.0 414.8 jit_solution(16615152562988132996)
XLA Ops:
  0.6 0.7 convert_element_type.30
  1.3 0.7 bitcast_convert_fusion.4
  2.0 0.7 bitcast_convert_fusion.2
  2.6 0.6 stack.48.small_ref
  3.2 2.8 fusion.4.stack_ref
  6.1 135.2 %attention_forward.1 = (bf16[3,4,2,2,2,48,1152]{6,5,4,3,2,1,0:T(8,128)(2,1)}, bf16[4,2,128,1536]{3,2,1,0:T(8,128)(2,1)}, bf16[4,2,2,2,48,256]{5,4,3,2,1,0:T(8,12...) custom-call(bf16[3,48,9216]{2,1,0:T(8,128)(2,1)} %fusion.4.stack_ref, ...), custom_call_target="tpu_custom_call" | custom-call | tf_op jit(solution)/shard_map/attention_forward/pallas_call | solution.py:1266
  141.3 103.9 %feed_forward.1 = (f32[128,1536]{1,0:T(8,128)}, bf16[4,2,128,1536]{3,2,1,0:T(8,128)(2,1)}, bf16[3,2,2,48,1152]{4,3,2,1,0:T(8,128)(2,1)}, bf16[3,2,2,2,48,1152]{5,4,3,2,1,0:T(8,128)(2,1)}) custom-call(bf16[3,4,2,2,2,48,1152]{6,5,4,3,2,1,0:T(8,128)(2,1)} %get-tuple-element.34.w_ref, bf16[4,2,128,1536]{3,2,1,0:T(8,128)(2,1)} %get-tuple-element.35.ct_ref, ...), custom_call_target="tpu_custom_call" | custom-call | tf_op jit(solution)/shard_map/feed_forward/pallas_call | solution.py:1302
  245.2 159.6 %attention_backward.1 = (bf16[128,1536]{1,0:T(8,128)(2,1)}, f32[128,1536]{1,0:T(8,128)}, f32[48,2048]{1,0:T(8,128)}, f32[48,1536]{1,0:T(8,128)}, f32[8,128]{1,0:T(8,128)}, /*index=5*/bf16[3,48,9216]{2,1,0:T(8,128)(2,1)}) custom-call(bf16[3,2,2,48,1152]{4,3,2,1,0:T(8,128)(2,1)} %get-tuple-element.37.done_ref, ...), custom_call_target="tpu_custom_call" | custom-call | tf_op jit(solution)/shard_map/attention_backward/pallas_call | solution.py:1341
  404.8 1.2 slice_bitcast_fusion.2
  406.0 1.3 slice_bitcast_fusion
  407.3 0.0 copy-start.2
  407.3 0.0 copy-start
  407.3 0.0 copy-start.1
  407.3 4.2 %convert_bitcast_fusion = (f32[8960,48]{0,1:T(8,128)}, f32[48,8960]{1,0:T(8,128)}, f32[48,8960]{1,0:T(8,128)}) fusion(bf16[3,48,9216]{2,1,0:T(8,128)(2,1)} %get-tuple-element.57), kind=kLoop, calls=%fused_computation.6 | loop fusion | flops 1290240 | bytes 7741440 | tf_op jit(solution)/shard_map/transpose | solution.py:1412
  411.5 0.0 copy-start.3
  411.5 0.0 copy-done.2
  411.5 0.7 copy.26
  412.2 0.0 copy-done
  412.2 0.9 copy.27
  413.1 0.0 copy-done.1
  413.1 0.7 copy.28
  413.9 0.0 copy-done.3
  413.9 0.7 copy.29
  (1 shorter events, 0.0 us)
Async XLA Ops:
  407.3 4.2 %copy-start.2 = (bf16[128,1536]{1,0:T(8,128)(2,1)S(1)}, bf16[128,1536]{1,0:T(8,128)(2,1)}, u32[]{:S(2)}) copy-start(bf16[128,1536]{1,0:T(8,128)(2,1)} %get-tuple-element.52) | copy-start | bytes 1179652
  407.3 5.0 %copy-start = (f32[128,1536]{1,0:T(8,128)S(1)}, f32[128,1536]{1,0:T(8,128)}, u32[]{:S(2)}) copy-start(f32[128,1536]{1,0:T(8,128)} %get-tuple-element.53) | copy-start | bytes 2359300
  407.3 5.9 %copy-start.1 = (f32[48,2048]{1,0:T(8,128)S(1)}, f32[48,2048]{1,0:T(8,128)}, u32[]{:S(2)}) copy-start(f32[48,2048]{1,0:T(8,128)} %get-tuple-element.77) | copy-start | bytes 1179652
  411.5 2.4 copy-start.3

commit v8 on v7

--- a/solution.py
+++ b/solution.py
@@ -674,28 +674,6 @@
         if dz + 2 < nz:
             pass_on(dz + 2)
 
-    scatter_on(0)
-
-    final = {
-        dz: courier.make(
-            zsend.at[source(dz)], zbuf.at[dz - 1], (source(dz), x, y, c)
-        )
-        for dz in range(1, nz)
-    }
-
-    def sum_on(dz):
-        group = group_at(dz)
-        scatter[dz].wait_recv()
-        total = part[group, y].astype(floats) + ybuf[group].astype(floats)
-        if dz == 0:
-            back_ref[...] = total
-        else:
-            zsend[group] = total.astype(halves)
-            for apart, made in final.items():
-                pl.when(source(apart) == group)(made.raw.start)
-
-    for group in range(nz):
-
         @pl.loop(0, 2)
         def _(step):
             rows = pl.ds(step * half, half)
@@ -707,6 +685,27 @@
                 preferred_element_type=floats,
             )
             branch_ref[group, :, :, lanes] = product.astype(halves).reshape(2, length, model // 2)
+
+
+    scatter_on(0)
+
+    final = {
+        dz: courier.make(
+            zsend.at[source(dz)], zbuf.at[dz - 1], (source(dz), x, y, c)
+        )
+        for dz in range(1, nz)
+    }
+
+    def sum_on(dz):
+        group = group_at(dz)
+        scatter[dz].wait_recv()
+        total = part[group, y].astype(floats) + ybuf[group].astype(floats)
+        if dz == 0:
+            back_ref[...] = total
+        else:
+            zsend[group] = total.astype(halves)
+            for apart, made in final.items():
+                pl.when(source(apart) == group)(made.raw.start)
 
     orders = far_first(nz)
     early = 2
@@ -1241,10 +1240,10 @@
         return jnp.pad(values.astype(floats), (0, 128 - values.shape[0]))
 
     own_labels = segments[0]
-    empty = jnp.zeros((128,), floats)
-    small = jnp.stack(
-        [lane_row(v) for v in (joint_bias, norm_first, norm_second, own_labels)] + [empty] * 4
-    )
+    at = lax.broadcasted_iota(jnp.int32, (8, 128), 0)
+    small = jnp.zeros((8, 128), floats)
+    for which, values in enumerate((joint_bias, norm_first, norm_second, own_labels)):
+        small = jnp.where(at == which, lane_row(values)[None], small)
     inverse = theta ** -(np.arange(HEAD_DIM // 2) * (2.0 / HEAD_DIM))
     inverse = jnp.asarray(np.tile(inverse, 2)[None], floats)
     outer = cotangent[0]

time: 423 us -> 419 us (level)
  Pallas kernels: 399 us -> 394 us
    pallas_call x1, Pallas kernels: 104 us -> 98.8 us  [body_kernels(): pl.pallas_call(functools.partial(feed_kernel, nz), name='feed_forward', o...]
where the time goes in v8:
time: 419 us; the launch traced here: 411 us
  Pallas kernels  394 us (94%)
  other arithmetic  9.75 us (2%)
  local copies, waits for them, and re-layouts  5.56 us (1%)
    pallas_call x1, Pallas kernels, body_kernels(): pl.pallas_call(functools.partial(back_kernel, nz), name='attention_backwa...  160 us
    pallas_call x1, Pallas kernels, body_kernels(): pl.pallas_call(functools.partial(attention_kernel, nz), name='attention_f...  135 us
    pallas_call x1, Pallas kernels, body_kernels(): pl.pallas_call(functools.partial(feed_kernel, nz), name='feed_forward', o...  98.8 us

profile of v8, /device:TPU:0, one launch (start us, length us, event | category | flops | bytes accessed | tf_op | source)
XLA Modules:
  0.0 410.6 jit_solution(11965538212039959960)
XLA Ops:
  0.6 0.7 convert_bitcast_fusion.1
  1.3 0.7 pad_convert_fusion.2
  2.0 0.7 pad_convert_fusion
  2.6 0.7 select_select_fusion.small_ref
  3.3 2.8 fusion.4.stack_ref
  6.2 135.3 %attention_forward.1 = (bf16[3,4,2,2,2,48,1152]{6,5,4,3,2,1,0:T(8,128)(2,1)}, bf16[4,2,128,1536]{3,2,1,0:T(8,128)(2,1)}, bf16[4,2,2,2,48,256]{5,4,3,2,1,0:T(8,12...) custom-call(bf16[3,48,9216]{2,1,0:T(8,128)(2,1)} %fusion.4.stack_ref, ...), custom_call_target="tpu_custom_call" | custom-call | tf_op jit(solution)/shard_map/attention_forward/pallas_call | solution.py:1265
  141.4 98.8 %feed_forward.1 = (f32[128,1536]{1,0:T(8,128)}, bf16[4,2,128,1536]{3,2,1,0:T(8,128)(2,1)}, bf16[3,2,2,48,1152]{4,3,2,1,0:T(8,128)(2,1)}, bf16[3,2,2,2,48,1152]{5,4,3,2,1,0:T(8,128)(2,1)}) custom-call(bf16[3,4,2,2,2,48,1152]{6,5,4,3,2,1,0:T(8,128)(2,1)} %get-tuple-element.34.w_ref, bf16[4,2,128,1536]{3,2,1,0:T(8,128)(2,1)} %get-tuple-element.35.ct_ref, ...), custom_call_target="tpu_custom_call" | custom-call | tf_op jit(solution)/shard_map/feed_forward/pallas_call | solution.py:1301
  240.2 160.4 %attention_backward.1 = (bf16[128,1536]{1,0:T(8,128)(2,1)}, f32[128,1536]{1,0:T(8,128)}, f32[48,2048]{1,0:T(8,128)}, f32[48,1536]{1,0:T(8,128)}, f32[8,128]{1,0:T(8,128)}, /*index=5*/bf16[3,48,9216]{2,1,0:T(8,128)(2,1)}) custom-call(bf16[3,2,2,48,1152]{4,3,2,1,0:T(8,128)(2,1)} %get-tuple-element.37.done_ref, ...), custom_call_target="tpu_custom_call" | custom-call | tf_op jit(solution)/shard_map/attention_backward/pallas_call | solution.py:1340
  400.6 1.2 slice_bitcast_fusion.2
  401.8 1.3 slice_bitcast_fusion
  403.1 0.0 copy-start.2
  403.1 0.0 copy-start
  403.1 0.0 copy-start.1
  403.1 4.2 %convert_bitcast_fusion = (f32[8960,48]{0,1:T(8,128)}, f32[48,8960]{1,0:T(8,128)}, f32[48,8960]{1,0:T(8,128)}) fusion(bf16[3,48,9216]{2,1,0:T(8,128)(2,1)} %get-tuple-element.57), kind=kLoop, calls=%fused_computation.6 | loop fusion | flops 1290240 | bytes 7741440 | tf_op jit(solution)/shard_map/transpose | solution.py:1411
  407.3 0.0 copy-start.3
  407.3 0.0 copy-done.2
  407.3 0.7 copy.26
  408.1 0.0 copy-done
  408.1 0.9 copy.27
  408.9 0.0 copy-done.1
  408.9 0.7 copy.28
  409.7 0.0 copy-done.3
  409.7 0.7 copy.29
  (2 shorter events, 0.0 us)
Async XLA Ops:
  403.1 4.2 %copy-start.2 = (bf16[128,1536]{1,0:T(8,128)(2,1)S(1)}, bf16[128,1536]{1,0:T(8,128)(2,1)}, u32[]{:S(2)}) copy-start(bf16[128,1536]{1,0:T(8,128)(2,1)} %get-tuple-element.52) | copy-start | bytes 1179652
  403.1 5.0 %copy-start = (f32[128,1536]{1,0:T(8,128)S(1)}, f32[128,1536]{1,0:T(8,128)}, u32[]{:S(2)}) copy-start(f32[128,1536]{1,0:T(8,128)} %get-tuple-element.53) | copy-start | bytes 2359300
  403.1 5.9 %copy-start.1 = (f32[48,2048]{1,0:T(8,128)S(1)}, f32[48,2048]{1,0:T(8,128)}, u32[]{:S(2)}) copy-start(f32[48,2048]{1,0:T(8,128)} %get-tuple-element.81) | copy-start | bytes 1179652
  407.3 2.4 copy-start.3

commit v9 on v8

--- a/solution.py
+++ b/solution.py
@@ -153,7 +153,7 @@
 
 
 def far_first(nz):
-    return sorted(range(nz), key=lambda dz: (dz == 0, abs(2 * dz - nz)))
+    return sorted(range(nz), key=lambda dz: (dz == 0, -abs(2 * dz - nz)))
 
 
 def near_first(nz):
@@ -1165,7 +1165,7 @@
     smalls.along()
     for step in range(nz - 1):
         smalls.line.forward_step(step)
-    for made in (merges, queries, keys_values, smalls):
+    for made in (smalls, keys_values, queries, merges):
         made.across()
     branches.finish()
     output_ref[...] = (mixed_ref[...] + branch_own[z].astype(floats)).astype(halves)

time: 419 us -> 422 us (level)
  no operation moved by 1% of the time
where the time goes in v9:
time: 422 us; the launch traced here: 414 us
  Pallas kernels  398 us (94%)
  other arithmetic  9.75 us (2%)
  local copies, waits for them, and re-layouts  5.56 us (1%)
    pallas_call x1, Pallas kernels, body_kernels(): pl.pallas_call(functools.partial(back_kernel, nz), name='attention_backwa...  164 us
    pallas_call x1, Pallas kernels, body_kernels(): pl.pallas_call(functools.partial(attention_kernel, nz), name='attention_f...  135 us
    pallas_call x1, Pallas kernels, body_kernels(): pl.pallas_call(functools.partial(feed_kernel, nz), name='feed_forward', o...  98.8 us

profile of v9, /device:TPU:0, one launch (start us, length us, event | category | flops | bytes accessed | tf_op | source)
XLA Modules:
  0.0 413.8 jit_solution(3224573057444488686)
XLA Ops:
  0.6 0.7 convert_bitcast_fusion.1
  1.3 0.7 pad_convert_fusion.2
  2.0 0.7 pad_convert_fusion
  2.6 0.7 select_select_fusion.small_ref
  3.3 2.8 fusion.4.stack_ref
  6.2 135.3 %attention_forward.1 = (bf16[3,4,2,2,2,48,1152]{6,5,4,3,2,1,0:T(8,128)(2,1)}, bf16[4,2,128,1536]{3,2,1,0:T(8,128)(2,1)}, bf16[4,2,2,2,48,256]{5,4,3,2,1,0:T(8,12...) custom-call(bf16[3,48,9216]{2,1,0:T(8,128)(2,1)} %fusion.4.stack_ref, ...), custom_call_target="tpu_custom_call" | custom-call | tf_op jit(solution)/shard_map/attention_forward/pallas_call | solution.py:1265
  141.4 98.8 %feed_forward.1 = (f32[128,1536]{1,0:T(8,128)}, bf16[4,2,128,1536]{3,2,1,0:T(8,128)(2,1)}, bf16[3,2,2,48,1152]{4,3,2,1,0:T(8,128)(2,1)}, bf16[3,2,2,2,48,1152]{5,4,3,2,1,0:T(8,128)(2,1)}) custom-call(bf16[3,4,2,2,2,48,1152]{6,5,4,3,2,1,0:T(8,128)(2,1)} %get-tuple-element.34.w_ref, bf16[4,2,128,1536]{3,2,1,0:T(8,128)(2,1)} %get-tuple-element.35.ct_ref, ...), custom_call_target="tpu_custom_call" | custom-call | tf_op jit(solution)/shard_map/feed_forward/pallas_call | solution.py:1301
  240.2 163.6 %attention_backward.1 = (bf16[128,1536]{1,0:T(8,128)(2,1)}, f32[128,1536]{1,0:T(8,128)}, f32[48,2048]{1,0:T(8,128)}, f32[48,1536]{1,0:T(8,128)}, f32[8,128]{1,0:T(8,128)}, /*index=5*/bf16[3,48,9216]{2,1,0:T(8,128)(2,1)}) custom-call(bf16[3,2,2,48,1152]{4,3,2,1,0:T(8,128)(2,1)} %get-tuple-element.37.done_ref, ...), custom_call_target="tpu_custom_call" | custom-call | tf_op jit(solution)/shard_map/attention_backward/pallas_call | solution.py:1340
  403.8 1.2 slice_bitcast_fusion.2
  405.0 1.3 slice_bitcast_fusion
  406.3 0.0 copy-start.2
  406.3 0.0 copy-start
  406.3 0.0 copy-start.1
  406.3 4.2 %convert_bitcast_fusion = (f32[8960,48]{0,1:T(8,128)}, f32[48,8960]{1,0:T(8,128)}, f32[48,8960]{1,0:T(8,128)}) fusion(bf16[3,48,9216]{2,1,0:T(8,128)(2,1)} %get-tuple-element.57), kind=kLoop, calls=%fused_computation.6 | loop fusion | flops 1290240 | bytes 7741440 | tf_op jit(solution)/shard_map/transpose | solution.py:1411
  410.5 0.0 copy-start.3
  410.5 0.0 copy-done.2
  410.5 0.7 copy.26
  411.3 0.0 copy-done
  411.3 0.9 copy.27
  412.2 0.0 copy-done.1
  412.2 0.7 copy.28
  412.9 0.0 copy-done.3
  412.9 0.7 copy.29
  (2 shorter events, 0.0 us)
Async XLA Ops:
  406.3 4.2 %copy-start.2 = (bf16[128,1536]{1,0:T(8,128)(2,1)S(1)}, bf16[128,1536]{1,0:T(8,128)(2,1)}, u32[]{:S(2)}) copy-start(bf16[128,1536]{1,0:T(8,128)(2,1)} %get-tuple-element.52) | copy-start | bytes 1179652
  406.3 5.0 %copy-start = (f32[128,1536]{1,0:T(8,128)S(1)}, f32[128,1536]{1,0:T(8,128)}, u32[]{:S(2)}) copy-start(f32[128,1536]{1,0:T(8,128)} %get-tuple-element.53) | copy-start | bytes 2359300
  406.3 5.9 %copy-start.1 = (f32[48,2048]{1,0:T(8,128)S(1)}, f32[48,2048]{1,0:T(8,128)}, u32[]{:S(2)}) copy-start(f32[48,2048]{1,0:T(8,128)} %get-tuple-element.81) | copy-start | bytes 1179652
  410.5 2.4 copy-start.3
